TPU v7x, 128 devices: a whole 4x4x4 slice. The times are simulated.
128 devices in a mesh: dp: 32 (over y, z, x_hi), sp: 4 (over x_lo, core).
Axes of the slice: x: 4 (x_hi: 2, x_lo: 2; x = x_hi * 2 + x_lo), y: 4, z: 4, core: 2. Of those that a mesh axis runs over, the one named last changes fastest.
Arguments:
- hidden_in: bfloat16 [32768, 768], P(('dp', 'sp')), may hold values from -6 to 6
- cotangent: bfloat16 [32768, 768], P(('dp', 'sp')), may hold values from -6 to 6
- attn_gain: bfloat16 [768], P(('dp', 'sp')), may hold values from 0.5 to 1.5
- attn_shift: bfloat16 [768], P(('dp', 'sp')), may hold values from -3 to 3
- mlp_gain: bfloat16 [768], P(('dp', 'sp')), may hold values from 0.5 to 1.5
- mlp_shift: bfloat16 [768], P(('dp', 'sp')), may hold values from -3 to 3
- qkv_weight: bfloat16 [768, 2304], P(('dp', 'sp')), may hold values from -0.21875 to 0.21875
- qkv_bias: bfloat16 [2304], P(('dp', 'sp')), may hold values from -3 to 3
- dense_weight: bfloat16 [768, 768], P(('dp', 'sp')), may hold values from -0.875 to 0.875
- dense_bias: bfloat16 [768], P(('dp', 'sp')), may hold values from -3 to 3
- up_weight: bfloat16 [768, 3072], P(('dp', 'sp')), may hold values from -0.21875 to 0.21875
- up_bias: bfloat16 [3072], P(('dp', 'sp')), may hold values from -3 to 3
- down_weight: bfloat16 [3072, 768], P(('dp', 'sp')), may hold values from -0.109375 to 0.109375
- down_bias: bfloat16 [768], P(('dp', 'sp')), may hold values from -3 to 3
Outputs:
- hidden_out: bfloat16 [32768, 768], P(('dp', 'sp'))
- hidden_grad: bfloat16 [32768, 768], P(('dp', 'sp'))
- attention_gain_gradient: float32 [768], P(('dp', 'sp'))
- attn_shift_grad: float32 [768], P(('dp', 'sp'))
- feedforward_gain_gradient: float32 [768], P(('dp', 'sp'))
- mlp_shift_grad: float32 [768], P(('dp', 'sp'))
- qkv_weight_grad: float32 [768, 2304], P(('dp', 'sp'))
- qkv_bias_grad: float32 [2304], P(('dp', 'sp'))
- dense_weight_grad: float32 [768, 768], P(('dp', 'sp'))
- dense_bias_grad: float32 [768], P(('dp', 'sp'))
- up_weight_grad: float32 [768, 3072], P(('dp', 'sp'))
- up_bias_grad: float32 [3072], P(('dp', 'sp'))
- down_weight_grad: float32 [3072, 768], P(('dp', 'sp'))
- down_bias_grad: float32 [768], P(('dp', 'sp'))
All inputs are finite; a program needn't handle non-finite values.
Results may differ from a plain program's by a relative error of at most 0.0099.
Values may be sent and summed in bfloat16 or wider, within the bound.
A program may use at most 128 MiB of HBM per device.

v0:
```python
import jax
import jax.numpy as jnp
from jax import lax
from jax.sharding import PartitionSpec as P

D = 768
HEADS = 12
HEAD_DIM = 64
ROT = 16


def contract_rows(left, right):
    return lax.dot_general(
        left, right, (((0,), (0,)), ((), ())), preferred_element_type=jnp.float32
    )


def contract_cols(left, right):
    return lax.dot_general(
        left, right, (((1,), (1,)), ((), ())), preferred_element_type=jnp.float32
    )


def norm_components(values_in):
    center = jnp.mean(values_in, -1, keepdims=True)
    centered = values_in - center
    spread = jnp.mean(centered * centered, -1, keepdims=True)
    inverse_deviation = lax.rsqrt(spread + 1e-05)
    return (centered * inverse_deviation, inverse_deviation)


def norm_backward_pass(normalized_gradient, standardized_input, inverse_deviation, norm_gain):
    standardized_gradient = normalized_gradient * norm_gain
    return inverse_deviation * (
        standardized_gradient
        - jnp.mean(standardized_gradient, -1, keepdims=True)
        - standardized_input
        * jnp.mean(standardized_gradient * standardized_input, -1, keepdims=True)
    )


def rotary_tables(positions):
    halfway = ROT // 2
    frequency = 10000.0 ** (-2.0 * jnp.arange(halfway, dtype=jnp.float32) / ROT)
    angles = positions.astype(jnp.float32)[:, None] * frequency[None, :]
    return (jnp.cos(angles)[:, None, :], jnp.sin(angles)[:, None, :], halfway)


def rotate(vector, cosine_b, sine_b, halfway):
    lead_half = vector[..., :halfway]
    next_half = vector[..., halfway:ROT]
    return jnp.concatenate(
        [
            lead_half * cosine_b - next_half * sine_b,
            next_half * cosine_b + lead_half * sine_b,
            vector[..., ROT:],
        ],
        -1,
    )


def unrotate(vector, cosine_b, sine_b, halfway):
    lead_half = vector[..., :halfway]
    next_half = vector[..., halfway:ROT]
    return jnp.concatenate(
        [
            lead_half * cosine_b + next_half * sine_b,
            next_half * cosine_b - lead_half * sine_b,
            vector[..., ROT:],
        ],
        -1,
    )


def local(
    hidden_in,
    cotangent,
    attn_gain,
    attn_shift,
    mlp_gain,
    mlp_shift,
    qkv_weight,
    qkv_bias,
    dense_weight,
    dense_bias,
    up_weight,
    up_bias,
    down_weight,
    down_bias,
):
    gathered = (
        lax.all_gather(qkv_weight, ("dp", "sp"), axis=0, tiled=True),
        lax.all_gather(dense_weight, ("dp", "sp"), axis=0, tiled=True),
        lax.all_gather(up_weight, ("dp", "sp"), axis=0, tiled=True),
        lax.all_gather(down_weight, ("dp", "sp"), axis=0, tiled=True),
        lax.all_gather(qkv_bias, ("dp", "sp"), axis=0, tiled=True),
        lax.all_gather(dense_bias, ("dp", "sp"), axis=0, tiled=True),
        lax.all_gather(up_bias, ("dp", "sp"), axis=0, tiled=True),
        lax.all_gather(down_bias, ("dp", "sp"), axis=0, tiled=True),
        lax.all_gather(attn_gain, ("dp", "sp"), axis=0, tiled=True),
        lax.all_gather(attn_shift, ("dp", "sp"), axis=0, tiled=True),
        lax.all_gather(mlp_gain, ("dp", "sp"), axis=0, tiled=True),
        lax.all_gather(mlp_shift, ("dp", "sp"), axis=0, tiled=True),
    )
    (
        qkv_full,
        dense_full,
        up_full,
        down_full,
        qkv_add,
        dense_add,
        up_add,
        down_add,
        first_gain,
        first_shift,
        second_gain,
        second_shift,
    ) = gathered
    rows_here = hidden_in.shape[0]
    inputs_wide = hidden_in.astype(jnp.float32)
    first_standardized, first_inverse_deviation = norm_components(inputs_wide)
    second_standardized, second_inverse_deviation = norm_components(inputs_wide)
    first_normalized = (
        first_standardized * first_gain.astype(jnp.float32) + first_shift.astype(jnp.float32)
    ).astype(jnp.bfloat16)
    second_normalized = (
        second_standardized * second_gain.astype(jnp.float32) + second_shift.astype(jnp.float32)
    ).astype(jnp.bfloat16)
    qkv = jnp.dot(first_normalized, qkv_full, preferred_element_type=jnp.float32) + qkv_add.astype(
        jnp.float32
    )
    qkv = qkv.reshape(rows_here, 3, HEADS, HEAD_DIM)
    positions = lax.axis_index("sp") * rows_here + jnp.arange(rows_here, dtype=jnp.int32)
    cosine_b, sine_b, halfway = rotary_tables(positions)
    stacked = jnp.stack(
        [
            rotate(qkv[:, 0], cosine_b, sine_b, halfway),
            rotate(qkv[:, 1], cosine_b, sine_b, halfway),
            qkv[:, 2],
        ],
        0,
    ).astype(jnp.bfloat16)
    head_layout = lax.all_to_all(stacked, "sp", split_axis=2, concat_axis=1, tiled=True)
    queries = head_layout[0]
    key_heads = head_layout[1]
    value_heads = head_layout[2]
    length = queries.shape[0]
    block_rows = min(512, length)
    block_count = length // block_rows
    score_scale = HEAD_DIM ** (-0.5)
    key_pos = jnp.arange(length, dtype=jnp.int32)

    def scores_of(block_index):
        first_row = block_index * block_rows
        query_block = lax.dynamic_slice_in_dim(queries, first_row, block_rows, 0)
        raw_scores = jnp.einsum(
            "qhd,khd->hqk", query_block, key_heads, preferred_element_type=jnp.float32
        )
        query_pos = first_row + jnp.arange(block_rows, dtype=jnp.int32)
        masked = jnp.where(
            key_pos[None, None, :] <= query_pos[None, :, None], raw_scores * score_scale, -1e30
        )
        return (query_block, masked)

    def forward_block(block_index):
        query_block, masked = scores_of(block_index)
        highest = jnp.max(masked, -1, keepdims=True)
        expo_terms = jnp.exp(masked - highest)
        denominator = jnp.sum(expo_terms, -1, keepdims=True)
        weights_low = (expo_terms / denominator).astype(jnp.bfloat16)
        attended = jnp.einsum(
            "hqk,khd->qhd", weights_low, value_heads, preferred_element_type=jnp.float32
        )
        return (attended, (highest + jnp.log(denominator))[..., 0])

    attended_all, log_sums = lax.map(forward_block, jnp.arange(block_count, dtype=jnp.int32))
    attn_heads = attended_all.reshape(length, -1, HEAD_DIM).astype(jnp.bfloat16)
    context = lax.all_to_all(attn_heads, "sp", split_axis=0, concat_axis=1, tiled=True).reshape(
        rows_here, D
    )
    attn_branch = jnp.dot(
        context, dense_full, preferred_element_type=jnp.float32
    ) + dense_add.astype(jnp.float32)
    pre_act = jnp.dot(
        second_normalized, up_full, preferred_element_type=jnp.float32
    ) + up_add.astype(jnp.float32)
    activated = jax.nn.gelu(pre_act, approximate=False).astype(jnp.bfloat16)
    mlp_branch = jnp.dot(
        activated, down_full, preferred_element_type=jnp.float32
    ) + down_add.astype(jnp.float32)
    hidden_out = (inputs_wide + attn_branch + mlp_branch).astype(jnp.bfloat16)
    qkv_back = gathered[0]
    dense_back = gathered[1]
    up_back = gathered[2]
    down_back = gathered[3]
    first_gain_wide = gathered[8].astype(jnp.float32)
    second_gain_wide = gathered[10].astype(jnp.float32)
    grad_out_f = cotangent.astype(jnp.float32)
    grad_context = (
        contract_cols(cotangent, dense_back)
        .astype(jnp.bfloat16)
        .reshape(rows_here, HEADS, HEAD_DIM)
    )
    grad_heads = lax.all_to_all(grad_context, "sp", split_axis=1, concat_axis=0, tiled=True)
    out_bias_sum = jnp.sum(grad_out_f, 0)
    dense_grad = contract_rows(context, cotangent)
    down_grad = contract_rows(activated, cotangent)
    grad_act = contract_cols(cotangent, down_back)
    normal_cdf = 0.5 * (1.0 + lax.erf(pre_act * 0.7071067811865476))
    normal_pdf = jnp.exp(-0.5 * pre_act * pre_act) * 0.3989422804014327
    grad_pre = (grad_act * (normal_cdf + pre_act * normal_pdf)).astype(jnp.bfloat16)
    up_grad = contract_rows(second_normalized, grad_pre)
    up_bias_grad = jnp.sum(grad_pre.astype(jnp.float32), 0)
    second_normalized_gradient = contract_cols(grad_pre, up_back)
    feedforward_gain_gradient = jnp.sum(second_normalized_gradient * second_standardized, 0)
    mlp_shift_grad = jnp.sum(second_normalized_gradient, 0)
    second_branch_gradient = norm_backward_pass(
        second_normalized_gradient, second_standardized, second_inverse_deviation, second_gain_wide
    )
    out_dense_bias = out_bias_sum
    out_down_bias = out_bias_sum

    def backward_block(carry, block_index):
        grad_keys, grad_values = carry
        query_block, masked = scores_of(block_index)
        probs = jnp.exp(masked - log_sums[block_index][..., None])
        grad_block = lax.dynamic_slice_in_dim(grad_heads, block_index * block_rows, block_rows, 0)
        grad_probs = jnp.einsum(
            "qhd,khd->hqk", grad_block, value_heads, preferred_element_type=jnp.float32
        )
        row_delta = jnp.sum(probs * grad_probs, -1, keepdims=True)
        grad_scores = (score_scale * probs * (grad_probs - row_delta)).astype(jnp.bfloat16)
        grad_query = jnp.einsum(
            "hqk,khd->qhd", grad_scores, key_heads, preferred_element_type=jnp.float32
        )
        grad_keys = grad_keys + jnp.einsum(
            "hqk,qhd->khd", grad_scores, query_block, preferred_element_type=jnp.float32
        )
        grad_values = grad_values + jnp.einsum(
            "hqk,qhd->khd",
            probs.astype(jnp.bfloat16),
            grad_block,
            preferred_element_type=jnp.float32,
        )
        return ((grad_keys, grad_values), grad_query)

    zero_heads = jnp.zeros(key_heads.shape, jnp.float32)
    (grad_keys, grad_values), grad_queries = lax.scan(
        backward_block, (zero_heads, zero_heads), jnp.arange(block_count, dtype=jnp.int32)
    )
    grad_stack = jnp.stack(
        [grad_queries.reshape(length, -1, HEAD_DIM), grad_keys, grad_values], 0
    ).astype(jnp.bfloat16)
    grad_tokens = lax.all_to_all(grad_stack, "sp", split_axis=1, concat_axis=2, tiled=True).astype(
        jnp.float32
    )
    grad_qkv = (
        jnp.stack(
            [
                unrotate(grad_tokens[0], cosine_b, sine_b, halfway),
                unrotate(grad_tokens[1], cosine_b, sine_b, halfway),
                grad_tokens[2],
            ],
            1,
        )
        .reshape(rows_here, 3 * D)
        .astype(jnp.bfloat16)
    )
    qkv_grad = contract_rows(first_normalized, grad_qkv)
    qkv_bias_grad = jnp.sum(grad_qkv.astype(jnp.float32), 0)
    first_normalized_gradient = contract_cols(grad_qkv, qkv_back)
    attention_gain_gradient = jnp.sum(first_normalized_gradient * first_standardized, 0)
    attn_shift_grad = jnp.sum(first_normalized_gradient, 0)
    first_branch_gradient = norm_backward_pass(
        first_normalized_gradient, first_standardized, first_inverse_deviation, first_gain_wide
    )
    hidden_grad = (grad_out_f + first_branch_gradient + second_branch_gradient).astype(jnp.bfloat16)
    (
        qkv_grad,
        dense_grad,
        up_grad,
        down_grad,
        qkv_bias_grad,
        out_dense_bias,
        up_bias_grad,
        out_down_bias,
        attention_gain_gradient,
        attn_shift_grad,
        feedforward_gain_gradient,
        mlp_shift_grad,
    ) = (
        lax.psum_scatter(qkv_grad, ("dp", "sp"), scatter_dimension=0, tiled=True),
        lax.psum_scatter(dense_grad, ("dp", "sp"), scatter_dimension=0, tiled=True),
        lax.psum_scatter(up_grad, ("dp", "sp"), scatter_dimension=0, tiled=True),
        lax.psum_scatter(down_grad, ("dp", "sp"), scatter_dimension=0, tiled=True),
        lax.psum_scatter(qkv_bias_grad, ("dp", "sp"), scatter_dimension=0, tiled=True),
        lax.psum_scatter(out_dense_bias, ("dp", "sp"), scatter_dimension=0, tiled=True),
        lax.psum_scatter(up_bias_grad, ("dp", "sp"), scatter_dimension=0, tiled=True),
        lax.psum_scatter(out_down_bias, ("dp", "sp"), scatter_dimension=0, tiled=True),
        lax.psum_scatter(attention_gain_gradient, ("dp", "sp"), scatter_dimension=0, tiled=True),
        lax.psum_scatter(attn_shift_grad, ("dp", "sp"), scatter_dimension=0, tiled=True),
        lax.psum_scatter(feedforward_gain_gradient, ("dp", "sp"), scatter_dimension=0, tiled=True),
        lax.psum_scatter(mlp_shift_grad, ("dp", "sp"), scatter_dimension=0, tiled=True),
    )
    return (
        hidden_out,
        hidden_grad,
        attention_gain_gradient,
        attn_shift_grad,
        feedforward_gain_gradient,
        mlp_shift_grad,
        qkv_grad,
        qkv_bias_grad,
        dense_grad,
        out_dense_bias,
        up_grad,
        up_bias_grad,
        down_grad,
        out_down_bias,
    )


def solution(mesh):
    placed = (
        P(("dp", "sp"), None),
        P(("dp", "sp"), None),
        P(("dp", "sp")),
        P(("dp", "sp")),
        P(("dp", "sp")),
        P(("dp", "sp")),
        P(("dp", "sp"), None),
        P(("dp", "sp")),
        P(("dp", "sp"), None),
        P(("dp", "sp")),
        P(("dp", "sp"), None),
        P(("dp", "sp")),
        P(("dp", "sp"), None),
        P(("dp", "sp")),
    )
    return jax.shard_map(
        local,
        mesh=mesh,
        in_specs=placed,
        out_specs=(
            P(("dp", "sp"), None),
            P(("dp", "sp"), None),
            P(("dp", "sp")),
            P(("dp", "sp")),
            P(("dp", "sp")),
            P(("dp", "sp")),
            P(("dp", "sp"), None),
            P(("dp", "sp")),
            P(("dp", "sp"), None),
            P(("dp", "sp")),
            P(("dp", "sp"), None),
            P(("dp", "sp")),
            P(("dp", "sp"), None),
            P(("dp", "sp")),
        ),
        check_vma=False,
    )
```

profile of v0, /device:TPU:1, one launch (start us, length us, event | category | flops | bytes accessed | tf_op | source)
XLA Modules:
  0.0 1182.4 jit_solution(579374381714195685)
XLA Ops:
  19.2 69.4 %all-reduce.22 = (bf16[3072]{0:T(1024)(128)(2,1)S(1)}, bf16[768]{0:T(1024)(128)(2,1)S(1)}, bf16[768]{0:T(1024)(128)(2,1)S(1)}, bf16[768]{0:T(1024)(128)(2,1)}, b...) all-reduce(bf16[3072]{0:T(1024)(128)(2,1)S(1)} %dynamic-update-slic, ...), channel_id=1, replica_groups=mesh['dp'=32,'sp'=4] {'dp','sp'}, use_global_device_ids=true, to_apply=%add.6 | all-reduce | flops 9984 | bytes 39936
  96.9 49.4 %all-gather.10.cloned.1.call-done = bf16[128,6,2304]{2,1,0:T(8,128)(2,1)} async-done(((bf16[1,6,2304]{2,1,0:T(8,128)(2,1)}), bf16[128,6,2304]{2,1,0:T(8,128)(2,1)}) %all-gather.10.cloned.1.call-update) | async-done | bytes 3538960 | tf_op jit(solution)/shard_map/all_gather | solution.py:92
  146.3 6.6 reshape.273
  169.8 15.4 %all-to-all-done = bf16[3,256,12,64]{1,3,0,2:T(8,128)(2,1)S(1)} async-done(((bf16[3,256,12,64]{1,3,0,2:T(8,128)(2,1)}), bf16[3,256,12,64]{1,3,0,2:T(8,128)(2,1)S(1)}, u32[]{:S(2)}, u32[]{:S(2)}) %all-to-all-start) | async-done | bytes 1179680 | tf_op jit(solution)/shard_map/all_to_all | solution.py:143
  188.6 19.1 %while.28 = (s32[]{:T(128)}, bf16[2,512,3,64]{1,3,2,0:T(8,128)(2,1)S(1)}, f32[2,3,512]{2,1,0:T(4,128)}, s32[2]{0:T(128)S(1)}, bf16[1024,3,64]{0,2,1:T(8,128)(2,1...) while((s32[]{:T(128)}, ...), condition=%wide.region_5.6_spmd.clone, body=%wide.region_2.5_spmd.clone.sunk | while | flops 422050816 | bytes 22407360 | solution.py:176
  215.6 7.8 reshape.277
  223.4 10.8 fusion.44
  241.7 53.9 %while.29 = (s32[]{:T(128)}, f32[1024,3,64]{0,2,1:T(8,128)}, f32[1024,3,64]{0,2,1:T(8,128)}, bf16[2,512,3,64]{1,3,2,0:T(8,128)(2,1)}, s32[2]{0:T(128)}, /*index=...) while((s32[]{:T(128)}, f32[1024,3,64]{0,2,1:T(8,128)}, ...), condition=%wide.region_8.9_spmd.clone, body=%wide.region_6.0_spmd.clone.sunk | while | flops 1033108480 | bytes 87341560 | solution.py:248
  251.3 5.7 multiply_reduce_fusion.4
  278.0 5.8 multiply_reduce_fusion.4
  316.1 10.9 all-to-all-done.3
  342.8 7.0 convert_reduce_fusion
  356.2 365.6 %fusion.91 = (f32[8,2304]{1,0:T(8,128)}, f32[8,768]{1,0:T(8,128)S(1)}, f32[8,3072]{1,0:T(8,128)}) fusion(f32[768,2304]{1,0:T(8,128)} %fusion.88, f32[768,768]{1,0:T(8,128)S(1)} %copy-done.7, f32[768,3072]{1,0:T(8,128)} %fusion.85), kind=kCustom, calls=%all-reduce-scatter.3 | all-reduce-scatter fusion | flops 6291457 | bytes 19070976
  733.6 14.6 %collective-permute-start.54 = (f32[8,768]{1,0:T(8,128)S(1)}, f32[8,768]{1,0:T(8,128)S(1)}, u32[]{:S(2)}, u32[]{:S(2)}) collective-permute-start(f32[8,768]{1,0:T(8,128)S(1)} %get-tuple-element.237), channel_id=1, source_target_pairs={{0,23},{1,24},{2,25},{3,26},{4,27},{5,28},{6,29},{7,30},{8,31},{9,... | collective-permute-start | bytes 73736
  748.2 7.1 collective-permute-start.53
  824.5 5.8 collective-permute-start.26
  918.5 5.7 collective-permute-done.95
  958.5 8.9 collective-permute-start.78
  971.4 7.3 collective-permute-start.74
  980.1 62.5 %all-reduce.21 = (f32[768]{0:T(1024)S(1)}, f32[768]{0:T(1024)S(1)}, f32[768]{0:T(1024)S(1)}, f32[768]{0:T(1024)S(1)}, f32[2304]{0:T(1024)S(1)}, /*index=5*/f32[768]{0:T(1024)S(1)}, f32[3072]{0:T(1024)S(1)}) all-reduce(f32[768]{0:T(1024)} %get-tuple-element.174, ...), channel_id=2, replica_groups=mesh['dp'=32,'sp'=4] {'dp','sp'}, use_global_device_ids=true, to_apply=%region_14.15.clone | all-reduce | flops 9216 | bytes 73728
  1046.2 25.7 %concatenate.19 = f32[262,768]{1,0:T(8,128)S(1)} concatenate(f32[6,768]{1,0:T(8,128)} %copy-done.107, f32[8,768]{1,0:T(8,128)S(1)} %copy-done.104, f32[8,768]{1,0:T(8,128)S(1)} %copy-done.106, f32[8,768]{1,0:T(8,128)} %copy-done.108, f32[8,768]{1,0:T(8,128)} %copy-done.109, f32[8,768]{1,0:T(8,128)} %copy-done.110, f32[8,768]{1,0:T(8,128)} %copy-done.111, f32[8,768]{1,0:T(8,128)} %copy-done.112, ...), dimensions={0} | concatenate | bytes 1609728
  1084.1 5.6 collective-permute-start.69
  1090.5 33.5 %concatenate.18 = f32[262,2304]{1,0:T(8,128)S(1)} concatenate(f32[6,2304]{1,0:T(8,128)} %copy-done.66, f32[8,2304]{1,0:T(8,128)} %copy-done.63, f32[8,2304]{1,0:T(8,128)} %copy-done.64, f32[8,2304]{1,0:T(8,128)} %copy-done.65, f32[8,2304]{1,0:T(8,128)} %copy-done.67, f32[8,2304]{1,0:T(8,128)} %copy-done.68, f32[8,2304]{1,0:T(8,128)} %copy-done.69, f32[8,2304]{1,0:T(8,128)} %copy-done.70, ...), dimensions={0} | concatenate | bytes 4829184
  1143.0 31.5 %concatenate.20 = f32[262,3072]{1,0:T(8,128)S(1)} concatenate(f32[6,3072]{1,0:T(8,128)S(1)} %copy-done.33, f32[8,3072]{1,0:T(8,128)S(1)} %copy-done.31, f32[8,3072]{1,0:T(8,128)} %copy-done.34, f32[8,3072]{1,0:T(8,128)} %copy-done.35, f32[8,3072]{1,0:T(8,128)} %copy-done.36, f32[8,3072]{1,0:T(8,128)} %copy-done.37, f32[8,3072]{1,0:T(8,128)} %copy-done.38, f32[8,3072]{1,0:T(8,128)} %copy-done.39, ...), dimensions={0} | concatenate | bytes 6438912
  (650 shorter events, 395.4 us)
Async XLA Ops:
  7.2 81.5 %all-gather.12.cloned.1.call-start = ((), (), s32[]{:S(2)}) async-start(), calls=%async_computation.8 | async-start | bytes 1585152 | tf_op jit(solution)/shard_map/all_gather | solution.py:93
  7.9 138.4 %all-gather.10.cloned.1.call-start = ((), (), s32[]{:S(2)}) async-start(), calls=%async_computation.7 | async-start | bytes 4755456 | tf_op jit(solution)/shard_map/all_gather | solution.py:92
  8.7 206.9 %all-gather.14.cloned.1.call-start = ((), (), s32[]{:S(2)}) async-start(), calls=%async_computation.9 | async-start | bytes 6340608 | tf_op jit(solution)/shard_map/all_gather | solution.py:94
  9.4 333.4 %all-gather.8.cloned.1.call-start = ((), (), s32[]{:S(2)}) async-start(), calls=%async_computation.5 | async-start | bytes 4755456 | tf_op jit(solution)/shard_map/all_gather | solution.py:95
  92.5 72.3 %all-to-all-start.2 = ((bf16[256,12,64]{0,2,1:T(8,128)(2,1)}), bf16[256,12,64]{0,2,1:T(8,128)(2,1)S(1)}, u32[]{:S(2)}, u32[]{:S(2)}) async-start(bf16[256,12,64]{0,2,1:T(8,128)(2,1)} %bitcast.17), calls=%async_computation.2 | async-start | bytes 786432 | tf_op jit(solution)/shard_map/all_to_all | solution.py:204
  209.9 97.5 %all-to-all-start.1 = ((bf16[4,2,24576]{2,1,0:T(2,128)(2,1)}), bf16[4,2,24576]{2,1,0:T(2,128)(2,1)}, u32[]{:S(2)}, u32[]{:S(2)}) async-start(bf16[4,2,24576]{2,1,0:T(2,128)(2,1)} %reshape.278), calls=%async_computation.1 | async-start | bytes 786432 | tf_op jit(solution)/shard_map/all_to_all | solution.py:178
  215.0 960.2 %reduce-scatter.8.cloned.1.call-start = ((), (), s32[]{:S(2)}) async-start(), calls=%async_computation.6 | async-start | bytes 9510912 | tf_op jit(solution)/shard_map/reduce_scatter | solution.py:295
  729.6 25.7 %collective-permute-start.57 = (f32[8,768]{1,0:T(8,128)S(1)}, f32[8,768]{1,0:T(8,128)S(1)}, u32[]{:S(2)}, u32[]{:S(2)}) collective-permute-start(f32[8,768]{1,0:T(8,128)S(1)} %get-tuple-element.237), channel_id=1, source_target_pairs={{0,26},{1,27},{2,28},{3,29},{4,30},{5,31},{6,32},{7,33},{8,34},{9,... | collective-permute-start | bytes 73736
  730.9 27.2 %collective-permute-start.56 = (f32[8,768]{1,0:T(8,128)S(1)}, f32[8,768]{1,0:T(8,128)S(1)}, u32[]{:S(2)}, u32[]{:S(2)}) collective-permute-start(f32[8,768]{1,0:T(8,128)S(1)} %get-tuple-element.237), channel_id=1, source_target_pairs={{0,25},{1,26},{2,27},{3,28},{4,29},{5,30},{6,31},{7,32},{8,33},{9,... | collective-permute-start | bytes 73736
  732.2 27.2 %collective-permute-start.55 = (f32[8,768]{1,0:T(8,128)S(1)}, f32[8,768]{1,0:T(8,128)S(1)}, u32[]{:S(2)}, u32[]{:S(2)}) collective-permute-start(f32[8,768]{1,0:T(8,128)S(1)} %get-tuple-element.237), channel_id=1, source_target_pairs={{0,24},{1,25},{2,26},{3,27},{4,28},{5,29},{6,30},{7,31},{8,32},{9,... | collective-permute-start | bytes 73736
  733.6 29.1 %collective-permute-start.54 = (f32[8,768]{1,0:T(8,128)S(1)}, f32[8,768]{1,0:T(8,128)S(1)}, u32[]{:S(2)}, u32[]{:S(2)}) collective-permute-start(f32[8,768]{1,0:T(8,128)S(1)} %get-tuple-element.237), channel_id=1, source_target_pairs={{0,23},{1,24},{2,25},{3,26},{4,27},{5,28},{6,29},{7,30},{8,31},{9,... | collective-permute-start | bytes 73736
  806.7 23.7 %collective-permute-start.30 = (f32[8,2304]{1,0:T(8,128)}, f32[8,2304]{1,0:T(8,128)S(1)}, u32[]{:S(2)}, u32[]{:S(2)}) collective-permute-start(f32[8,2304]{1,0:T(8,128)} %get-tuple-element.236), channel_id=1, source_target_pairs={{0,31},{1,32},{2,33},{3,34},{4,35},{5,36},{6,37},{7,38},{8,39},{9,... | collective-permute-start | bytes 221192
  808.0 23.7 %collective-permute-start.29 = (f32[8,2304]{1,0:T(8,128)}, f32[8,2304]{1,0:T(8,128)S(1)}, u32[]{:S(2)}, u32[]{:S(2)}) collective-permute-start(f32[8,2304]{1,0:T(8,128)} %get-tuple-element.236), channel_id=1, source_target_pairs={{0,30},{1,31},{2,32},{3,33},{4,34},{5,35},{6,36},{7,37},{8,38},{9,... | collective-permute-start | bytes 221192
  809.4 23.7 %collective-permute-start.28 = (f32[8,2304]{1,0:T(8,128)}, f32[8,2304]{1,0:T(8,128)S(1)}, u32[]{:S(2)}, u32[]{:S(2)}) collective-permute-start(f32[8,2304]{1,0:T(8,128)} %get-tuple-element.236), channel_id=1, source_target_pairs={{0,29},{1,30},{2,31},{3,32},{4,33},{5,34},{6,35},{7,36},{8,37},{9,... | collective-permute-start | bytes 221192
  958.5 113.4 %collective-permute-start.78 = (f32[8,3072]{1,0:T(8,128)S(1)}, f32[8,3072]{1,0:T(8,128)S(1)}, u32[]{:S(2)}, u32[]{:S(2)}) collective-permute-start(f32[8,3072]{1,0:T(8,128)S(1)} %copy-done.20), channel_id=1, source_target_pairs={{0,15},{1,16},{2,17},{3,18},{4,19},{5,20},{6,21},{7,22},{8,23},{9,... | collective-permute-start | bytes 294920
  967.4 106.8 %collective-permute-start.77 = (f32[8,3072]{1,0:T(8,128)S(1)}, f32[8,3072]{1,0:T(8,128)S(1)}, u32[]{:S(2)}, u32[]{:S(2)}) collective-permute-start(f32[8,3072]{1,0:T(8,128)S(1)} %copy-done.20), channel_id=1, source_target_pairs={{0,14},{1,15},{2,16},{3,17},{4,18},{5,19},{6,20},{7,21},{8,22},{9,... | collective-permute-start | bytes 294920
  968.8 109.7 %collective-permute-start.76 = (f32[8,3072]{1,0:T(8,128)S(1)}, f32[8,3072]{1,0:T(8,128)S(1)}, u32[]{:S(2)}, u32[]{:S(2)}) collective-permute-start(f32[8,3072]{1,0:T(8,128)S(1)} %copy-done.20), channel_id=1, source_target_pairs={{0,13},{1,14},{2,15},{3,16},{4,17},{5,18},{6,19},{7,20},{8,21},{9,... | collective-permute-start | bytes 294920
  970.1 112.1 %collective-permute-start.75 = (f32[8,3072]{1,0:T(8,128)S(1)}, f32[8,3072]{1,0:T(8,128)S(1)}, u32[]{:S(2)}, u32[]{:S(2)}) collective-permute-start(f32[8,3072]{1,0:T(8,128)S(1)} %copy-done.20), channel_id=1, source_target_pairs={{0,12},{1,13},{2,14},{3,15},{4,16},{5,17},{6,18},{7,19},{8,20},{9,... | collective-permute-start | bytes 294920
  971.4 112.7 %collective-permute-start.74 = (f32[8,3072]{1,0:T(8,128)S(1)}, f32[8,3072]{1,0:T(8,128)S(1)}, u32[]{:S(2)}, u32[]{:S(2)}) collective-permute-start(f32[8,3072]{1,0:T(8,128)S(1)} %copy-done.20), channel_id=1, source_target_pairs={{0,11},{1,12},{2,13},{3,14},{4,15},{5,16},{6,17},{7,18},{8,19},{9,... | collective-permute-start | bytes 294920
  1071.9 52.2 %collective-permute-start.73 = (f32[8,3072]{1,0:T(8,128)S(1)}, f32[8,3072]{1,0:T(8,128)S(1)}, u32[]{:S(2)}, u32[]{:S(2)}) collective-permute-start(f32[8,3072]{1,0:T(8,128)S(1)} %copy-done.20), channel_id=1, source_target_pairs={{0,10},{1,11},{2,12},{3,13},{4,14},{5,15},{6,16},{7,17},{8,18},{9,... | collective-permute-start | bytes 294920
  1074.3 53.2 %collective-permute-start.72 = (f32[8,3072]{1,0:T(8,128)S(1)}, f32[8,3072]{1,0:T(8,128)}, u32[]{:S(2)}, u32[]{:S(2)}) collective-permute-start(f32[8,3072]{1,0:T(8,128)S(1)} %copy-done.20), channel_id=1, source_target_pairs={{0,9},{1,10},{2,11},{3,12},{4,13},{5,14},{6,15},{7,16},{8,17},{9,1... | collective-permute-start | bytes 294920
  1078.5 52.0 %collective-permute-start.71 = (f32[8,3072]{1,0:T(8,128)S(1)}, f32[8,3072]{1,0:T(8,128)}, u32[]{:S(2)}, u32[]{:S(2)}) collective-permute-start(f32[8,3072]{1,0:T(8,128)S(1)} %copy-done.20), channel_id=1, source_target_pairs={{0,8},{1,9},{2,10},{3,11},{4,12},{5,13},{6,14},{7,15},{8,16},{9,17... | collective-permute-start | bytes 294920
  1082.2 53.1 %collective-permute-start.70 = (f32[8,3072]{1,0:T(8,128)S(1)}, f32[8,3072]{1,0:T(8,128)}, u32[]{:S(2)}, u32[]{:S(2)}) collective-permute-start(f32[8,3072]{1,0:T(8,128)S(1)} %copy-done.20), channel_id=1, source_target_pairs={{0,7},{1,8},{2,9},{3,10},{4,11},{5,12},{6,13},{7,14},{8,15},{9,16}... | collective-permute-start | bytes 294920
  1084.1 53.4 %collective-permute-start.69 = (f32[8,3072]{1,0:T(8,128)S(1)}, f32[8,3072]{1,0:T(8,128)}, u32[]{:S(2)}, u32[]{:S(2)}) collective-permute-start(f32[8,3072]{1,0:T(8,128)S(1)} %copy-done.20), channel_id=1, source_target_pairs={{0,6},{1,7},{2,8},{3,9},{4,10},{5,11},{6,12},{7,13},{8,14},{9,15},... | collective-permute-start | bytes 294920
  (230 other events, 8210.7 us)
Sparse Core Ops, SparseCore 0:
  10.8 67.8 all-gather.11
  81.7 64.4 all-gather.9
  149.4 65.6 all-gather.13
  218.0 64.9 all-gather.7
  288.4 218.8 reduce-scatter.7
where the time goes:
time: 1200 us; the launch traced here: 1180 us
  blocking collectives  497 us (41%)
  starting transfers between devices  285 us (24%)
  local copies, waits for them, and re-layouts  172 us (14%)
  matrix products  99.6 us (8%)
  waiting for transfers between devices  86.1 us (7%)
  other arithmetic  18.1 us (2%)
  between operations  17.5 us (1%)
    unnamed x3, blocking collectives  497 us
    unnamed x96, starting transfers between devices  266 us
    unnamed x306, local copies, waits for them, and re-layouts  136 us
    all_gather x1, waiting for transfers between devices, local(): lax.all_gather(qkv_weight, ('dp', 'sp'), axis=0, tiled=True)  49.4 us
  transfers between devices with their start and end apart: 105, of which 6 were waited for; matrix products, arithmetic and copies ran while one was open for 55% of the time, Pallas kernels for 0%

commit v1 on v0

v1 whole, which is shorter than its diff:
```python
import jax
import jax.numpy as jnp
from jax import lax
from jax.sharding import PartitionSpec as P

D = 768
HEADS = 12
HEAD_DIM = 64
ROT = 16
FF = 3072
BF = jnp.bfloat16
F32 = jnp.float32
BOTH = ("dp", "sp")


def dot(left, right):
    return jnp.dot(left, right, preferred_element_type=F32)


def contract_rows(left, right):
    return lax.dot_general(left, right, (((0,), (0,)), ((), ())), preferred_element_type=F32)


def contract_cols(left, right):
    return lax.dot_general(left, right, (((1,), (1,)), ((), ())), preferred_element_type=F32)


def norm_components(values_in):
    center = jnp.mean(values_in, -1, keepdims=True)
    centered = values_in - center
    spread = jnp.mean(centered * centered, -1, keepdims=True)
    inverse_deviation = lax.rsqrt(spread + 1e-05)
    return (centered * inverse_deviation, inverse_deviation)


def rotary_tables(length):
    half = ROT // 2
    frequency = 10000.0 ** (-2.0 * jnp.arange(half, dtype=F32) / ROT)
    angles = jnp.arange(length, dtype=F32)[:, None] * frequency[None, :]
    return (jnp.cos(angles)[:, None, :], jnp.sin(angles)[:, None, :])


def rotate(vector, cosine, sine):
    half = ROT // 2
    lead = vector[..., :half]
    after = vector[..., half:ROT]
    return jnp.concatenate(
        [lead * cosine - after * sine, after * cosine + lead * sine, vector[..., ROT:]], -1
    )


def make_local(n_dp, n_sp):
    n_all = n_dp * n_sp
    to_slice = []
    for dp in range(n_dp):
        for sp in range(n_sp):
            to_slice.append((sp * n_dp + dp, dp * n_sp + sp))
    to_owner = [(b, a) for a, b in to_slice]

    def local(
        hidden_in,
        cotangent,
        attn_gain,
        attn_shift,
        mlp_gain,
        mlp_shift,
        qkv_weight,
        qkv_bias,
        dense_weight,
        dense_bias,
        up_weight,
        up_bias,
        down_weight,
        down_bias,
    ):
        sp = lax.axis_index("sp")
        d_model = hidden_in.shape[1]
        heads_here = HEADS // n_sp
        width = heads_here * HEAD_DIM
        ff_here = FF // n_sp

        small = (
            attn_gain,
            attn_shift,
            mlp_gain,
            mlp_shift,
            qkv_bias,
            dense_bias,
            up_bias,
            down_bias,
        )
        sizes = [item.shape[0] for item in small]
        total = sum(sizes)
        packed = jnp.pad(jnp.concatenate(small), (0, 128 - total)).reshape(1, 128)
        packed = lax.all_gather(packed, BOTH, axis=0, tiled=True).astype(F32)
        vectors = []
        at = 0
        for size in sizes:
            vectors.append(packed[:, at : at + size].reshape(-1))
            at += size
        gain_1, shift_1, gain_2, shift_2, qkv_add, dense_add, up_add, down_add = vectors
        qkv_add = lax.dynamic_slice_in_dim(qkv_add.reshape(3, n_sp, width), sp, 1, 1).reshape(-1)
        up_add = lax.dynamic_slice_in_dim(up_add, sp * ff_here, ff_here, 0)

        up_part = lax.all_to_all(
            up_weight.reshape(-1, n_sp, ff_here), "sp", split_axis=1, concat_axis=0, tiled=True
        ).reshape(-1, ff_here)
        down_part = lax.ppermute(down_weight, BOTH, to_slice)
        qkv_part = lax.all_to_all(
            qkv_weight.reshape(-1, 3, n_sp, width).transpose(0, 2, 1, 3).reshape(-1, n_sp, 3 * width),
            "sp",
            split_axis=1,
            concat_axis=0,
            tiled=True,
        ).reshape(-1, 3 * width)
        dense_part = lax.ppermute(dense_weight, BOTH, to_slice)
        up_t = lax.all_gather(up_part, "dp", axis=0, tiled=True)
        down_t = lax.all_gather(down_part, "dp", axis=0, tiled=True)
        qkv_t = lax.all_gather(qkv_part, "dp", axis=0, tiled=True)
        dense_t = lax.all_gather(dense_part, "dp", axis=0, tiled=True)

        x_seq = lax.all_gather(hidden_in, "sp", axis=0, tiled=True).astype(F32)
        g_seq = lax.all_gather(cotangent, "sp", axis=0, tiled=True)
        length = x_seq.shape[0]
        xhat, rstd = norm_components(x_seq)
        normed_1 = (xhat * gain_1 + shift_1).astype(BF)
        normed_2 = (xhat * gain_2 + shift_2).astype(BF)

        pre = dot(normed_2, up_t) + up_add
        cdf = 0.5 * (1.0 + lax.erf(pre * 0.7071067811865476))
        act = (pre * cdf).astype(BF)
        out_part = dot(act, down_t)
        pdf = jnp.exp(-0.5 * pre * pre) * 0.3989422804014327
        dpre = (contract_cols(g_seq, down_t) * (cdf + pre * pdf)).astype(BF)
        down_grad = contract_rows(act, g_seq)
        up_grad = contract_rows(normed_2, dpre)
        up_bias_grad = jnp.sum(dpre.astype(F32), 0)
        dnormed_2 = contract_cols(dpre, up_t)

        qkv = (dot(normed_1, qkv_t) + qkv_add).reshape(length, 3, heads_here, HEAD_DIM)
        cosine, sine = rotary_tables(length)
        q = rotate(qkv[:, 0], cosine, sine).astype(BF).transpose(1, 0, 2)
        k = rotate(qkv[:, 1], cosine, sine).astype(BF).transpose(1, 0, 2)
        v = qkv[:, 2].astype(BF).transpose(1, 0, 2)
        dctx = contract_cols(g_seq, dense_t).astype(BF)
        do = dctx.reshape(length, heads_here, HEAD_DIM).transpose(1, 0, 2)
        scale = HEAD_DIM ** (-0.5)
        scores = jnp.einsum("hqd,hkd->hqk", q, k, preferred_element_type=F32) * scale
        where = jnp.arange(length)[:, None] >= jnp.arange(length)[None, :]
        scores = jnp.where(where[None], scores, -1e30)
        top = jnp.max(scores, -1, keepdims=True)
        probs = jnp.exp(scores - top)
        probs = probs / jnp.sum(probs, -1, keepdims=True)
        probs_low = probs.astype(BF)
        ctx = jnp.einsum("hqk,hkd->hqd", probs_low, v, preferred_element_type=F32)
        ctx = ctx.astype(BF).transpose(1, 0, 2).reshape(length, width)
        out_part = out_part + dot(ctx, dense_t)
        dense_grad = contract_rows(ctx, g_seq)
        dprobs = jnp.einsum("hqd,hkd->hqk", do, v, preferred_element_type=F32)
        delta = jnp.sum(probs * dprobs, -1, keepdims=True)
        dscores = (scale * probs * (dprobs - delta)).astype(BF)
        dq = jnp.einsum("hqk,hkd->qhd", dscores, k, preferred_element_type=F32)
        dk = jnp.einsum("hqk,hqd->khd", dscores, q, preferred_element_type=F32)
        dv = jnp.einsum("hqk,hqd->khd", probs_low, do, preferred_element_type=F32)
        dq = dq.astype(BF).astype(F32)
        dk = dk.astype(BF).astype(F32)
        dqkv = jnp.stack(
            [rotate(dq, cosine, -sine), rotate(dk, cosine, -sine), dv], 1
        ).astype(BF).reshape(length, 3 * width)
        qkv_grad = contract_rows(normed_1, dqkv)
        qkv_bias_grad = jnp.sum(dqkv.astype(F32), 0)
        dnormed_1 = contract_cols(dqkv, qkv_t)

        out_sum = lax.psum_scatter(out_part, "sp", scatter_dimension=0, tiled=True)
        x_here = hidden_in.astype(F32)
        hidden_out = (x_here + out_sum + (dense_add + down_add)).astype(BF)
        dxhat = lax.psum_scatter(
            dnormed_1 * gain_1 + dnormed_2 * gain_2, "sp", scatter_dimension=0, tiled=True
        )
        xhat_here, rstd_here = norm_components(x_here)
        g_here = cotangent.astype(F32)
        hidden_grad = (
            g_here
            + rstd_here
            * (
                dxhat
                - jnp.mean(dxhat, -1, keepdims=True)
                - xhat_here * jnp.mean(dxhat * xhat_here, -1, keepdims=True)
            )
        ).astype(BF)

        up_own = lax.psum_scatter(up_grad, "dp", scatter_dimension=0, tiled=True)
        down_own = lax.psum_scatter(down_grad, "dp", scatter_dimension=0, tiled=True)
        qkv_own = lax.psum_scatter(qkv_grad, "dp", scatter_dimension=0, tiled=True)
        dense_own = lax.psum_scatter(
            jnp.pad(dense_grad.reshape(n_dp, -1, d_model), ((0, 0), (0, 2), (0, 0))),
            "dp",
            scatter_dimension=0,
            tiled=True,
        )[0, : dense_weight.shape[0]]
        rows = up_weight.shape[0]
        up_own = lax.all_to_all(
            up_own.reshape(n_sp, rows, ff_here), "sp", split_axis=0, concat_axis=0, tiled=True
        ).transpose(1, 0, 2).reshape(rows, FF)
        qkv_own = lax.all_to_all(
            qkv_own.reshape(n_sp, rows, 3 * width), "sp", split_axis=0, concat_axis=0, tiled=True
        ).reshape(n_sp, rows, 3, width).transpose(1, 2, 0, 3).reshape(rows, 3 * d_model)
        down_own = lax.ppermute(down_own, BOTH, to_owner)
        dense_own = lax.ppermute(dense_own, BOTH, to_owner)

        zeros_qkv = jnp.zeros((3, n_sp, width), F32)
        qkv_bias_full = lax.dynamic_update_slice(
            zeros_qkv, qkv_bias_grad.reshape(3, 1, width), (0, sp, 0)
        ).reshape(-1)
        up_bias_full = lax.dynamic_update_slice(
            jnp.zeros((FF,), F32), up_bias_grad, (sp * ff_here,)
        )
        g_sum = jnp.sum(g_here, 0)
        full = (
            jnp.sum(dnormed_1 * xhat, 0),
            jnp.sum(dnormed_1, 0),
            jnp.sum(dnormed_2 * xhat, 0),
            jnp.sum(dnormed_2, 0),
            qkv_bias_full,
            g_sum,
            up_bias_full,
        )
        packed = jnp.concatenate([item.reshape(n_all, -1) for item in full], 1)
        packed = jnp.pad(packed, ((0, 0), (0, 128 - packed.shape[1])))
        mine = lax.psum_scatter(packed, BOTH, scatter_dimension=0, tiled=True).reshape(-1)
        parts = []
        at = 0
        for item in full:
            size = item.size // n_all
            parts.append(mine[at : at + size])
            at += size
        return (
            hidden_out,
            hidden_grad,
            parts[0],
            parts[1],
            parts[2],
            parts[3],
            qkv_own,
            parts[4],
            dense_own,
            parts[5],
            up_own,
            parts[6],
            down_own,
            parts[5],
        )

    return local


def solution(mesh):
    matrix = P(BOTH, None)
    vector = P(BOTH)
    ins = (matrix, matrix) + (vector,) * 4 + (matrix, vector) * 4
    outs = (matrix, matrix) + (vector,) * 4 + (matrix, vector) * 4
    return jax.shard_map(
        make_local(mesh.shape["dp"], mesh.shape["sp"]),
        mesh=mesh,
        in_specs=ins,
        out_specs=outs,
        check_vma=False,
    )
```

time: 1200 us -> 1470 us (1.23)
  waiting for transfers between devices: 86.1 us -> 1110 us
  blocking collectives: 497 us -> 203 us
  starting transfers between devices: 285 us -> 33.3 us
  local copies, waits for them, and re-layouts: 172 us -> 30.3 us
  matrix products: 99.6 us -> 62 us
    reduce_scatter x1 -> x5, waiting for transfers between devices: 0.01 us -> 735 us  [the longest x1 226 us: local(): lax.psum_scatter(down_grad, 'dp', scatter_dimension=0, tiled=True)]
    unnamed x3 -> x0, blocking collectives: 497 us -> none
    unnamed x101 -> x13, waiting for transfers between devices: 10.3 us -> 328 us
    unnamed x96 -> x2, starting transfers between devices: 266 us -> 0.04 us
    all_gather x0 -> x3, blocking collectives: none -> 196 us  [the longest x1 82.3 us: local(): qkv_t = lax.all_gather(qkv_part, 'dp', axis=0, tiled=True)]
    unnamed x306 -> x88, local copies, waits for them, and re-layouts: 136 us -> 11.5 us
    dot_general x18 -> x9, matrix products: 69.9 us -> 29.7 us  [the longest x4 10.8 us: dot(): return jnp.dot(left, right, preferred_element_type=F32)]
    all_to_all x4 -> x3, waiting for transfers between devices: 26.3 us -> 0.01 us  [the longest x1 0.01 us: local(): lax.all_to_all(qkv_weight.reshape(-1, 3, n_sp, width).transpose(0, 2, 1,...]
  transfers between devices with their start and end apart: 105 -> 18, of which waited for: 6 -> 9; matrix products, arithmetic and copies ran while one was open for 55% -> 6% of each run, Pallas kernels for 0% -> 0%
where the time goes in v1:
time: 1470 us
  waiting for transfers between devices  1110 us (76%)
  blocking collectives  203 us (14%)
  matrix products  62 us (4%)
  starting transfers between devices  33.3 us (2%)
  local copies, waits for them, and re-layouts  30.3 us (2%)
  other arithmetic  14.9 us (1%)
    unnamed x13, waiting for transfers between devices  328 us
    reduce_scatter x1, waiting for transfers between devices, local(): lax.psum_scatter(down_grad, 'dp', scatter_dimension=0, tiled=True)  226 us
    reduce_scatter x1, waiting for transfers between devices, local(): up_own = lax.psum_scatter(up_grad, 'dp', scatter_dimension=0, tiled=True)  220 us
    reduce_scatter x1, waiting for transfers between devices, local(): lax.psum_scatter(jnp.pad(dense_grad.reshape(n_dp, -1, d_model), ((0, 0),...  216 us
    all_gather x1, blocking collectives, local(): qkv_t = lax.all_gather(qkv_part, 'dp', axis=0, tiled=True)  82.3 us
    all_gather x1, blocking collectives, local(): dense_t = lax.all_gather(dense_part, 'dp', axis=0, tiled=True)  80.5 us
    all_gather x1, waiting for transfers between devices, local(): down_t = lax.all_gather(down_part, 'dp', axis=0, tiled=True)  41.7 us
    reduce_scatter x1, waiting for transfers between devices, local(): out_sum = lax.psum_scatter(out_part, 'sp', scatter_dimension=0, tiled=True)  38.7 us
  transfers between devices with their start and end apart: 18, of which 9 were waited for; matrix products, arithmetic and copies ran while one was open for 6% of the time, Pallas kernels for 0%

profile of v1, /device:TPU:1, one launch (start us, length us, event | category | flops | bytes accessed | tf_op | source)
XLA Modules:
  0.0 1465.6 jit_solution(2094343523021867025)
XLA Ops:
  8.7 7.9 all_to_all.40
  17.3 5.4 collective-permute-start.1
  27.7 5.7 collective-permute-start
  33.4 5.4 concatenate.20
  38.9 32.7 %all-gather.1 = bf16[128,1,128]{2,1,0:T(2,128)(2,1)S(1)} all-gather(bf16[1,1,128]{2,1,0:T(2,128)(2,1)S(1)} %pad_bitcast_fusion), channel_id=2, replica_groups=mesh['dp'=32,'sp'=4] {'dp','sp'}, dimensions={0}, use_global_device_ids=true | all-gather | bytes 33024 | tf_op jit(solution)/shard_map/all_gather | solution.py:95
  74.2 80.5 %all-gather.2 = bf16[32,6,768]{2,1,0:T(8,128)(2,1)S(1)} all-gather(bf16[1,6,768]{2,1,0:T(8,128)(2,1)S(1)} %bitcast.140), channel_id=1, replica_groups=mesh['dp'=32,'sp'=4] {'dp'}, dimensions={0}, use_global_device_ids=true | all-gather | bytes 304128 | tf_op jit(solution)/shard_map/all_gather | solution.py:120
  154.9 82.3 %all_gather.25 = bf16[768,576]{1,0:T(8,128)(2,1)S(1)} all-gather(bf16[24,576]{1,0:T(8,128)(2,1)S(1)} %reshape.239), channel_id=1, replica_groups=mesh['dp'=32,'sp'=4] {'dp'}, dimensions={0}, use_global_device_ids=true | all-gather | bytes 912384 | tf_op jit(solution)/shard_map/all_gather | solution.py:119
  244.8 8.3 fusion.73
  255.2 6.7 multiply_reduce_fusion
  263.8 4.2 multiply_convert_fusion
  280.5 5.6 multiply_convert_fusion.1
  286.1 41.7 %all-gather.12.cloned.1.call-done = bf16[768,768]{1,0:T(8,128)(2,1)} async-done(((bf16[24,768]{1,0:T(8,128)(2,1)}), bf16[768,768]{1,0:T(8,128)(2,1)}) %all-gather.12.cloned.1.call-update) | async-done | bytes 1179664 | tf_op jit(solution)/shard_map/all_gather | solution.py:118
  336.2 4.3 fusion.76
  347.4 6.1 fusion.35
  362.4 192.0 %reduce-scatter.19.cloned.1.call-done = f32[24,576]{1,0:T(8,128)} async-done(((f32[768,576]{1,0:T(8,128)}), f32[24,576]{1,0:T(8,128)}) %reduce-scatter.19.cloned.1.call-update) | async-done | bytes 55312
  555.8 6.0 all-to-all-start.2
  561.8 219.6 %reduce-scatter.15.cloned.1.call-done = f32[24,768]{1,0:T(8,128)} async-done(((f32[768,768]{1,0:T(8,128)}), f32[24,768]{1,0:T(8,128)}) %reduce-scatter.15.cloned.1.call-update) | async-done | bytes 73744 | tf_op jit(solution)/shard_map/reduce_scatter | solution.py:192
  782.9 226.5 %reduce-scatter.17.cloned.1.call-done = f32[24,768]{1,0:T(8,128)} async-done(((f32[768,768]{1,0:T(8,128)}), f32[24,768]{1,0:T(8,128)}) %reduce-scatter.17.cloned.1.call-update) | async-done | bytes 73744 | tf_op jit(solution)/shard_map/reduce_scatter | solution.py:193
  1009.4 4.4 collective-permute-start.3
  1013.8 34.0 %reduce-scatter.11.cloned.1.call-done = f32[256,768]{1,0:T(8,128)} async-done(((f32[1024,768]{1,0:T(8,128)}), f32[256,768]{1,0:T(8,128)}) %reduce-scatter.11.cloned.1.call-update) | async-done | bytes 786448 | tf_op jit(solution)/shard_map/reduce_scatter | solution.py:177
  1049.3 38.7 %reduce-scatter.9.cloned.1.call-done = f32[256,768]{1,0:T(8,128)} async-done(((f32[1024,768]{1,0:T(8,128)}), f32[256,768]{1,0:T(8,128)}) %reduce-scatter.9.cloned.1.call-update) | async-done | bytes 786448 | tf_op jit(solution)/shard_map/reduce_scatter | solution.py:174
  1095.3 216.0 %reduce-scatter.13.cloned.1.call-done = f32[1,8,768]{2,1,0:T(8,128)} async-done(((f32[32,8,768]{2,1,0:T(8,128)}), f32[1,8,768]{2,1,0:T(8,128)}) %reduce-scatter.13.cloned.1.call-update) | async-done | bytes 24592 | tf_op jit(solution)/shard_map/reduce_scatter | solution.py:195
  1312.0 4.4 collective-permute-start.2
  1319.6 134.6 %all-reduce.7.cloned.1.call-done = f32[128,128]{1,0:T(8,128)} async-done(((f32[128,128]{1,0:T(8,128)}), f32[128,128]{1,0:T(8,128)}) %all-reduce.7.cloned.1.call-update) | async-done | bytes 65552
  (206 shorter events, 77.7 us)
Async XLA Ops:
  7.2 230.8 %all-gather.8.cloned.1.call-start = ((), (), s32[]{:S(2)}) async-start(), calls=%async_computation.10 | async-start | bytes 1966080 | tf_op jit(solution)/shard_map/all_gather | solution.py:122
  7.9 245.2 %all-gather.14.cloned.1.call-start = ((), (), s32[]{:S(2)}) async-start(), calls=%async_computation.14 | async-start | bytes 1966080 | tf_op jit(solution)/shard_map/all_gather | solution.py:123
  8.7 271.8 %all-gather.10.cloned.1.call-start = ((), (), s32[]{:S(2)}) async-start(), calls=%async_computation.11 | async-start | bytes 1216512 | tf_op jit(solution)/shard_map/all_gather | solution.py:117
  17.3 56.9 %collective-permute-start.1 = (bf16[6,768]{1,0:T(8,128)(2,1)}, bf16[6,768]{1,0:T(8,128)(2,1)S(1)}, u32[]{:S(2)}, u32[]{:S(2)}) collective-permute-start(bf16[6,768]{1,0:T(8,128)(2,1)} %param.22), channel_id=1, source_target_pairs={{0,0},{32,1},{64,2},{96,3},{1,4},{33,5},{65,6},{97,7},{2,8},{34,9}... | collective-permute-start | bytes 27656 | tf_op jit(solution)/shard_map/ppermute | solution.py:116
  24.3 130.5 %all-to-all-start.1 = ((bf16[6,4,576]{2,0,1:T(8,128)(2,1)}), bf16[6,4,576]{2,0,1:T(8,128)(2,1)S(1)}, u32[]{:S(2)}, u32[]{:S(2)}) async-start(bf16[6,4,576]{2,0,1:T(8,128)(2,1)} %copy.54), calls=%async_computation.1 | async-start | bytes 81920 | tf_op jit(solution)/shard_map/all_to_all | solution.py:109
  27.6 300.2 %all-gather.12.cloned.1.call-start = ((), (), s32[]{:S(2)}) async-start(), calls=%async_computation.12 | async-start | bytes 1216512 | tf_op jit(solution)/shard_map/all_gather | solution.py:118
  27.7 209.6 %collective-permute-start = (bf16[24,768]{1,0:T(8,128)(2,1)}, bf16[24,768]{1,0:T(8,128)(2,1)S(1)}, u32[]{:S(2)}, u32[]{:S(2)}) collective-permute-start(bf16[24,768]{1,0:T(8,128)(2,1)} %param.26), channel_id=1, source_target_pairs={{0,0},{32,1},{64,2},{96,3},{1,4},{33,5},{65,6},{97,7},{2,8},{34,9}... | collective-permute-start | bytes 110600 | tf_op jit(solution)/shard_map/ppermute | solution.py:108
  72.5 171.1 %copy-start.10 = (f32[1024,8]{0,1:T(8,128)}, f32[1024,8]{0,1:T(8,128)S(1)}, u32[]{:S(2)}) copy-start(f32[1024,8]{0,1:T(8,128)S(1)} %get-tuple-element.54) | copy-start | bytes 98308
  74.2 169.1 %copy-start.25 = (f32[768]{0:T(1024)}, f32[768]{0:T(1024)S(1)}, u32[]{:S(2)}) copy-start(f32[768]{0:T(1024)S(1)} %add.149) | copy-start | bytes 9220
  154.8 98.3 %copy-start.6 = (bf16[192,768]{1,0:T(8,128)(2,1)}, bf16[192,768]{1,0:T(8,128)(2,1)S(1)}, u32[]{:S(2)}) copy-start(bf16[192,768]{1,0:T(8,128)(2,1)S(1)} %reshape.260) | copy-start | bytes 884740
  237.9 316.5 %reduce-scatter.19.cloned.1.call-start = ((), (), s32[]{:S(2)}) async-start(), calls=%async_computation.20 | async-start | bytes 2027520
  255.2 8.6 slice-start.2
  279.8 501.6 %reduce-scatter.15.cloned.1.call-start = ((), (), s32[]{:S(2)}) async-start(), calls=%async_computation.17 | async-start | bytes 2433024 | tf_op jit(solution)/shard_map/reduce_scatter | solution.py:192
  280.5 47.4 %copy-start.3 = (bf16[1024,768]{1,0:T(8,128)(2,1)S(1)}, bf16[1024,768]{1,0:T(8,128)(2,1)}, u32[]{:S(2)}) copy-start(bf16[1024,768]{1,0:T(8,128)(2,1)} %all-gather.14.cloned.1.call-done) | copy-start | bytes 4718596
  336.2 673.2 %reduce-scatter.17.cloned.1.call-start = ((), (), s32[]{:S(2)}) async-start(), calls=%async_computation.18 | async-start | bytes 2433024 | tf_op jit(solution)/shard_map/reduce_scatter | solution.py:193
  340.5 707.3 %reduce-scatter.11.cloned.1.call-start = ((), (), s32[]{:S(2)}) async-start(), calls=%async_computation.15 | async-start | bytes 3932160 | tf_op jit(solution)/shard_map/reduce_scatter | solution.py:177
  347.3 740.7 %reduce-scatter.9.cloned.1.call-start = ((), (), s32[]{:S(2)}) async-start(), calls=%async_computation.13 | async-start | bytes 3932160 | tf_op jit(solution)/shard_map/reduce_scatter | solution.py:174
  358.4 952.9 %reduce-scatter.13.cloned.1.call-start = ((), (), s32[]{:S(2)}) async-start(), calls=%async_computation.16 | async-start | bytes 811008 | tf_op jit(solution)/shard_map/reduce_scatter | solution.py:195
  359.2 728.8 %copy-start.4 = (bf16[256,768]{1,0:T(8,128)(2,1)S(1)}, bf16[256,768]{1,0:T(8,128)(2,1)}, u32[]{:S(2)}) copy-start(bf16[256,768]{1,0:T(8,128)(2,1)} %param.15) | copy-start | bytes 1179652
  555.8 535.8 %all-to-all-start.2 = ((f32[4,6,576]{2,1,0:T(8,128)}), f32[4,6,576]{2,1,0:T(8,128)S(1)}, u32[]{:S(2)}, u32[]{:S(2)}) async-start(f32[4,6,576]{2,1,0:T(8,128)} %reshape.250), calls=%async_computation.4 | async-start | bytes 163840 | tf_op jit(solution)/shard_map/all_to_all | solution.py:205
  561.8 892.4 %all-reduce.7.cloned.1.call-start = ((), (), s32[]{:S(2)}) async-start(), calls=%async_computation.19 | async-start | bytes 131072
  1009.4 310.2 %collective-permute-start.3 = (f32[24,768]{1,0:T(8,128)}, f32[24,768]{1,0:T(8,128)S(1)}, u32[]{:S(2)}, u32[]{:S(2)}) collective-permute-start(f32[24,768]{1,0:T(8,128)} %reduce-scatter.17.cloned.1.call-done), channel_id=1, source_target_pairs={{0,0},{1,32},{2,64},{3,96},{4,1},{5,33},{6,65},{7,97},{8,2},{9,34}... | collective-permute-start | bytes 221192 | tf_op jit(solution)/shard_map/ppermute | solution.py:208
  1091.6 228.0 %all-to-all-start.3 = ((f32[4,6,768]{2,1,0:T(8,128)}), f32[4,6,768]{2,1,0:T(8,128)S(1)}, u32[]{:S(2)}, u32[]{:S(2)}) async-start(f32[4,6,768]{2,1,0:T(8,128)} %reshape.253), calls=%async_computation.7 | async-start | bytes 196608 | tf_op jit(solution)/shard_map/all_to_all | solution.py:202
  1312.0 6.6 collective-permute-start.2
  (34 other events, 120.3 us)
Sparse Core Ops, SparseCore 0:
  9.7 29.2 all-gather.7
  40.6 25.6 all-gather.13
  69.4 66.6 all-gather.9
  238.0 89.7 all-gather.11
  332.5 221.7 reduce-scatter.18
  559.1 222.2 reduce-scatter.14
  787.1 222.2 reduce-scatter.16
  1011.8 35.9 reduce-scatter.10
  1050.2 37.7 reduce-scatter.8
  1092.6 218.6 reduce-scatter.12
  1317.3 136.8 all-reduce.6

commit v2 on v1

--- a/solution.py
+++ b/solution.py
@@ -1,6 +1,10 @@
+import functools
+
 import jax
 import jax.numpy as jnp
 from jax import lax
+from jax.experimental import pallas as pl
+from jax.experimental.pallas import tpu as pltpu
 from jax.sharding import PartitionSpec as P
 
 D = 768
@@ -49,14 +53,353 @@
     )
 
 
+MESH = pl.DeviceIdType.MESH
+SMALL = 128
+
+
+def place():
+    return lax.axis_index("dp"), lax.axis_index("sp")
+
+
+def rows_paths(n_dp, n_sp, dp, sp):
+    mine = dp * n_sp + sp
+
+    def owner(b):
+        line = sp * n_dp + b
+        return line // n_sp, lax.rem(line, n_sp)
+
+    return mine // n_dp, lax.rem(mine, n_dp), owner
+
+
+def greet(n_dp, n_sp, dp, sp, to_rows, count_rows):
+    barrier = pltpu.get_barrier_semaphore()
+
+    def signal(d, s):
+        pl.semaphore_signal(barrier, inc=1, device_id=(d, s), device_id_type=MESH)
+
+    @pl.loop(1, n_dp)
+    def _(k):
+        signal(lax.rem(dp + k, n_dp), sp)
+
+    for k in range(1, n_sp):
+        signal(dp, lax.rem(sp + k, n_sp))
+
+    @pl.loop(0, n_dp)
+    def _(k):
+        d, s = to_rows(k)
+
+        @pl.when(jnp.logical_or(d != dp, s != sp))
+        def _():
+            signal(d, s)
+
+    pl.semaphore_wait(barrier, n_dp - 1 + n_sp - 1 + count_rows)
+
+
+def gather_kernel(
+    n_dp, n_sp, x_ref, g_ref, cols_ref, rows_ref,
+    x_out, g_out, cols_out, rows_out,
+    stage, tight_wide, tight,
+    local_sem, x_send, x_recv, g_send, g_recv, p_send, p_recv, c_send, c_recv, r_send, r_recv,
+):
+    dp, sp = place()
+    column, slot, owner = rows_paths(n_dp, n_sp, dp, sp)
+    count = n_dp - jnp.where(column == sp, 1, 0)
+    greet(n_dp, n_sp, dp, sp, owner, count)
+    tokens = x_ref.shape[0]
+    own_rows = pl.ds(pl.multiple_of(sp * tokens, tokens), tokens)
+
+    def copy(src, dst, send, recv, d, s):
+        return pltpu.make_async_remote_copy(
+            src_ref=src, dst_ref=dst, send_sem=send, recv_sem=recv,
+            device_id=(d, s), device_id_type=MESH,
+        )
+
+    def piece(k):
+        t = lax.rem(sp + k, n_sp)
+        return copy(cols_ref.at[t], stage.at[sp], p_send.at[k - 1], p_recv.at[sp], dp, t)
+
+    def tokens_of(k):
+        t = lax.rem(sp + k, n_sp)
+        return (
+            copy(x_ref, x_out.at[own_rows], x_send.at[k - 1], x_recv.at[sp], dp, t),
+            copy(g_ref, g_out.at[own_rows], g_send.at[k - 1], g_recv.at[sp], dp, t),
+        )
+
+    for k in range(1, n_sp):
+        piece(k).start()
+    own = (
+        pltpu.make_async_copy(cols_ref.at[sp], stage.at[sp], p_recv.at[sp]),
+        pltpu.make_async_copy(x_ref, x_out.at[own_rows], x_recv.at[sp]),
+        pltpu.make_async_copy(g_ref, g_out.at[own_rows], g_recv.at[sp]),
+    )
+    for item in own:
+        item.start()
+
+    def rows_to(k):
+        d = lax.rem(dp + k, n_dp)
+        return copy(rows_ref, rows_out.at[slot], r_send.at[k], r_recv.at[slot], d, column)
+
+    @pl.when(column == sp)
+    def _():
+        pltpu.make_async_copy(rows_ref, rows_out.at[slot], r_recv.at[slot]).start()
+
+    @pl.when(column != sp)
+    def _():
+        rows_to(0).start()
+
+    @pl.loop(1, n_dp)
+    def _(k):
+        rows_to(k).start()
+
+    for k in range(1, n_sp):
+        for item in tokens_of(k):
+            item.start()
+
+    for s in range(n_sp):
+        pltpu.make_async_copy(cols_ref.at[s], stage.at[s], p_recv.at[s]).wait()
+    part = stage.shape[1]
+    for s in range(n_sp):
+        tight_wide[s * part : (s + 1) * part, :] = stage[s].astype(F32)
+    tight[...] = tight_wide[...].astype(BF)
+
+    def cols_to(k):
+        d = lax.rem(dp + k, n_dp)
+        return copy(tight, cols_out.at[dp], c_send.at[k], c_recv.at[dp], d, sp)
+
+    own_cols = pltpu.make_async_copy(tight, cols_out.at[dp], c_recv.at[dp])
+    own_cols.start()
+
+    @pl.loop(1, n_dp)
+    def _(k):
+        cols_to(k).start()
+
+    @pl.loop(0, n_dp)
+    def _(b):
+        pltpu.make_async_copy(tight, cols_out.at[b], c_recv.at[b]).wait()
+        pltpu.make_async_copy(rows_ref, rows_out.at[b], r_recv.at[b]).wait()
+
+    for s in range(n_sp):
+        there = pl.ds(s * tokens, tokens)
+        pltpu.make_async_copy(x_ref, x_out.at[there], x_recv.at[s]).wait()
+        pltpu.make_async_copy(g_ref, g_out.at[there], g_recv.at[s]).wait()
+
+    for k in range(1, n_sp):
+        piece(k).wait_send()
+        for item in tokens_of(k):
+            item.wait_send()
+
+    @pl.when(column != sp)
+    def _():
+        rows_to(0).wait_send()
+
+    @pl.loop(1, n_dp)
+    def _(k):
+        rows_to(k).wait_send()
+        cols_to(k).wait_send()
+
+
+def gather_all(n_dp, n_sp, x, g, cols, rows):
+    part = cols.shape[1]
+    tokens, d_model = x.shape
+    dma = pltpu.SemaphoreType.DMA
+    return pl.pallas_call(
+        functools.partial(gather_kernel, n_dp, n_sp),
+        out_shape=(
+            jax.ShapeDtypeStruct((tokens * n_sp, d_model), BF),
+            jax.ShapeDtypeStruct((tokens * n_sp, d_model), BF),
+            jax.ShapeDtypeStruct((n_dp, part * n_sp, cols.shape[2]), BF),
+            jax.ShapeDtypeStruct((n_dp,) + rows.shape, BF),
+        ),
+        in_specs=[pl.BlockSpec(memory_space=pl.ANY)] * 4,
+        out_specs=(pl.BlockSpec(memory_space=pl.ANY),) * 4,
+        scratch_shapes=[
+            pltpu.VMEM(cols.shape, BF),
+            pltpu.VMEM((part * n_sp, cols.shape[2]), F32),
+            pltpu.VMEM((part * n_sp, cols.shape[2]), BF),
+            dma,
+        ]
+        + [dma((n_sp,))] * 6
+        + [dma((n_dp,))] * 4,
+        compiler_params=pltpu.CompilerParams(collective_id=0, has_side_effects=True),
+        name="gather_all",
+    )(x, g, cols, rows)
+
+
+def reduce_kernel(
+    n_dp, n_sp, cols_ref, rows_ref, small_ref, out_ref, dx_ref,
+    up_out, qkv_out, rows_out, small_out, hidden_out, dxhat_out,
+    cols_in, rows_in, small_in, out_in, dx_in,
+    stage, land, small_stage, small_land,
+    c_send, c_recv, r_send, r_recv, s_send, s_recv,
+    o_send, o_recv, d_send, d_recv, p_send, p_recv, t_send, t_recv,
+):
+    dp, sp = place()
+    column, slot, owner = rows_paths(n_dp, n_sp, dp, sp)
+    count = n_dp - jnp.where(column == sp, 1, 0)
+    greet(n_dp, n_sp, dp, sp, lambda k: (lax.rem(dp + k, n_dp), column), count)
+
+    def copy(src, dst, send, recv, d, s):
+        return pltpu.make_async_remote_copy(
+            src_ref=src, dst_ref=dst, send_sem=send, recv_sem=recv,
+            device_id=(d, s), device_id_type=MESH,
+        )
+
+    def cols_to(k):
+        d = lax.rem(dp + k, n_dp)
+        return (
+            copy(cols_ref.at[d], cols_in.at[dp], c_send.at[k], c_recv.at[dp], d, sp),
+            copy(small_ref.at[d], small_in.at[dp], s_send.at[k], s_recv.at[dp], d, sp),
+        )
+
+    def rows_to(b):
+        d, s = owner(b)
+        return copy(rows_ref.at[b], rows_in.at[dp], r_send.at[b], r_recv.at[dp], d, s)
+
+    def place_of(k):
+        return lax.rem(slot + k, n_dp)
+
+    def away(b):
+        d, s = owner(b)
+        return jnp.logical_or(d != dp, s != sp)
+
+    def tokens_to(k):
+        t = lax.rem(sp + k, n_sp)
+        return (
+            copy(out_ref.at[t], out_in.at[sp], o_send.at[k], o_recv.at[sp], dp, t),
+            copy(dx_ref.at[t], dx_in.at[sp], d_send.at[k], d_recv.at[sp], dp, t),
+        )
+
+    pltpu.make_async_copy(cols_ref.at[dp], cols_in.at[dp], c_recv.at[dp]).start()
+    pltpu.make_async_copy(small_ref.at[dp], small_in.at[dp], s_recv.at[dp]).start()
+    pltpu.make_async_copy(out_ref.at[sp], out_in.at[sp], o_recv.at[sp]).start()
+    pltpu.make_async_copy(dx_ref.at[sp], dx_in.at[sp], d_recv.at[sp]).start()
+
+    @pl.when(column == sp)
+    def _():
+        pltpu.make_async_copy(rows_ref.at[slot], rows_in.at[dp], r_recv.at[dp]).start()
+
+    @pl.loop(1, n_dp)
+    def _(k):
+        for item in cols_to(k):
+            item.start()
+
+    for k in range(1, n_sp):
+        for item in tokens_to(k):
+            item.start()
+
+    @pl.loop(0, n_dp)
+    def _(k):
+        b = place_of(k)
+
+        @pl.when(away(b))
+        def _():
+            rows_to(b).start()
+
+    @pl.loop(0, n_dp)
+    def _(b):
+        pltpu.make_async_copy(cols_ref.at[b], cols_in.at[b], c_recv.at[b]).wait()
+        pltpu.make_async_copy(small_ref.at[b], small_in.at[b], s_recv.at[b]).wait()
+
+    part = land.shape[1]
+    small_stage[...] = jnp.sum(small_in[...], 0)
+    total = jnp.sum(cols_in[...].astype(F32), 0)
+    for t in range(n_sp):
+        stage[t] = total[t * part : (t + 1) * part, :]
+
+    def piece(k):
+        t = lax.rem(sp + k, n_sp)
+        return (
+            copy(stage.at[t], land.at[sp], p_send.at[k], p_recv.at[sp], dp, t),
+            copy(small_stage, small_land.at[sp], t_send.at[k], t_recv.at[sp], dp, t),
+        )
+
+    pltpu.make_async_copy(stage.at[sp], land.at[sp], p_recv.at[sp]).start()
+    pltpu.make_async_copy(small_stage, small_land.at[sp], t_recv.at[sp]).start()
+    for k in range(1, n_sp):
+        for item in piece(k):
+            item.start()
+
+    @pl.loop(0, n_dp)
+    def _(b):
+        pltpu.make_async_copy(rows_ref.at[b], rows_in.at[b], r_recv.at[b]).wait()
+
+    rows_out[...] = jnp.sum(rows_in[...].astype(F32), 0)
+
+    for s in range(n_sp):
+        pltpu.make_async_copy(out_ref.at[s], out_in.at[s], o_recv.at[s]).wait()
+        pltpu.make_async_copy(dx_ref.at[s], dx_in.at[s], d_recv.at[s]).wait()
+    hidden_out[...] = jnp.sum(out_in[...].astype(F32), 0)
+    dxhat_out[...] = jnp.sum(dx_in[...].astype(F32), 0)
+
+    for s in range(n_sp):
+        pltpu.make_async_copy(stage.at[s], land.at[s], p_recv.at[s]).wait()
+        pltpu.make_async_copy(small_stage, small_land.at[s], t_recv.at[s]).wait()
+    ff_here = up_out.shape[1] // n_sp
+    width = qkv_out.shape[1] // 3 // n_sp
+    for s in range(n_sp):
+        block = land[s]
+        up_out[:, s * ff_here : (s + 1) * ff_here] = block[:, :ff_here]
+        for j in range(3):
+            to = (j * n_sp + s) * width
+            at = ff_here + j * width
+            qkv_out[:, to : to + width] = block[:, at : at + width]
+    small_out[...] = jnp.sum(small_land[...], 0)
+
+    for k in range(1, n_sp):
+        for item in piece(k) + tokens_to(k):
+            item.wait_send()
+
+    @pl.loop(1, n_dp)
+    def _(k):
+        for item in cols_to(k):
+            item.wait_send()
+
+    @pl.loop(0, n_dp)
+    def _(b):
+        @pl.when(away(b))
+        def _():
+            rows_to(b).wait_send()
+
+
+def reduce_all(n_dp, n_sp, cols, rows, small, out, dx):
+    part = cols.shape[1] // n_sp
+    d_model = rows.shape[2]
+    dma = pltpu.SemaphoreType.DMA
+    vmem = pl.BlockSpec(memory_space=pltpu.VMEM)
+    return pl.pallas_call(
+        functools.partial(reduce_kernel, n_dp, n_sp),
+        out_shape=(
+            jax.ShapeDtypeStruct((part, FF), F32),
+            jax.ShapeDtypeStruct((part, 3 * d_model), F32),
+            jax.ShapeDtypeStruct(rows.shape[1:], F32),
+            jax.ShapeDtypeStruct(small.shape[1:], F32),
+            jax.ShapeDtypeStruct(out.shape[1:], F32),
+            jax.ShapeDtypeStruct(dx.shape[1:], F32),
+        ),
+        in_specs=[pl.BlockSpec(memory_space=pl.ANY)] * 5,
+        out_specs=(vmem,) * 6,
+        scratch_shapes=[
+            pltpu.VMEM(cols.shape, BF),
+            pltpu.VMEM(rows.shape, BF),
+            pltpu.VMEM(small.shape, F32),
+            pltpu.VMEM(out.shape, BF),
+            pltpu.VMEM(dx.shape, BF),
+            pltpu.VMEM((n_sp, part, cols.shape[2]), F32),
+            pltpu.VMEM((n_sp, part, cols.shape[2]), F32),
+            pltpu.VMEM(small.shape[1:], F32),
+            pltpu.VMEM((n_sp,) + small.shape[1:], F32),
+        ]
+        + [dma((n_dp,))] * 6
+        + [dma((n_sp,))] * 8,
+        compiler_params=pltpu.CompilerParams(
+            collective_id=1, has_side_effects=True, vmem_limit_bytes=40 * 1024 * 1024
+        ),
+        name="reduce_all",
+    )(cols, rows, small, out, dx)
+
+
 def make_local(n_dp, n_sp):
     n_all = n_dp * n_sp
-    to_slice = []
-    for dp in range(n_dp):
-        for sp in range(n_sp):
-            to_slice.append((sp * n_dp + dp, dp * n_sp + sp))
-    to_owner = [(b, a) for a, b in to_slice]
-
     def local(
         hidden_in,
         cotangent,
@@ -91,8 +434,29 @@
         )
         sizes = [item.shape[0] for item in small]
         total = sum(sizes)
-        packed = jnp.pad(jnp.concatenate(small), (0, 128 - total)).reshape(1, 128)
-        packed = lax.all_gather(packed, BOTH, axis=0, tiled=True).astype(F32)
+        part = up_weight.shape[0]
+        packed = jnp.pad(jnp.concatenate(small), (0, SMALL - total)).reshape(1, 1, SMALL)
+        packed = jnp.pad(jnp.broadcast_to(packed, (n_sp, 1, SMALL)), ((0, 0), (0, part - 1), (0, 0)))
+        cols = jnp.concatenate(
+            [
+                up_weight.reshape(part, n_sp, ff_here).transpose(1, 0, 2),
+                qkv_weight.reshape(part, 3, n_sp, width)
+                .transpose(2, 0, 1, 3)
+                .reshape(n_sp, part, 3 * width),
+                packed,
+            ],
+            2,
+        )
+        block = down_weight.shape[0]
+        fill = jnp.zeros((-(block + part) % 16, d_model), BF)
+        rows = jnp.concatenate([down_weight, dense_weight, fill], 0)
+        x_seq, g_seq, cols, rows = gather_all(n_dp, n_sp, hidden_in, cotangent, cols, rows)
+        split = ff_here + 3 * width
+        up_t = cols[:, :, :ff_here].reshape(d_model, ff_here)
+        qkv_t = cols[:, :, ff_here:split].reshape(d_model, 3 * width)
+        down_t = rows[:, :block].reshape(ff_here, d_model)
+        dense_t = rows[:, block : block + part].reshape(width, d_model)
+        packed = cols[:, ::part, split:].reshape(n_all, SMALL).astype(F32)
         vectors = []
         at = 0
         for size in sizes:
@@ -101,26 +465,7 @@
         gain_1, shift_1, gain_2, shift_2, qkv_add, dense_add, up_add, down_add = vectors
         qkv_add = lax.dynamic_slice_in_dim(qkv_add.reshape(3, n_sp, width), sp, 1, 1).reshape(-1)
         up_add = lax.dynamic_slice_in_dim(up_add, sp * ff_here, ff_here, 0)
-
-        up_part = lax.all_to_all(
-            up_weight.reshape(-1, n_sp, ff_here), "sp", split_axis=1, concat_axis=0, tiled=True
-        ).reshape(-1, ff_here)
-        down_part = lax.ppermute(down_weight, BOTH, to_slice)
-        qkv_part = lax.all_to_all(
-            qkv_weight.reshape(-1, 3, n_sp, width).transpose(0, 2, 1, 3).reshape(-1, n_sp, 3 * width),
-            "sp",
-            split_axis=1,
-            concat_axis=0,
-            tiled=True,
-        ).reshape(-1, 3 * width)
-        dense_part = lax.ppermute(dense_weight, BOTH, to_slice)
-        up_t = lax.all_gather(up_part, "dp", axis=0, tiled=True)
-        down_t = lax.all_gather(down_part, "dp", axis=0, tiled=True)
-        qkv_t = lax.all_gather(qkv_part, "dp", axis=0, tiled=True)
-        dense_t = lax.all_gather(dense_part, "dp", axis=0, tiled=True)
-
-        x_seq = lax.all_gather(hidden_in, "sp", axis=0, tiled=True).astype(F32)
-        g_seq = lax.all_gather(cotangent, "sp", axis=0, tiled=True)
+        x_seq = x_seq.astype(F32)
         length = x_seq.shape[0]
         xhat, rstd = norm_components(x_seq)
         normed_1 = (xhat * gain_1 + shift_1).astype(BF)
@@ -171,14 +516,53 @@
         qkv_bias_grad = jnp.sum(dqkv.astype(F32), 0)
         dnormed_1 = contract_cols(dqkv, qkv_t)
 
-        out_sum = lax.psum_scatter(out_part, "sp", scatter_dimension=0, tiled=True)
+        g_here = cotangent.astype(F32)
+        zeros_qkv = jnp.zeros((3, n_sp, width), F32)
+        qkv_bias_full = lax.dynamic_update_slice(
+            zeros_qkv, qkv_bias_grad.reshape(3, 1, width), (0, sp, 0)
+        ).reshape(-1)
+        up_bias_full = lax.dynamic_update_slice(
+            jnp.zeros((FF,), F32), up_bias_grad, (sp * ff_here,)
+        )
+        full = (
+            jnp.sum(dnormed_1 * xhat, 0),
+            jnp.sum(dnormed_1, 0),
+            jnp.sum(dnormed_2 * xhat, 0),
+            jnp.sum(dnormed_2, 0),
+            qkv_bias_full,
+            jnp.sum(g_here, 0),
+            up_bias_full,
+        )
+        packed = jnp.concatenate([item.reshape(n_all, -1) for item in full], 1)
+        packed = jnp.pad(packed, ((0, 0), (0, SMALL - packed.shape[1])))
+        packed = jnp.pad(packed.reshape(n_dp, n_sp, SMALL), ((0, 0), (0, -n_sp % 8), (0, 0)))
+
+        cols = jnp.concatenate([up_grad.astype(BF), qkv_grad.astype(BF)], 1)
+        rows = jnp.concatenate(
+            [
+                down_grad.astype(BF).reshape(n_dp, block, d_model),
+                dense_grad.astype(BF).reshape(n_dp, part, d_model),
+                jnp.zeros((n_dp, fill.shape[0], d_model), BF),
+            ],
+            1,
+        )
+        here = hidden_in.shape[0]
+        up_own, qkv_own, rows_own, packed, out_sum, dxhat = reduce_all(
+            n_dp,
+            n_sp,
+            cols.reshape(n_dp, part * n_sp, split),
+            rows,
+            packed,
+            out_part.astype(BF).reshape(n_sp, here, d_model),
+            (dnormed_1 * gain_1 + dnormed_2 * gain_2).astype(BF).reshape(n_sp, here, d_model),
+        )
+        down_own = rows_own[:block]
+        dense_own = rows_own[block : block + part]
+        mine = lax.dynamic_slice_in_dim(packed, sp, 1, 0).reshape(-1)
+
         x_here = hidden_in.astype(F32)
         hidden_out = (x_here + out_sum + (dense_add + down_add)).astype(BF)
-        dxhat = lax.psum_scatter(
-            dnormed_1 * gain_1 + dnormed_2 * gain_2, "sp", scatter_dimension=0, tiled=True
-        )
         xhat_here, rstd_here = norm_components(x_here)
-        g_here = cotangent.astype(F32)
         hidden_grad = (
             g_here
             + rstd_here
@@ -188,46 +572,6 @@
                 - xhat_here * jnp.mean(dxhat * xhat_here, -1, keepdims=True)
             )
         ).astype(BF)
-
-        up_own = lax.psum_scatter(up_grad, "dp", scatter_dimension=0, tiled=True)
-        down_own = lax.psum_scatter(down_grad, "dp", scatter_dimension=0, tiled=True)
-        qkv_own = lax.psum_scatter(qkv_grad, "dp", scatter_dimension=0, tiled=True)
-        dense_own = lax.psum_scatter(
-            jnp.pad(dense_grad.reshape(n_dp, -1, d_model), ((0, 0), (0, 2), (0, 0))),
-            "dp",
-            scatter_dimension=0,
-            tiled=True,
-        )[0, : dense_weight.shape[0]]
-        rows = up_weight.shape[0]
-        up_own = lax.all_to_all(
-            up_own.reshape(n_sp, rows, ff_here), "sp", split_axis=0, concat_axis=0, tiled=True
-        ).transpose(1, 0, 2).reshape(rows, FF)
-        qkv_own = lax.all_to_all(
-            qkv_own.reshape(n_sp, rows, 3 * width), "sp", split_axis=0, concat_axis=0, tiled=True
-        ).reshape(n_sp, rows, 3, width).transpose(1, 2, 0, 3).reshape(rows, 3 * d_model)
-        down_own = lax.ppermute(down_own, BOTH, to_owner)
-        dense_own = lax.ppermute(dense_own, BOTH, to_owner)
-
-        zeros_qkv = jnp.zeros((3, n_sp, width), F32)
-        qkv_bias_full = lax.dynamic_update_slice(
-            zeros_qkv, qkv_bias_grad.reshape(3, 1, width), (0, sp, 0)
-        ).reshape(-1)
-        up_bias_full = lax.dynamic_update_slice(
-            jnp.zeros((FF,), F32), up_bias_grad, (sp * ff_here,)
-        )
-        g_sum = jnp.sum(g_here, 0)
-        full = (
-            jnp.sum(dnormed_1 * xhat, 0),
-            jnp.sum(dnormed_1, 0),
-            jnp.sum(dnormed_2 * xhat, 0),
-            jnp.sum(dnormed_2, 0),
-            qkv_bias_full,
-            g_sum,
-            up_bias_full,
-        )
-        packed = jnp.concatenate([item.reshape(n_all, -1) for item in full], 1)
-        packed = jnp.pad(packed, ((0, 0), (0, 128 - packed.shape[1])))
-        mine = lax.psum_scatter(packed, BOTH, scatter_dimension=0, tiled=True).reshape(-1)
         parts = []
         at = 0
         for item in full:

time: 1470 us -> 341 us (0.23)
  waiting for transfers between devices: 1110 us -> 0 us
  Pallas kernels: 0 us -> 210 us
  blocking collectives: 203 us -> 0 us
  starting transfers between devices: 33.3 us -> 0 us
    reduce_scatter x5 -> x0, waiting for transfers between devices: 735 us -> none  [the longest x1 226 us: local(): lax.psum_scatter(down_grad, 'dp', scatter_dimension=0, tiled=True)]
    unnamed x13 -> x0, waiting for transfers between devices: 328 us -> none
    pallas_call x0 -> x2, Pallas kernels: none -> 210 us  [the longest x1 105 us: gather_all(): pl.pallas_call(functools.partial(gather_kernel, n_dp, n_sp), out_shape=(j...]
    all_gather x3 -> x0, blocking collectives: 196 us -> none  [the longest x1 82.3 us: local(): qkv_t = lax.all_gather(qkv_part, 'dp', axis=0, tiled=True)]
    all_gather x4 -> x0, waiting for transfers between devices: 41.8 us -> none  [the longest x1 41.7 us: local(): down_t = lax.all_gather(down_part, 'dp', axis=0, tiled=True)]
    ppermute x4 -> x0, starting transfers between devices: 20 us -> none  [the longest x1 5.74 us: local(): down_part = lax.ppermute(down_weight, BOTH, to_slice)]
  transfers between devices with their start and end apart: 18 -> 0, of which waited for: 9 -> 0; matrix products, arithmetic and copies ran while one was open for 6% -> 0% of each run, Pallas kernels for 0% -> 0%
where the time goes in v2:
time: 341 us; the launch traced here: 335 us
  Pallas kernels  210 us (62%)
  matrix products  62.8 us (18%)
  local copies, waits for them, and re-layouts  38.9 us (11%)
  other arithmetic  22.1 us (6%)
    pallas_call x1, Pallas kernels, gather_all(): pl.pallas_call(functools.partial(gather_kernel, n_dp, n_sp), out_shape=(j...  105 us
    pallas_call x1, Pallas kernels, reduce_all(): pl.pallas_call(functools.partial(reduce_kernel, n_dp, n_sp), out_shape=(j...  105 us
    dot_general x4, matrix products, contract_cols(): lax.dot_general(left, right, (((1,), (1,)), ((), ())), preferred_element_...  14 us
    sub x1, matrix products, local(): probs = jnp.exp(scores - top)  10.7 us
    unnamed x107, local copies, waits for them, and re-layouts  9.64 us
    dot_general x4, matrix products, contract_rows(): lax.dot_general(left, right, (((0,), (0,)), ((), ())), preferred_element_...  8.75 us
    dot_general x4, matrix products, dot(): return jnp.dot(left, right, preferred_element_type=F32)  7.98 us
    dot_general x1, matrix products, local(): dv = jnp.einsum('hqk,hqd->khd', probs_low, do, preferred_element_type=F32)  7.61 us

profile of v2, /device:TPU:1, one launch (start us, length us, event | category | flops | bytes accessed | tf_op | source)
XLA Modules:
  0.0 335.0 jit_solution(9280375060340670491)
XLA Ops:
  0.7 5.4 %concatenate.32 = bf16[78]{0:T(256)(128)(2,1)S(1)} concatenate(bf16[6]{0:T(256)(128)(2,1)} %param.16, bf16[6]{0:T(256)(128)(2,1)} %param.17, bf16[6]{0:T(256)(128)(2,1)} %param.18, bf16[6]{0:T(256)(128)(2,1)} %param.19, bf16[18]{0:T(256)(128)(2,1)} %param.21, bf16[6]{0:T(256)(128)(2,1)} %param.23, bf16[24]{0:T(256)(128)(2,1)} %param.25, bf16[6]{0:T(256)(128)(2,1)} %param.27), dimensions={0} | concatenate | bytes 312 | tf_op jit(solution)/shard_map/concatenate | solution.py:438
  11.2 1.5 concatenate.33.cols_ref
  12.8 1.5 maximum_maximum_fusion.1.rows_ref
  16.6 105.1 %gather_all.1 = (bf16[1024,768]{1,0:T(8,128)(2,1)}, bf16[1024,768]{1,0:T(8,128)(2,1)}, bf16[32,24,1472]{2,1,0:T(8,128)(2,1)}, bf16[32,32,768]{2,1,0:T(8,128)(2,1)}) custom-call(bf16[256,768]{1,0:T(8,128)(2,1)} %x_ref.1, bf16[256,768]{1,0:T(8,128)(2,1)} %g_ref.1, bf16[4,6,1472]{2,1,0:T(8,128)(2,1)} %concatenate.33.cols_ref, ...), custom_call_target="tpu_custom_call" | custom-call | tf_op jit(solution)/shard_map/gather_all/pallas_call | solution.py:205
  121.7 1.7 convert_reduce_fusion
  123.4 2.0 fusion.17
  132.1 2.4 slice.138
  137.4 1.7 slice.139
  143.1 3.3 multiply_convert_fusion.1
  146.4 4.4 %convert_reduce_fusion.1 = (f32[768]{0:T(1024)}, bf16[1024,768]{1,0:T(8,128)(2,1)}) fusion(f32[1024,768]{1,0:T(8,128)S(1)} %get-tuple-element.78, f32[768]{0:T(1024)S(1)} %copy-done.43, bf16[1024,768]{1,0:T(8,128)(2,1)S(1)} %copy-done.8, bf16[768,768]{1,0:T(8,128)(2,1)S(1)} %bitcast.121), kind=kOutput, calls=%fused_computation.35 | convolution fusion | flops 1218182400 | bytes 7477248 | tf_op jit(solution)/shard_map/dot_general | solution.py:29
  152.5 4.4 %convolution_convert_fusion.1 = bf16[768,768]{0,1:T(8,128)(2,1)} fusion(bf16[1024,768]{1,0:T(8,128)(2,1)} %get-tuple-element.80, bf16[1024,768]{1,0:T(8,128)(2,1)S(1)} %copy-done.5, f32[768]{0:T(1024)} %add.132, f32[768]{0:T(1024)} %copy-done.38, f32[1024]{0:T(1024)} %add_rsqrt_fusion, f32[1024]{0:T(1024)S(1)} %broadcast_multiply_fusion), kind=kOutput, calls=%fused_computation.48 | convolution fusion | flops 1213267968 | bytes 4339712 | tf_op jit(solution)/shard_map/dot_general | solution.py:25
  156.9 3.1 fusion.70
  159.9 2.5 convolution_convert_fusion
  163.9 10.7 %fusion.69 = (f32[3,1024]{1,0:T(4,128)S(1)}, f32[3,1024,1024]{1,2,0:T(8,128)}) fusion(pred[1024,1024]{0,1:T(8,128)(4,1)} %iota_compare_fusion, bf16[1024,3,48]{0,2,1:T(8,128)(2,1)} %slice.236, bf16[1024,3,8]{0,2,1:T(8,128)(2,1)} %get-tuple-element.59, bf16[1024,3,8]{0,2,1:T(8,128)(2,1)} %get-tuple-element.60, bf16[1024,3,48]{0,2,1:T(8,128)(2,1)S(1)} %slice.237, ...), kind=kOutput, calls=%fused_computation.126 | convolution fusion | flops 417596416 | bytes 14430208 | tf_op jit(solution)/shard_map/sub | solution.py:497
  174.6 7.6 %fusion.30 = bf16[1024,1,3,64]{0,3,2,1:T(8,128)(2,1)} fusion(bf16[3,1024,64]{1,2,0:T(8,128)(2,1)} %bitcast.136, f32[3,1024,1024]{1,2,0:T(8,128)} %get-tuple-element.74, f32[3,1024]{1,0:T(4,128)S(1)} %get-tuple-element.73), kind=kOutput, calls=%fused_computation.51 | convolution fusion | flops 408944640 | bytes 13381632 | tf_op jit(solution)/shard_map/hqk,hqd->khd/dot_general | solution.py:509
  183.0 2.6 fusion.33
  185.6 1.8 add_convert_fusion.1
  188.7 2.5 maximum_maximum_fusion.rows_ref
  191.2 6.9 %multiply_reduce_fusion = (f32[3,1024]{1,0:T(4,128)S(1)}, f32[3,1024,1024]{1,2,0:T(8,128)S(1)}) fusion(f32[3,1024,1024]{1,2,0:T(8,128)} %get-tuple-element.74, f32[3,1024]{1,0:T(4,128)S(1)} %get-tuple-element.73, bf16[3,1024,64]{1,2,0:T(8,128)(2,1)} %bitcast.137, f32[1024,3,3,64]{0,3,2,1:T(8,128)} %bitcast.130), kind=kOutput, calls=%fused_computation.2 | convolution fusion | flops 412087296 | bytes 25976832 | tf_op jit(solution)/shard_map/hqd,hkd->hqk/dot_general | solution.py:504
  198.6 3.4 %multiply_convert_fusion = bf16[3,1024,1024]{1,2,0:T(8,128)(2,1)S(1)} fusion(f32[3,1024,1024]{1,2,0:T(8,128)S(1)} %get-tuple-element.76, f32[3,1024]{1,0:T(4,128)S(1)} %get-tuple-element.75, f32[3,1024,1024]{1,2,0:T(8,128)S(1)} %bitcast.114, f32[3,1024]{1,0:T(4,128)S(1)} %get-tuple-element.73), kind=kLoop, calls=%fused_computation.1 | loop fusion | flops 15728640 | bytes 31481856 | tf_op jit(solution)/shard_map/convert_element_type | solution.py:506
  202.1 3.0 fusion.37
  207.9 5.1 %fusion.66 = (f32[768]{0:T(1024)S(1)}, f32[768]{0:T(1024)S(1)}, bf16[1024,768]{1,0:T(8,128)(2,1)}, f32[768]{0:T(1024)S(1)}, f32[768]{0:T(1024)S(1)}) fusion(f32[1024]{0:T(1024)S(1)} %copy-done.42, f32[1024]{0:T(1024)S(1)} %copy-done.32, bf16[1024,768]{1,0:T(8,128)(2,1)S(1)} %copy-done.6, f32[1024,768]{1,0:T(8,128)} %fusion.70, f32[768]{0:T(1024)S(1)} %copy-done.39, ...), kind=kOutput, calls=%fused_computation.123 | convolution fusion | flops 916190208 | bytes 8382464 | tf_op jit(solution)/shard_map/dot_general | solution.py:29
  216.8 2.9 copy.39
  224.0 104.6 %reduce_all.1 = (f32[6,3072]{1,0:T(8,128)S(1)}, f32[6,2304]{1,0:T(8,128)S(1)}, f32[32,768]{1,0:T(8,128)S(1)}, f32[8,128]{1,0:T(8,128)S(1)}, f32[256,768]{1,0:T(8,128)S(1)}, /*index=5*/f32[256,768]{1,0:T(8,128)S(1)}) custom-call(bf16[32,24,1344]{2,1,0:T(8,128)(2,1)S(1)} %bitcast.110, bf16[32,32,768]{2,1,0:T(8,128)(2,1)S(1)} %copy-done.1, ...), custom_call_target="tpu_custom_call" | custom-call | tf_op jit(solution)/shard_map/reduce_all/pallas_call | solution.py:369
  (188 shorter events, 43.2 us)
Async XLA Ops:
  6.2 119.2 %copy-start.45 = (bf16[32]{0:T(256)(128)(2,1)}, bf16[32]{0:T(256)(128)(2,1)S(1)}, u32[]{:S(2)}) copy-start(bf16[32]{0:T(256)(128)(2,1)S(1)} %pad.42.clone) | copy-start | bytes 196
  123.4 29.1 %copy-start.31 = (f32[1024]{0:T(1024)}, f32[1024]{0:T(1024)S(1)}, u32[]{:S(2)}) copy-start(f32[1024]{0:T(1024)S(1)} %broadcast_multiply_fusion) | copy-start | bytes 12292
  125.4 9.3 %copy-start.8 = (bf16[1024,768]{1,0:T(8,128)(2,1)S(1)}, bf16[1024,768]{1,0:T(8,128)(2,1)}, u32[]{:S(2)}) copy-start(bf16[1024,768]{1,0:T(8,128)(2,1)} %get-tuple-element.26) | copy-start | bytes 4718596
  130.1 12.9 %copy-start.38 = (f32[768]{0:T(1024)}, f32[768]{0:T(1024)S(1)}, u32[]{:S(2)}) copy-start(f32[768]{0:T(1024)S(1)} %mul.375) | copy-start | bytes 9220
  130.2 8.9 %copy-start.34 = (f32[768]{0:T(1024)}, f32[768]{0:T(1024)S(1)}, u32[]{:S(2)}) copy-start(f32[768]{0:T(1024)S(1)} %mul.390) | copy-start | bytes 9220
  131.1 8.1 %copy-start.36 = (f32[768]{0:T(1024)}, f32[768]{0:T(1024)S(1)}, u32[]{:S(2)}) copy-start(f32[768]{0:T(1024)S(1)} %add.141) | copy-start | bytes 9220
  134.7 4.5 %copy-start.16 = (bf16[192,768]{1,0:T(8,128)(2,1)}, bf16[192,768]{1,0:T(8,128)(2,1)S(1)}, u32[]{:S(2)}) copy-start(bf16[192,768]{1,0:T(8,128)(2,1)S(1)} %reshape.257) | copy-start | bytes 884740
  134.7 4.5 %copy-start.5 = (bf16[1024,768]{1,0:T(8,128)(2,1)S(1)}, bf16[1024,768]{1,0:T(8,128)(2,1)}, u32[]{:S(2)}) copy-start(bf16[1024,768]{1,0:T(8,128)(2,1)} %get-tuple-element.24) | copy-start | bytes 4718596
  134.7 4.5 %copy-start.41 = (f32[1024]{0:T(1024)S(1)}, f32[1024]{0:T(1024)}, u32[]{:S(2)}) copy-start(f32[1024]{0:T(1024)} %add_rsqrt_fusion) | copy-start | bytes 12292
  134.7 4.5 %copy-start.44 = (f32[576]{0:T(1024)S(1)}, f32[576]{0:T(1024)}, u32[]{:S(2)}) copy-start(f32[576]{0:T(1024)} %add.145) | copy-start | bytes 6916
  139.1 3.9 %copy-start.12 = (bf16[32,24,768]{2,1,0:T(8,128)(2,1)}, bf16[32,24,768]{2,1,0:T(8,128)(2,1)S(1)}, u32[]{:S(2)}) copy-start(bf16[32,24,768]{2,1,0:T(8,128)(2,1)S(1)} %slice.139) | copy-start | bytes 3538948
  152.5 4.4 %copy-start.13 = (bf16[32,24,768]{2,1,0:T(8,128)(2,1)S(1)}, bf16[32,24,768]{2,1,0:T(8,128)(2,1)}, u32[]{:S(2)}) copy-start(bf16[32,24,768]{2,1,0:T(8,128)(2,1)} %copy-done.12) | copy-start | bytes 3538948
  152.5 4.4 %copy-start.48 = (bf16[1024,768]{1,0:T(8,128)(2,1)S(1)}, bf16[1024,768]{1,0:T(8,128)(2,1)}, u32[]{:S(2)}) copy-start(bf16[1024,768]{1,0:T(8,128)(2,1)} %get-tuple-element.80) | copy-start | bytes 4718596
  174.6 8.4 %copy-start.3 = (f32[3,1024,1024]{1,2,0:T(8,128)S(1)}, f32[3,1024,1024]{1,2,0:T(8,128)}, u32[]{:S(2)}) copy-start(f32[3,1024,1024]{1,2,0:T(8,128)} %get-tuple-element.74) | copy-start | bytes 37748740
  188.7 9.4 %slice-start = ((s8[12582912]{0:T(1024)(128)(4,1)}), s8[4194304]{0:T(1024)(128)(4,1)S(1)}, s32[]{:S(2)}) async-start(s8[12582912]{0:T(1024)(128)(4,1)} %bitcast.113), calls=%async_computation | async-start | bytes 8388608
  191.2 7.0 %slice-start.1 = ((s8[12582912]{0:T(1024)(128)(4,1)}), s8[4194304]{0:T(1024)(128)(4,1)S(1)}, s32[]{:S(2)}) async-start(s8[12582912]{0:T(1024)(128)(4,1)} %bitcast.113), calls=%async_computation.1 | async-start | bytes 8388608
  191.2 7.4 %slice-start.2 = ((s8[12582912]{0:T(1024)(128)(4,1)}), s8[4194304]{0:T(1024)(128)(4,1)S(1)}, s32[]{:S(2)}) async-start(s8[12582912]{0:T(1024)(128)(4,1)} %bitcast.113), calls=%async_computation.2 | async-start | bytes 8388608
  207.9 5.2 %copy-start.37 = (f32[768]{0:T(1024)S(1)}, f32[768]{0:T(1024)}, u32[]{:S(2)}) copy-start(f32[768]{0:T(1024)} %copy-done.36) | copy-start | bytes 9220
  223.9 106.4 %copy-start.4 = (bf16[256,768]{1,0:T(8,128)(2,1)S(1)}, bf16[256,768]{1,0:T(8,128)(2,1)}, u32[]{:S(2)}) copy-start(bf16[256,768]{1,0:T(8,128)(2,1)} %x_ref.1) | copy-start | bytes 1179652
  223.9 106.4 %copy-start.29 = (f32[256]{0:T(256)S(1)}, f32[256]{0:T(256)}, u32[]{:S(2)}) copy-start(f32[256]{0:T(256)} %copy-done.28) | copy-start | bytes 3076
  223.9 106.4 %copy-start.33 = (f32[256]{0:T(256)S(1)}, f32[256]{0:T(256)}, u32[]{:S(2)}) copy-start(f32[256]{0:T(256)} %add_rsqrt_fusion.1) | copy-start | bytes 3076
  223.9 106.8 %copy-start.7 = (bf16[256,768]{1,0:T(8,128)(2,1)S(1)}, bf16[256,768]{1,0:T(8,128)(2,1)}, u32[]{:S(2)}) copy-start(bf16[256,768]{1,0:T(8,128)(2,1)} %g_ref.1) | copy-start | bytes 1179652
  223.9 106.8 %copy-start.30 = (f32[768]{0:T(1024)S(1)}, f32[768]{0:T(1024)}, u32[]{:S(2)}) copy-start(f32[768]{0:T(1024)} %add.156) | copy-start | bytes 9220
  330.3 4.6 %copy-start.46 = (f32[6]{0:T(128)}, f32[6]{0:T(128)S(1)}, u32[]{:S(2)}) copy-start(f32[6]{0:T(128)S(1)} %get-tuple-element.134) | copy-start | bytes 76
  (28 other events, 59.1 us)

commit v3 on v1

--- a/solution.py
+++ b/solution.py
@@ -1,6 +1,8 @@
 import jax
 import jax.numpy as jnp
 from jax import lax
+from jax.experimental import pallas as pl
+from jax.experimental.pallas import tpu as pltpu
 from jax.sharding import PartitionSpec as P
 
 D = 768
@@ -49,14 +51,542 @@
     )
 
 
+MESH = pl.DeviceIdType.MESH
+SMALL = 128
+PAGE = 768
+NY, NZ, NX = 4, 4, 2
+GROUP = NZ * NX
+N_SP = 4
+PART = 6
+
+
+def place():
+    dp, sp = lax.axis_index("dp"), lax.axis_index("sp")
+    return dp, sp, dp // GROUP, lax.rem(dp // NX, NZ), lax.rem(dp, NX)
+
+
+def send(src, dst, send_sem, recv_sem, device):
+    return pltpu.make_async_remote_copy(
+        src_ref=src,
+        dst_ref=dst,
+        send_sem=send_sem,
+        recv_sem=recv_sem,
+        device_id=device,
+        device_id_type=MESH,
+    )
+
+
+def index_of(y, z, x):
+    return (y * NZ + z) * NX + x
+
+
+def slot_device(dp, sp):
+    line = dp * N_SP + sp
+    return lax.rem(line, NY * GROUP), line // (NY * GROUP)
+
+
+def owner_device(dp, sp):
+    line = sp * NY * GROUP + dp
+    return line // N_SP, lax.rem(line, N_SP)
+
+
+def differs(device, dp, sp):
+    return jnp.logical_or(device[0] != dp, device[1] != sp)
+
+
+class Plane:
+    def __init__(self, last):
+        self.last = last
+        dp, sp, y, z, x = place()
+        self.sp, self.y, self.z, self.x = sp, y, z, x
+        self.mine = (z if last == "y" else y) * NX + x
+        self.axis = y if last == "y" else z
+
+    def member(self, k):
+        e = lax.rem(self.mine + k, GROUP)
+        a, x = e // NX, lax.rem(e, NX)
+        y, z = (self.y, a) if self.last == "y" else (a, self.z)
+        return (index_of(y, z, x), self.sp), e, a, x
+
+    def along(self, k):
+        a = lax.rem(self.axis + k, NY)
+        y, z = (a, self.z) if self.last == "y" else (self.y, a)
+        return (index_of(y, z, self.x), self.sp), a
+
+    def block(self, ref, a):
+        return ref.at[a] if self.last == "y" else ref.at[:, a]
+
+    def chunk(self, ref, e):
+        a, x = e // NX, lax.rem(e, NX)
+        return ref.at[self.y, a, x] if self.last == "y" else ref.at[a, self.z, x]
+
+
+def greet(partner_in, partner_out):
+    dp, sp, y, z, x = place()
+    barrier = pltpu.get_barrier_semaphore()
+
+    def signal(device):
+        pl.semaphore_signal(barrier, inc=1, device_id=device, device_id_type=MESH)
+
+    for k in range(1, N_SP):
+        signal((dp, lax.rem(sp + k, N_SP)))
+    by_y, by_z = Plane("y"), Plane("z")
+    for k in range(1, GROUP):
+        signal(by_y.member(k)[0])
+        signal(by_z.member(k)[0])
+
+    @pl.when(differs(partner_in, dp, sp))
+    def _():
+        signal(partner_in)
+
+    count = N_SP - 1 + 2 * (GROUP - 1)
+    pl.semaphore_wait(barrier, count + jnp.where(differs(partner_out, dp, sp), 1, 0))
+
+
+def gather_kernel(
+    x_ref, g_ref, up_ref, qkv_ref, small_ref, down_ref, dense_ref,
+    x_out, g_out, up_out, qk_out, down_out, dense_out,
+    pieces, landed, tight_wide, up_tight, qk_tight,
+    t_send, t_recv, p_send, p_recv, r_send, r_recv, a_send, a_recv, b_send, b_recv,
+):
+    dp, sp, y, z, x = place()
+    to_slot, from_owner = slot_device(dp, sp), owner_device(dp, sp)
+    sibling = sp + 1 - 2 * lax.rem(sp, 2)
+    across = lax.rem(sp + 2, N_SP)
+    greet(from_owner, to_slot)
+    by_y, by_z = Plane("y"), Plane("z")
+
+    row_arrays = ((dense_ref, dense_out), (down_ref, down_out))
+    slot = to_slot[0]
+    slot_at = (slot // GROUP, lax.rem(slot // NX, NZ), lax.rem(slot, NX))
+    moves = differs(to_slot, dp, sp)
+
+    @pl.when(moves)
+    def _():
+        for i, (src, dst) in enumerate(row_arrays):
+            send(src, dst.at[slot_at], r_send.at[i], r_recv.at[i], to_slot).start()
+
+    @pl.when(jnp.logical_not(moves))
+    def _():
+        for i, (src, dst) in enumerate(row_arrays):
+            pltpu.make_async_copy(src, dst.at[y, z, x], r_recv.at[i]).start()
+
+    wide = qkv_ref[...].astype(F32)
+    third = wide.shape[1] // 3
+    width = third // N_SP
+    for t in range(N_SP):
+        pieces[t, :, :PAGE] = up_ref[:, t * PAGE : (t + 1) * PAGE].astype(F32)
+        for j in range(3):
+            at = j * third + t * width
+            pieces[t, :, PAGE + j * width : PAGE + (j + 1) * width] = wide[:, at : at + width]
+        pieces[t, :, PAGE + third * 3 // N_SP :] = jnp.zeros((PART, PAGE - third * 3 // N_SP), F32)
+        pieces[t, 0:1, PAGE + third * 3 // N_SP : PAGE + third * 3 // N_SP + SMALL] = small_ref[...]
+
+    def piece(k):
+        t = lax.rem(sp + k, N_SP)
+        return send(pieces.at[t], landed.at[sp], p_send.at[k], p_recv.at[sp], (dp, t))
+
+    for k in range(1, N_SP):
+        piece(k).start()
+    pltpu.make_async_copy(pieces.at[sp], landed.at[sp], p_recv.at[sp]).start()
+
+    tokens = x_ref.shape[0]
+    token_arrays = ((x_ref, x_out), (g_ref, g_out))
+
+    def rows_of(s):
+        return pl.ds(pl.multiple_of(s * tokens, tokens), tokens)
+
+    def token_copies(kind):
+        made = []
+        for i, (src, dst) in enumerate(token_arrays):
+            if kind == "pass":
+                there = dst.at[rows_of(across)]
+                made.append(send(there, there, t_send.at[i, 2], t_recv.at[i, across], (dp, sibling)))
+            else:
+                to, n = (across, 0) if kind == "across" else (sibling, 1)
+                made.append(
+                    send(src, dst.at[rows_of(sp)], t_send.at[i, n], t_recv.at[i, sp], (dp, to))
+                )
+        return made
+
+    def token_wait(s):
+        for i, (src, dst) in enumerate(token_arrays):
+            pltpu.make_async_copy(src, dst.at[rows_of(s)], t_recv.at[i, s]).wait()
+
+    for item in token_copies("across") + token_copies("sibling"):
+        item.start()
+    for i, (src, dst) in enumerate(token_arrays):
+        pltpu.make_async_copy(src, dst.at[rows_of(sp)], t_recv.at[i, sp]).start()
+
+    arrays = ((by_y, up_out), (by_z, qk_out), (by_y, dense_out), (by_z, down_out))
+
+    def stage_a(n, src):
+        plane, out = arrays[n]
+        mine = out.at[y, z, x]
+        return [
+            send(
+                mine if src is None else src, mine, a_send.at[n, k], a_recv.at[n, plane.mine],
+                plane.member(k)[0],
+            )
+            for k in range(1, GROUP)
+        ]
+
+    def stage_b(n):
+        plane, out = arrays[n]
+        there = plane.block(out, plane.axis)
+        return [
+            send(there, there, b_send.at[n, k], b_recv.at[n, plane.axis], plane.along(k)[0])
+            for k in range(1, NY)
+        ]
+
+    for s in range(N_SP):
+        pltpu.make_async_copy(pieces.at[s], landed.at[s], p_recv.at[s]).wait()
+    for s in range(N_SP):
+        tight_wide[s * PART : (s + 1) * PART, :] = landed[s]
+    up_tight[...] = tight_wide[:, :PAGE].astype(BF)
+    qk_tight[...] = tight_wide[:, PAGE:].astype(BF)
+    sources = (up_tight, qk_tight, None, None)
+    for n in (0, 1):
+        for item in stage_a(n, sources[n]):
+            item.start()
+        pltpu.make_async_copy(
+            sources[n], arrays[n][1].at[y, z, x], a_recv.at[n, arrays[n][0].mine]
+        ).start()
+    for i, (src, dst) in enumerate(row_arrays):
+        pltpu.make_async_copy(src, dst.at[y, z, x], r_recv.at[i]).wait()
+        for item in stage_a(2 + i, None):
+            item.start()
+    for n in range(4):
+        plane, out = arrays[n]
+        for k in range(0 if n < 2 else 1, GROUP):
+            e = lax.rem(plane.mine + k, GROUP)
+            there = plane.chunk(out, e)
+            pltpu.make_async_copy(there, there, a_recv.at[n, e]).wait()
+        for item in stage_b(n):
+            item.start()
+    token_wait(across)
+    for item in token_copies("pass"):
+        item.start()
+    for s in (sp, sibling, lax.rem(sibling + 2, N_SP)):
+        token_wait(s)
+    for n in range(4):
+        plane, out = arrays[n]
+        for k in range(1, NY):
+            a = plane.along(k)[1]
+            there = plane.block(out, a)
+            pltpu.make_async_copy(there, there, b_recv.at[n, a]).wait()
+
+    for kind in ("across", "sibling", "pass"):
+        for item in token_copies(kind):
+            item.wait_send()
+    for k in range(1, N_SP):
+        piece(k).wait_send()
+
+    @pl.when(moves)
+    def _():
+        for i, (src, dst) in enumerate(row_arrays):
+            send(src, dst.at[slot_at], r_send.at[i], r_recv.at[i], to_slot).wait_send()
+
+    for n in range(4):
+        for item in stage_a(n, sources[n]) + stage_b(n):
+            item.wait_send()
+
+
+def gather_all(x, g, up, qkv, small, down, dense):
+    tokens, d_model = x.shape
+    dma = pltpu.SemaphoreType.DMA
+    anywhere = pl.BlockSpec(memory_space=pl.ANY)
+    vmem = pl.BlockSpec(memory_space=pltpu.VMEM)
+    grid = (NY, NZ, NX)
+    own = PART * N_SP
+    return pl.pallas_call(
+        gather_kernel,
+        out_shape=(
+            jax.ShapeDtypeStruct((tokens * N_SP, d_model), BF),
+            jax.ShapeDtypeStruct((tokens * N_SP, d_model), BF),
+            jax.ShapeDtypeStruct(grid + (own, PAGE), BF),
+            jax.ShapeDtypeStruct(grid + (own, PAGE), BF),
+            jax.ShapeDtypeStruct(grid + down.shape, BF),
+            jax.ShapeDtypeStruct(grid + dense.shape, BF),
+        ),
+        in_specs=[anywhere, anywhere, vmem, vmem, vmem, anywhere, anywhere],
+        out_specs=(anywhere,) * 6,
+        scratch_shapes=[
+            pltpu.VMEM((N_SP, PART, 2 * PAGE), F32),
+            pltpu.VMEM((N_SP, PART, 2 * PAGE), F32),
+            pltpu.VMEM((own, 2 * PAGE), F32),
+            pltpu.VMEM((own, PAGE), BF),
+            pltpu.VMEM((own, PAGE), BF),
+            dma((2, 3)),
+            dma((2, N_SP)),
+            dma((N_SP,)),
+            dma((N_SP,)),
+            dma((2,)),
+            dma((2,)),
+            dma((4, GROUP)),
+            dma((4, GROUP)),
+            dma((4, NY)),
+            dma((4, NY)),
+        ],
+        compiler_params=pltpu.CompilerParams(collective_id=0, has_side_effects=True),
+        name="gather_all",
+    )(x, g, up, qkv, small, down, dense)
+
+
+def reduce_kernel(
+    up_ref, qk_ref, dense_ref, down_ref, small_ref, out_ref, dx_ref,
+    up_out, qkv_out, down_out, dense_out, small_out, hidden_out, dxhat_out,
+    up_1, qk_1, dense_1, down_1, small_1,
+    up_m, qk_m, dense_m, down_m, small_m,
+    up_2, qk_2, dense_2, down_2, small_2,
+    token_own, token_in, token_mid, token_far,
+    pieces, landed, small_land, down_sum, dense_sum,
+    b_send, b_recv, a_send, a_recv, t_own, t_send, t_recv, f_send, f_recv,
+    p_send, p_recv, s_send, s_recv, r_send, r_recv,
+):
+    dp, sp, y, z, x = place()
+    to_owner, from_slot = owner_device(dp, sp), slot_device(dp, sp)
+    sibling = sp + 1 - 2 * lax.rem(sp, 2)
+    across = lax.rem(sp + 2, N_SP)
+    greet(from_slot, to_owner)
+    by_y, by_z = Plane("y"), Plane("z")
+    arrays = (
+        (by_y, up_ref, up_1, up_m, up_2),
+        (by_z, qk_ref, qk_1, qk_m, qk_2),
+        (by_z, down_ref, down_1, down_m, down_2),
+        (by_y, dense_ref, dense_1, dense_m, dense_2),
+        (by_y, small_ref, small_1, small_m, small_2),
+    )
+
+    def stage_1(n):
+        plane, src, land = arrays[n][:3]
+        made = []
+        for k in range(1, NY):
+            device, a = plane.along(k)
+            made.append(
+                send(
+                    plane.block(src, a), land.at[plane.axis], b_send.at[n, k],
+                    b_recv.at[n, plane.axis], device,
+                )
+            )
+        return made
+
+    def stage_2(n):
+        plane, _, _, mid, land = arrays[n]
+        made = []
+        for k in range(1, GROUP):
+            device, e, a, xx = plane.member(k)
+            made.append(
+                send(
+                    mid.at[a, xx], land.at[plane.mine], a_send.at[n, k],
+                    a_recv.at[n, plane.mine], device,
+                )
+            )
+        return made
+
+    for n, (plane, src, land, mid, last) in enumerate(arrays):
+        for item in stage_1(n):
+            item.start()
+        pltpu.make_async_copy(
+            plane.block(src, plane.axis), land.at[plane.axis], b_recv.at[n, plane.axis]
+        ).start()
+
+    token_arrays = (out_ref, dx_ref)
+    sib_across = lax.rem(sibling + 2, N_SP)
+
+    def token_pair(i):
+        src = token_arrays[i]
+        return [
+            send(src.at[t], token_in.at[i, n], t_send.at[i, n], t_recv.at[i, n], (dp, sibling))
+            for n, t in enumerate((sibling, sib_across))
+        ]
+
+    def token_own_copy(i):
+        src = token_arrays[i]
+        return [
+            pltpu.make_async_copy(src.at[t], token_own.at[i, n], t_own.at[i, n])
+            for n, t in enumerate((sp, across))
+        ]
+
+    def token_far_copy(i):
+        return send(token_mid.at[i], token_far.at[i], f_send.at[i], f_recv.at[i], (dp, across))
+
+    for i in range(2):
+        for item in token_pair(i) + token_own_copy(i):
+            item.start()
+    for i in range(2):
+        for item in token_own_copy(i):
+            item.wait()
+        for item in token_pair(i):
+            item.wait_recv()
+        token_mid[i] = (token_own[i, 1].astype(F32) + token_in[i, 1].astype(F32)).astype(BF)
+        token_far_copy(i).start()
+
+    for n, (plane, src, land, mid, last) in enumerate(arrays):
+        for a in range(NY):
+            pltpu.make_async_copy(plane.block(src, a), land.at[a], b_recv.at[n, a]).wait()
+        for a in range(mid.shape[0]):
+            for xx in range(NX):
+                total = land[0, a, xx].astype(F32)
+                for s in range(1, NY):
+                    total = total + land[s, a, xx].astype(F32)
+                mid[a, xx] = total.astype(mid.dtype)
+        for item in stage_2(n):
+            item.start()
+        own = mid.at[plane.mine // NX, lax.rem(plane.mine, NX)]
+        pltpu.make_async_copy(own, last.at[plane.mine], a_recv.at[n, plane.mine]).start()
+
+    def finish(n):
+        plane, src, land, mid, last = arrays[n]
+        for e in range(GROUP):
+            pltpu.make_async_copy(mid.at[0, 0], last.at[e], a_recv.at[n, e]).wait()
+        total = last[0].astype(F32)
+        for e in range(1, GROUP):
+            total = total + last[e].astype(F32)
+        return total
+
+    total = finish(0)
+    for t in range(N_SP):
+        pieces[t, :, :PAGE] = total[t * PART : (t + 1) * PART, :]
+    total = finish(1)
+    for t in range(N_SP):
+        pieces[t, :, PAGE:] = total[t * PART : (t + 1) * PART, :]
+
+    def piece(k):
+        t = lax.rem(sp + k, N_SP)
+        return send(pieces.at[t], landed.at[sp], p_send.at[k], p_recv.at[sp], (dp, t))
+
+    for k in range(1, N_SP):
+        piece(k).start()
+    pltpu.make_async_copy(pieces.at[sp], landed.at[sp], p_recv.at[sp]).start()
+
+    down_sum[...] = finish(2)
+    dense_sum[...] = finish(3)
+    row_arrays = ((down_sum, down_out), (dense_sum, dense_out))
+    moves = differs(to_owner, dp, sp)
+
+    @pl.when(moves)
+    def _():
+        for i, (src, dst) in enumerate(row_arrays):
+            send(src, dst, r_send.at[i], r_recv.at[i], to_owner).start()
+
+    @pl.when(jnp.logical_not(moves))
+    def _():
+        for i, (src, dst) in enumerate(row_arrays):
+            pltpu.make_async_copy(src, dst, r_recv.at[i]).start()
+
+    small_land[sp] = finish(4)
+
+    def small_copy(k):
+        there = small_land.at[sp]
+        return send(
+            there, there, s_send.at[k], s_recv.at[sp], (dp, lax.rem(sp + k, N_SP))
+        )
+
+    for k in range(1, N_SP):
+        small_copy(k).start()
+
+    for i, result in enumerate((hidden_out, dxhat_out)):
+        token_far_copy(i).wait()
+        result[...] = (
+            token_own[i, 0].astype(F32) + token_in[i, 0].astype(F32) + token_far[i].astype(F32)
+        )
+
+    for s in range(N_SP):
+        pltpu.make_async_copy(pieces.at[s], landed.at[s], p_recv.at[s]).wait()
+    third = qkv_out.shape[1] // 3
+    width = third // N_SP
+    for s in range(N_SP):
+        up_out[:, s * PAGE : (s + 1) * PAGE] = landed[s, :, :PAGE]
+        block = landed[s, :, PAGE:]
+        for j in range(3):
+            to = j * third + s * width
+            qkv_out[:, to : to + width] = block[:, j * width : (j + 1) * width]
+    for k in range(1, N_SP):
+        s = lax.rem(sp + k, N_SP)
+        pltpu.make_async_copy(small_land.at[s], small_land.at[s], s_recv.at[s]).wait()
+    small_out[...] = jnp.sum(small_land[...], 0)
+    for i, (src, dst) in enumerate(row_arrays):
+        pltpu.make_async_copy(src, dst, r_recv.at[i]).wait()
+
+    @pl.when(moves)
+    def _():
+        for i, (src, dst) in enumerate(row_arrays):
+            send(src, dst, r_send.at[i], r_recv.at[i], to_owner).wait_send()
+
+    for k in range(1, N_SP):
+        piece(k).wait_send()
+        small_copy(k).wait_send()
+    for i in range(2):
+        for item in token_pair(i):
+            item.wait_send()
+    for n in range(len(arrays)):
+        for item in stage_1(n) + stage_2(n):
+            item.wait_send()
+
+
+def reduce_all(up, qk, dense, down, small, out, dx):
+    dma = pltpu.SemaphoreType.DMA
+    anywhere = pl.BlockSpec(memory_space=pl.ANY)
+    vmem = pl.BlockSpec(memory_space=pltpu.VMEM)
+    chunks = (up, qk, dense, down, small)
+    tokens = out.shape[1:]
+    first = [pltpu.VMEM((NY, NZ, NX) + item.shape[3:], item.dtype) for item in chunks]
+    mid = [pltpu.VMEM((NZ, NX) + item.shape[3:], item.dtype) for item in chunks]
+    last = [pltpu.VMEM((GROUP,) + item.shape[3:], item.dtype) for item in chunks]
+    return pl.pallas_call(
+        reduce_kernel,
+        out_shape=(
+            jax.ShapeDtypeStruct((PART, N_SP * PAGE), F32),
+            jax.ShapeDtypeStruct((PART, 3 * D), F32),
+            jax.ShapeDtypeStruct(down.shape[3:], F32),
+            jax.ShapeDtypeStruct(dense.shape[3:], F32),
+            jax.ShapeDtypeStruct(small.shape[3:], F32),
+            jax.ShapeDtypeStruct(tokens, F32),
+            jax.ShapeDtypeStruct(tokens, F32),
+        ),
+        in_specs=[anywhere] * 7,
+        out_specs=(vmem,) * 7,
+        scratch_shapes=first
+        + mid
+        + last
+        + [
+            pltpu.VMEM((2, 2) + tokens, BF),
+            pltpu.VMEM((2, 2) + tokens, BF),
+            pltpu.VMEM((2,) + tokens, BF),
+            pltpu.VMEM((2,) + tokens, BF),
+            pltpu.VMEM((N_SP, PART, 2 * PAGE), F32),
+            pltpu.VMEM((N_SP, PART, 2 * PAGE), F32),
+            pltpu.VMEM((N_SP,) + small.shape[3:], F32),
+            pltpu.VMEM(down.shape[3:], F32),
+            pltpu.VMEM(dense.shape[3:], F32),
+        ]
+        + [
+            dma((5, NY)),
+            dma((5, NY)),
+            dma((5, GROUP)),
+            dma((5, GROUP)),
+            dma((2, 2)),
+            dma((2, 2)),
+            dma((2, 2)),
+            dma((2,)),
+            dma((2,)),
+            dma((N_SP,)),
+            dma((N_SP,)),
+            dma((N_SP,)),
+            dma((N_SP,)),
+            dma((2,)),
+            dma((2,)),
+        ],
+        compiler_params=pltpu.CompilerParams(
+            collective_id=1, has_side_effects=True, vmem_limit_bytes=40 * 1024 * 1024
+        ),
+        name="reduce_all",
+    )(up, qk, dense, down, small, out, dx)
+
+
 def make_local(n_dp, n_sp):
     n_all = n_dp * n_sp
-    to_slice = []
-    for dp in range(n_dp):
-        for sp in range(n_sp):
-            to_slice.append((sp * n_dp + dp, dp * n_sp + sp))
-    to_owner = [(b, a) for a, b in to_slice]
-
     def local(
         hidden_in,
         cotangent,
@@ -90,9 +620,29 @@
             down_bias,
         )
         sizes = [item.shape[0] for item in small]
-        total = sum(sizes)
-        packed = jnp.pad(jnp.concatenate(small), (0, 128 - total)).reshape(1, 128)
-        packed = lax.all_gather(packed, BOTH, axis=0, tiled=True).astype(F32)
+        part = up_weight.shape[0]
+        part = up_weight.shape[0]
+        packed = jnp.zeros((SMALL,), F32)
+        at = 0
+        for item in small:
+            size = item.shape[0]
+            packed = packed + jnp.pad(item.astype(F32), (at, SMALL - at - size))
+            at += size
+        x_seq, g_seq, up_t, qk, down_t, dense_t = gather_all(
+            hidden_in,
+            cotangent,
+            up_weight,
+            qkv_weight,
+            packed.reshape(1, SMALL),
+            down_weight,
+            dense_weight,
+        )
+        up_t = up_t.reshape(d_model, ff_here)
+        down_t = down_t.reshape(ff_here, d_model)
+        dense_t = dense_t.reshape(width, d_model)
+        qk = qk.reshape(d_model, PAGE)
+        qkv_t = qk[:, : 3 * width]
+        packed = qk[::part, 3 * width : 3 * width + SMALL].astype(F32)
         vectors = []
         at = 0
         for size in sizes:
@@ -101,26 +651,7 @@
         gain_1, shift_1, gain_2, shift_2, qkv_add, dense_add, up_add, down_add = vectors
         qkv_add = lax.dynamic_slice_in_dim(qkv_add.reshape(3, n_sp, width), sp, 1, 1).reshape(-1)
         up_add = lax.dynamic_slice_in_dim(up_add, sp * ff_here, ff_here, 0)
-
-        up_part = lax.all_to_all(
-            up_weight.reshape(-1, n_sp, ff_here), "sp", split_axis=1, concat_axis=0, tiled=True
-        ).reshape(-1, ff_here)
-        down_part = lax.ppermute(down_weight, BOTH, to_slice)
-        qkv_part = lax.all_to_all(
-            qkv_weight.reshape(-1, 3, n_sp, width).transpose(0, 2, 1, 3).reshape(-1, n_sp, 3 * width),
-            "sp",
-            split_axis=1,
-            concat_axis=0,
-            tiled=True,
-        ).reshape(-1, 3 * width)
-        dense_part = lax.ppermute(dense_weight, BOTH, to_slice)
-        up_t = lax.all_gather(up_part, "dp", axis=0, tiled=True)
-        down_t = lax.all_gather(down_part, "dp", axis=0, tiled=True)
-        qkv_t = lax.all_gather(qkv_part, "dp", axis=0, tiled=True)
-        dense_t = lax.all_gather(dense_part, "dp", axis=0, tiled=True)
-
-        x_seq = lax.all_gather(hidden_in, "sp", axis=0, tiled=True).astype(F32)
-        g_seq = lax.all_gather(cotangent, "sp", axis=0, tiled=True)
+        x_seq = x_seq.astype(F32)
         length = x_seq.shape[0]
         xhat, rstd = norm_components(x_seq)
         normed_1 = (xhat * gain_1 + shift_1).astype(BF)
@@ -171,14 +702,46 @@
         qkv_bias_grad = jnp.sum(dqkv.astype(F32), 0)
         dnormed_1 = contract_cols(dqkv, qkv_t)
 
-        out_sum = lax.psum_scatter(out_part, "sp", scatter_dimension=0, tiled=True)
+        g_here = cotangent.astype(F32)
+        zeros_qkv = jnp.zeros((3, n_sp, width), F32)
+        qkv_bias_full = lax.dynamic_update_slice(
+            zeros_qkv, qkv_bias_grad.reshape(3, 1, width), (0, sp, 0)
+        ).reshape(-1)
+        up_bias_full = lax.dynamic_update_slice(
+            jnp.zeros((FF,), F32), up_bias_grad, (sp * ff_here,)
+        )
+        full = (
+            jnp.sum(dnormed_1 * xhat, 0),
+            jnp.sum(dnormed_1, 0),
+            jnp.sum(dnormed_2 * xhat, 0),
+            jnp.sum(dnormed_2, 0),
+            qkv_bias_full,
+            jnp.sum(g_here, 0),
+            up_bias_full,
+        )
+        packed = jnp.concatenate([item.reshape(n_all, -1) for item in full], 1)
+        packed = jnp.pad(packed, ((0, 0), (0, SMALL - packed.shape[1])))
+        packed = jnp.pad(packed.reshape(n_dp, n_sp, SMALL), ((0, 0), (0, -n_sp % 8), (0, 0)))
+
+        here = hidden_in.shape[0]
+        grid = (NY, NZ, NX)
+        own = part * n_sp
+        up_own, qkv_own, down_own, dense_own, packed, out_sum, dxhat = reduce_all(
+            up_grad.astype(BF).reshape(grid + (own, ff_here)),
+            jnp.pad(qkv_grad.astype(BF), ((0, 0), (0, PAGE - 3 * width))).reshape(
+                grid + (own, PAGE)
+            ),
+            dense_grad.astype(BF).reshape(grid + (part, d_model)),
+            down_grad.astype(BF).reshape(grid + (own, d_model)),
+            packed.reshape(grid + packed.shape[1:]),
+            out_part.astype(BF).reshape(n_sp, here, d_model),
+            (dnormed_1 * gain_1 + dnormed_2 * gain_2).astype(BF).reshape(n_sp, here, d_model),
+        )
+        mine = lax.dynamic_slice_in_dim(packed, sp, 1, 0).reshape(-1)
+
         x_here = hidden_in.astype(F32)
         hidden_out = (x_here + out_sum + (dense_add + down_add)).astype(BF)
-        dxhat = lax.psum_scatter(
-            dnormed_1 * gain_1 + dnormed_2 * gain_2, "sp", scatter_dimension=0, tiled=True
-        )
         xhat_here, rstd_here = norm_components(x_here)
-        g_here = cotangent.astype(F32)
         hidden_grad = (
             g_here
             + rstd_here
@@ -188,46 +751,6 @@
                 - xhat_here * jnp.mean(dxhat * xhat_here, -1, keepdims=True)
             )
         ).astype(BF)
-
-        up_own = lax.psum_scatter(up_grad, "dp", scatter_dimension=0, tiled=True)
-        down_own = lax.psum_scatter(down_grad, "dp", scatter_dimension=0, tiled=True)
-        qkv_own = lax.psum_scatter(qkv_grad, "dp", scatter_dimension=0, tiled=True)
-        dense_own = lax.psum_scatter(
-            jnp.pad(dense_grad.reshape(n_dp, -1, d_model), ((0, 0), (0, 2), (0, 0))),
-            "dp",
-            scatter_dimension=0,
-            tiled=True,
-        )[0, : dense_weight.shape[0]]
-        rows = up_weight.shape[0]
-        up_own = lax.all_to_all(
-            up_own.reshape(n_sp, rows, ff_here), "sp", split_axis=0, concat_axis=0, tiled=True
-        ).transpose(1, 0, 2).reshape(rows, FF)
-        qkv_own = lax.all_to_all(
-            qkv_own.reshape(n_sp, rows, 3 * width), "sp", split_axis=0, concat_axis=0, tiled=True
-        ).reshape(n_sp, rows, 3, width).transpose(1, 2, 0, 3).reshape(rows, 3 * d_model)
-        down_own = lax.ppermute(down_own, BOTH, to_owner)
-        dense_own = lax.ppermute(dense_own, BOTH, to_owner)
-
-        zeros_qkv = jnp.zeros((3, n_sp, width), F32)
-        qkv_bias_full = lax.dynamic_update_slice(
-            zeros_qkv, qkv_bias_grad.reshape(3, 1, width), (0, sp, 0)
-        ).reshape(-1)
-        up_bias_full = lax.dynamic_update_slice(
-            jnp.zeros((FF,), F32), up_bias_grad, (sp * ff_here,)
-        )
-        g_sum = jnp.sum(g_here, 0)
-        full = (
-            jnp.sum(dnormed_1 * xhat, 0),
-            jnp.sum(dnormed_1, 0),
-            jnp.sum(dnormed_2 * xhat, 0),
-            jnp.sum(dnormed_2, 0),
-            qkv_bias_full,
-            g_sum,
-            up_bias_full,
-        )
-        packed = jnp.concatenate([item.reshape(n_all, -1) for item in full], 1)
-        packed = jnp.pad(packed, ((0, 0), (0, 128 - packed.shape[1])))
-        mine = lax.psum_scatter(packed, BOTH, scatter_dimension=0, tiled=True).reshape(-1)
         parts = []
         at = 0
         for item in full:

time: 1470 us -> 237 us (0.16)
  waiting for transfers between devices: 1110 us -> 0 us
  blocking collectives: 203 us -> 0 us
  Pallas kernels: 0 us -> 115 us
  starting transfers between devices: 33.3 us -> 0 us
    reduce_scatter x5 -> x0, waiting for transfers between devices: 735 us -> none  [the longest x1 226 us: local(): lax.psum_scatter(down_grad, 'dp', scatter_dimension=0, tiled=True)]
    unnamed x13 -> x0, waiting for transfers between devices: 328 us -> none
    all_gather x3 -> x0, blocking collectives: 196 us -> none  [the longest x1 82.3 us: local(): qkv_t = lax.all_gather(qkv_part, 'dp', axis=0, tiled=True)]
    pallas_call x0 -> x2, Pallas kernels: none -> 115 us  [the longest x1 64.2 us: gather_all(): pl.pallas_call(gather_kernel, out_shape=(jax.ShapeDtypeStruct((tokens * N...]
    all_gather x4 -> x0, waiting for transfers between devices: 41.8 us -> none  [the longest x1 41.7 us: local(): down_t = lax.all_gather(down_part, 'dp', axis=0, tiled=True)]
    ppermute x4 -> x0, starting transfers between devices: 20 us -> none  [the longest x1 5.74 us: local(): down_part = lax.ppermute(down_weight, BOTH, to_slice)]
  transfers between devices with their start and end apart: 18 -> 0, of which waited for: 9 -> 0; matrix products, arithmetic and copies ran while one was open for 6% -> 0% of each run, Pallas kernels for 0% -> 0%
where the time goes in v3:
time: 237 us; the launch traced here: 235 us
  Pallas kernels  115 us (49%)
  matrix products  62.1 us (26%)
  local copies, waits for them, and re-layouts  34.7 us (15%)
  other arithmetic  21.7 us (9%)
    pallas_call x1, Pallas kernels, gather_all(): pl.pallas_call(gather_kernel, out_shape=(jax.ShapeDtypeStruct((tokens * N...  64.2 us
    pallas_call x1, Pallas kernels, reduce_all(): pl.pallas_call(reduce_kernel, out_shape=(jax.ShapeDtypeStruct((PART, N_SP...  51 us
    dot_general x4, matrix products, contract_cols(): lax.dot_general(left, right, (((1,), (1,)), ((), ())), preferred_element_...  14.3 us
    unnamed x118, local copies, waits for them, and re-layouts  11.7 us
    dot_general x4, matrix products, contract_rows(): lax.dot_general(left, right, (((0,), (0,)), ((), ())), preferred_element_...  10.4 us
    dot_general x4, matrix products, dot(): return jnp.dot(left, right, preferred_element_type=F32)  9.66 us
    dot_general x1, matrix products, local(): dv = jnp.einsum('hqk,hqd->khd', probs_low, do, preferred_element_type=F32)  7.61 us
    sub x1, matrix products, local(): probs = jnp.exp(scores - top)  7.51 us

profile of v3, /device:TPU:1, one launch (start us, length us, event | category | flops | bytes accessed | tf_op | source)
XLA Modules:
  0.0 235.1 jit_solution(165305112303204834)
XLA Ops:
  9.4 64.2 %gather_all.1 = (bf16[1024,768]{1,0:T(8,128)(2,1)}, bf16[1024,768]{1,0:T(8,128)(2,1)}, bf16[4,4,2,24,768]{4,3,2,1,0:T(8,128)(2,1)}, bf16[4,4,2,24,768]{4,3,2,1,0...) custom-call(bf16[256,768]{1,0:T(8,128)(2,1)} %x_ref.1, bf16[256,768]{1,0:T(8,128)(2,1)} %g_ref.1, ...), custom_call_target="tpu_custom_call" | custom-call | tf_op jit(solution)/shard_map/gather_all/pallas_call | solution.py:302
  73.6 1.8 convert_reduce_fusion
  75.5 2.1 fusion.17
  85.1 2.6 %convolution_add_fusion = f32[1024,576]{0,1:T(8,128)S(1)} fusion(f32[576]{0:T(1024)S(1)} %add.187, bf16[768,768]{1,0:T(8,128)(2,1)} %bitcast.117, bf16[1024,768]{1,0:T(8,128)(2,1)S(1)} %copy-done.5, f32[768]{0:T(1024)S(1)} %add.183, f32[768]{0:T(1024)S(1)} %mul.390, f32[1024]{0:T(1024)S(1)} %add_rsqrt_fusion, f32[1024]{0:T(1024)S(1)} %broadcast_multiply_fusion), kind=kOutput, calls=%fused_computation.44 | convolution fusion | flops 911278080 | bytes 4931840 | tf_op jit(solution)/shard_map/dot_general | solution.py:19
  90.2 3.3 %multiply_convert_fusion.1 = (bf16[1024,768]{1,0:T(8,128)(2,1)}, f32[1024,768]{1,0:T(8,128)S(1)}) fusion(f32[768]{0:T(1024)S(1)} %copy-done.48, bf16[768,768]{1,0:T(8,128)(2,1)S(1)} %bitcast.121, bf16[1024,768]{1,0:T(8,128)(2,1)S(1)} %copy-done.5, f32[768]{0:T(1024)S(1)} %copy-done.42, f32[768]{0:T(1024)S(1)} %copy-done.40, f32[1024]{0:T(1024)S(1)} %copy-done.45, ...), kind=kOutput, calls=%fused_computation.36 | convolution fusion | flops 1217396736 | bytes 7488512 | tf_op jit(solution)/shard_map/dot_general | solution.py:19
  93.5 3.8 %convert_reduce_fusion.1 = (f32[768]{0:T(1024)S(1)}, bf16[1024,768]{1,0:T(8,128)(2,1)}) fusion(f32[1024,768]{1,0:T(8,128)S(1)} %get-tuple-element.84, f32[768]{0:T(1024)S(1)} %copy-done.48, bf16[1024,768]{1,0:T(8,128)(2,1)S(1)} %copy-done.9, bf16[768,768]{1,0:T(8,128)(2,1)S(1)} %bitcast.119), kind=kOutput, calls=%fused_computation.35 | convolution fusion | flops 1218182400 | bytes 7477248 | tf_op jit(solution)/shard_map/dot_general | solution.py:27
  98.4 4.4 %convolution_convert_fusion.1 = bf16[768,768]{1,0:T(8,128)(2,1)} fusion(bf16[1024,768]{1,0:T(8,128)(2,1)} %get-tuple-element.86, bf16[1024,768]{1,0:T(8,128)(2,1)S(1)} %copy-done.5, f32[768]{0:T(1024)S(1)} %copy-done.43, f32[768]{0:T(1024)S(1)} %copy-done.41, f32[1024]{0:T(1024)S(1)} %copy-done.46, f32[1024]{0:T(1024)S(1)} %copy-done.33), kind=kOutput, calls=%fused_computation.46 | convolution fusion | flops 1213267968 | bytes 4339712 | tf_op jit(solution)/shard_map/dot_general | solution.py:23
  102.8 3.1 %fusion.73 = f32[1024,768]{1,0:T(8,128)} fusion(bf16[1024,768]{1,0:T(8,128)(2,1)S(1)} %copy-done.55, bf16[768,768]{1,0:T(8,128)(2,1)S(1)} %bitcast.122), kind=kOutput, calls=%fused_computation.127 | convolution fusion | flops 1207959552 | bytes 5898240 | tf_op jit(solution)/shard_map/dot_general | solution.py:27
  105.9 2.6 %convolution_convert_fusion = bf16[768,768]{1,0:T(8,128)(2,1)} fusion(bf16[1024,768]{1,0:T(8,128)(2,1)S(1)} %copy-done.54, bf16[1024,768]{1,0:T(8,128)(2,1)S(1)} %copy-done.9), kind=kOutput, calls=%fused_computation.45 | convolution fusion | flops 1208549376 | bytes 4325376 | tf_op jit(solution)/shard_map/dot_general | solution.py:23
  108.4 3.1 %fusion.74 = f32[1024,768]{1,0:T(8,128)} fusion(bf16[1024,768]{1,0:T(8,128)(2,1)S(1)} %copy-done.54, bf16[768,768]{1,0:T(8,128)(2,1)S(1)} %bitcast.120), kind=kOutput, calls=%fused_computation.128 | convolution fusion | flops 1207959552 | bytes 5898240 | tf_op jit(solution)/shard_map/dot_general | solution.py:19
  111.5 7.5 %fusion.72 = (f32[3,1024]{1,0:T(4,128)S(1)}, f32[3,1024,1024]{1,2,0:T(8,128)}) fusion(pred[1024,1024]{0,1:T(8,128)(4,1)S(1)} %copy-done.16, bf16[1024,3,48]{0,2,1:T(8,128)(2,1)S(1)} %copy-done.10, bf16[1024,3,8]{0,2,1:T(8,128)(2,1)S(1)} %copy-done.20, bf16[1024,3,8]{0,2,1:T(8,128)(2,1)S(1)} %copy-done.22, bf16[1024,3,48]{0,2,1:T(8,128)(2,1)S(1)} %slice.222, ...), kind=kOutput, calls=%fused_computation.126 | convolution fusion | flops 417596416 | bytes 14430208 | tf_op jit(solution)/shard_map/sub | solution.py:683
  119.0 7.6 %fusion.30 = bf16[1024,1,3,64]{0,3,2,1:T(8,128)(2,1)} fusion(bf16[3,1024,64]{1,2,0:T(8,128)(2,1)} %bitcast.123, f32[3,1024,1024]{1,2,0:T(8,128)} %get-tuple-element.80, f32[3,1024]{1,0:T(4,128)S(1)} %get-tuple-element.79), kind=kOutput, calls=%fused_computation.49 | convolution fusion | flops 408944640 | bytes 13381632 | tf_op jit(solution)/shard_map/hqk,hqd->khd/dot_general | solution.py:695
  127.5 2.5 %fusion.33 = bf16[3,1024,64]{1,2,0:T(8,128)(2,1)S(1)} fusion(f32[1024,3,3,64]{0,3,2,1:T(8,128)} %bitcast.113, f32[3,1024,1024]{1,2,0:T(8,128)S(1)} %copy-done.3, f32[3,1024]{1,0:T(4,128)S(1)} %get-tuple-element.79), kind=kOutput, calls=%fused_computation.50 | convolution fusion | flops 409141248 | bytes 13381632 | tf_op jit(solution)/shard_map/hqk,hkd->hqd/dot_general | solution.py:686
  132.9 6.8 %multiply_reduce_fusion = (f32[3,1024]{1,0:T(4,128)S(1)}, f32[3,1024,1024]{1,2,0:T(8,128)S(1)}) fusion(f32[3,1024,1024]{1,2,0:T(8,128)} %get-tuple-element.80, f32[3,1024]{1,0:T(4,128)} %copy-done.26, bf16[3,1024,64]{1,2,0:T(8,128)(2,1)} %bitcast.124, f32[1024,3,3,64]{0,3,2,1:T(8,128)} %bitcast.114), kind=kOutput, calls=%fused_computation.2 | convolution fusion | flops 412087296 | bytes 25980928 | tf_op jit(solution)/shard_map/hqd,hkd->hqk/dot_general | solution.py:690
  139.8 6.6 %multiply_convert_fusion = bf16[3,1024,1024]{1,2,0:T(8,128)(2,1)S(1)} fusion(f32[3,1024,1024]{1,2,0:T(8,128)S(1)} %get-tuple-element.82, f32[3,1024]{1,0:T(4,128)S(1)} %get-tuple-element.81, f32[3,1024,1024]{1,2,0:T(8,128)} %get-tuple-element.80, f32[3,1024]{1,0:T(4,128)S(1)} %copy-done.27), kind=kLoop, calls=%fused_computation.1 | loop fusion | flops 15728640 | bytes 31481856 | tf_op jit(solution)/shard_map/convert_element_type | solution.py:692
  146.5 2.0 fusion.37
  152.4 6.0 %fusion.69 = (f32[768]{0:T(1024)}, f32[768]{0:T(1024)}, bf16[1024,768]{1,0:T(8,128)(2,1)S(1)}, f32[768]{0:T(1024)}, f32[768]{0:T(1024)}) fusion(f32[1024]{0:T(1024)} %copy-done.44, f32[1024]{0:T(1024)S(1)} %copy-done.34, bf16[1024,768]{1,0:T(8,128)(2,1)} %get-tuple-element.27, f32[1024,768]{1,0:T(8,128)} %fusion.73, f32[768]{0:T(1024)} %mul.375, ...), kind=kOutput, calls=%fused_computation.123 | convolution fusion | flops 916190208 | bytes 8482816 | tf_op jit(solution)/shard_map/dot_general | solution.py:27
  158.4 2.3 convolution_convert_fusion.2
  161.5 1.4 reshape.249
  163.0 1.4 reshape.248
  164.4 1.4 reshape.250
  167.3 1.8 concatenate.21
  170.6 2.3 copy.42
  177.7 51.0 %reduce_all.1 = (f32[6,3072]{1,0:T(8,128)S(1)}, f32[6,2304]{1,0:T(8,128)S(1)}, f32[24,768]{1,0:T(8,128)S(1)}, f32[6,768]{1,0:T(8,128)S(1)}, f32[8,128]{1,0:T(8,1...) custom-call(bf16[4,4,2,24,768]{4,3,2,1,0:T(8,128)(2,1)S(1)} %bitcast.105, ...), custom_call_target="tpu_custom_call" | custom-call | tf_op jit(solution)/shard_map/reduce_all/pallas_call | solution.py:537
  (179 shorter events, 41.8 us)
Async XLA Ops:
  73.6 10.1 %copy-start.9 = (bf16[1024,768]{1,0:T(8,128)(2,1)S(1)}, bf16[1024,768]{1,0:T(8,128)(2,1)}, u32[]{:S(2)}) copy-start(bf16[1024,768]{1,0:T(8,128)(2,1)} %get-tuple-element.29) | copy-start | bytes 4718596
  75.4 9.7 %copy-start.5 = (bf16[1024,768]{1,0:T(8,128)(2,1)S(1)}, bf16[1024,768]{1,0:T(8,128)(2,1)}, u32[]{:S(2)}) copy-start(bf16[1024,768]{1,0:T(8,128)(2,1)} %get-tuple-element.27) | copy-start | bytes 4718596
  75.4 12.3 %copy-start.31 = (f32[1024]{0:T(1024)}, f32[1024]{0:T(1024)S(1)}, u32[]{:S(2)}) copy-start(f32[1024]{0:T(1024)S(1)} %broadcast_multiply_fusion) | copy-start | bytes 12292
  77.6 10.2 %copy-start.44 = (f32[1024]{0:T(1024)}, f32[1024]{0:T(1024)S(1)}, u32[]{:S(2)}) copy-start(f32[1024]{0:T(1024)S(1)} %add_rsqrt_fusion) | copy-start | bytes 12292
  87.8 5.7 %copy-start.15 = (f32[1024,576]{0,1:T(8,128)}, f32[1024,576]{0,1:T(8,128)S(1)}, u32[]{:S(2)}) copy-start(f32[1024,576]{0,1:T(8,128)S(1)} %convolution_add_fusion) | copy-start | bytes 7077892
  93.5 4.8 %copy-start.33 = (f32[1024]{0:T(1024)S(1)}, f32[1024]{0:T(1024)}, u32[]{:S(2)}) copy-start(f32[1024]{0:T(1024)} %copy-done.31) | copy-start | bytes 12292
  93.5 4.8 %copy-start.41 = (f32[768]{0:T(1024)S(1)}, f32[768]{0:T(1024)}, u32[]{:S(2)}) copy-start(f32[768]{0:T(1024)} %mul.375) | copy-start | bytes 9220
  93.5 4.8 %copy-start.43 = (f32[768]{0:T(1024)S(1)}, f32[768]{0:T(1024)}, u32[]{:S(2)}) copy-start(f32[768]{0:T(1024)} %add.174) | copy-start | bytes 9220
  119.0 7.6 %copy-start.26 = (f32[3,1024]{1,0:T(4,128)}, f32[3,1024]{1,0:T(4,128)S(1)}, u32[]{:S(2)}) copy-start(f32[3,1024]{1,0:T(4,128)S(1)} %get-tuple-element.79) | copy-start | bytes 36868
  119.0 8.4 %copy-start.3 = (f32[3,1024,1024]{1,2,0:T(8,128)S(1)}, f32[3,1024,1024]{1,2,0:T(8,128)}, u32[]{:S(2)}) copy-start(f32[3,1024,1024]{1,2,0:T(8,128)} %get-tuple-element.80) | copy-start | bytes 37748740
  132.9 6.8 %copy-start.27 = (f32[3,1024]{1,0:T(4,128)S(1)}, f32[3,1024]{1,0:T(4,128)}, u32[]{:S(2)}) copy-start(f32[3,1024]{1,0:T(4,128)} %copy-done.26) | copy-start | bytes 36868
  139.8 6.7 %copy-start.11 = (bf16[1024,3,48]{0,2,1:T(8,128)(2,1)S(1)}, bf16[1024,3,48]{0,2,1:T(8,128)(2,1)}, u32[]{:S(2)}) copy-start(bf16[1024,3,48]{0,2,1:T(8,128)(2,1)} %slice.221) | copy-start | bytes 884740
  139.8 6.7 %copy-start.21 = (bf16[1024,3,8]{0,2,1:T(8,128)(2,1)S(1)}, bf16[1024,3,8]{0,2,1:T(8,128)(2,1)}, u32[]{:S(2)}) copy-start(bf16[1024,3,8]{0,2,1:T(8,128)(2,1)} %get-tuple-element.65) | copy-start | bytes 147460
  139.8 6.7 %copy-start.23 = (bf16[1024,3,8]{0,2,1:T(8,128)(2,1)S(1)}, bf16[1024,3,8]{0,2,1:T(8,128)(2,1)}, u32[]{:S(2)}) copy-start(bf16[1024,3,8]{0,2,1:T(8,128)(2,1)} %get-tuple-element.66) | copy-start | bytes 147460
  152.4 6.1 %copy-start.6 = (bf16[1024,768]{1,0:T(8,128)(2,1)S(1)}, bf16[1024,768]{1,0:T(8,128)(2,1)}, u32[]{:S(2)}) copy-start(bf16[1024,768]{1,0:T(8,128)(2,1)} %get-tuple-element.27) | copy-start | bytes 4718596
  152.4 6.1 %copy-start.12 = (bf16[1024,3,3,64]{0,3,2,1:T(8,128)(2,1)S(1)}, bf16[1024,3,3,64]{0,3,2,1:T(8,128)(2,1)}, u32[]{:S(2)}) copy-start(bf16[1024,3,3,64]{0,3,2,1:T(8,128)(2,1)} %get-tuple-element.47) | copy-start | bytes 3538948
  152.4 6.0 %copy-start.37 = (f32[768]{0:T(1024)S(1)}, f32[768]{0:T(1024)}, u32[]{:S(2)}) copy-start(f32[768]{0:T(1024)} %copy-done.36) | copy-start | bytes 9220
  152.4 6.0 %copy-start.39 = (f32[768]{0:T(1024)S(1)}, f32[768]{0:T(1024)}, u32[]{:S(2)}) copy-start(f32[768]{0:T(1024)} %copy-done.38) | copy-start | bytes 9220
  152.4 6.0 %copy-start.47 = (f32[1024]{0:T(1024)S(1)}, f32[1024]{0:T(1024)}, u32[]{:S(2)}) copy-start(f32[1024]{0:T(1024)} %copy-done.44) | copy-start | bytes 12292
  177.7 52.9 %copy-start.4 = (bf16[256,768]{1,0:T(8,128)(2,1)S(1)}, bf16[256,768]{1,0:T(8,128)(2,1)}, u32[]{:S(2)}) copy-start(bf16[256,768]{1,0:T(8,128)(2,1)} %x_ref.1) | copy-start | bytes 1179652
  177.7 52.9 %copy-start.29 = (f32[256]{0:T(256)S(1)}, f32[256]{0:T(256)}, u32[]{:S(2)}) copy-start(f32[256]{0:T(256)} %copy-done.28) | copy-start | bytes 3076
  177.7 52.9 %copy-start.35 = (f32[256]{0:T(256)S(1)}, f32[256]{0:T(256)}, u32[]{:S(2)}) copy-start(f32[256]{0:T(256)} %add_rsqrt_fusion.1) | copy-start | bytes 3076
  177.7 53.2 %copy-start.7 = (bf16[256,768]{1,0:T(8,128)(2,1)S(1)}, bf16[256,768]{1,0:T(8,128)(2,1)}, u32[]{:S(2)}) copy-start(bf16[256,768]{1,0:T(8,128)(2,1)} %g_ref.1) | copy-start | bytes 1179652
  177.7 53.2 %copy-start.30 = (f32[768]{0:T(1024)S(1)}, f32[768]{0:T(1024)}, u32[]{:S(2)}) copy-start(f32[768]{0:T(1024)} %add.198) | copy-start | bytes 9220
  (32 other events, 84.5 us)

commit v4 on v3

--- a/solution.py
+++ b/solution.py
@@ -1,5 +1,6 @@
 import jax
 import jax.numpy as jnp
+import numpy as np
 from jax import lax
 from jax.experimental import pallas as pl
 from jax.experimental.pallas import tpu as pltpu
@@ -19,36 +20,12 @@
     return jnp.dot(left, right, preferred_element_type=F32)
 
 
-def contract_rows(left, right):
-    return lax.dot_general(left, right, (((0,), (0,)), ((), ())), preferred_element_type=F32)
-
-
-def contract_cols(left, right):
-    return lax.dot_general(left, right, (((1,), (1,)), ((), ())), preferred_element_type=F32)
-
-
 def norm_components(values_in):
     center = jnp.mean(values_in, -1, keepdims=True)
     centered = values_in - center
     spread = jnp.mean(centered * centered, -1, keepdims=True)
     inverse_deviation = lax.rsqrt(spread + 1e-05)
     return (centered * inverse_deviation, inverse_deviation)
-
-
-def rotary_tables(length):
-    half = ROT // 2
-    frequency = 10000.0 ** (-2.0 * jnp.arange(half, dtype=F32) / ROT)
-    angles = jnp.arange(length, dtype=F32)[:, None] * frequency[None, :]
-    return (jnp.cos(angles)[:, None, :], jnp.sin(angles)[:, None, :])
-
-
-def rotate(vector, cosine, sine):
-    half = ROT // 2
-    lead = vector[..., :half]
-    after = vector[..., half:ROT]
-    return jnp.concatenate(
-        [lead * cosine - after * sine, after * cosine + lead * sine, vector[..., ROT:]], -1
-    )
 
 
 MESH = pl.DeviceIdType.MESH
@@ -585,207 +562,390 @@
     )(up, qk, dense, down, small, out, dx)
 
 
-def make_local(n_dp, n_sp):
-    n_all = n_dp * n_sp
-    def local(
-        hidden_in,
-        cotangent,
+BLOCK = 256
+
+
+def dot_nt(left, right):
+    return lax.dot_general(left, right, (((1,), (1,)), ((), ())), preferred_element_type=F32)
+
+
+def dot_tn(left, right):
+    return lax.dot_general(left, right, (((0,), (0,)), ((), ())), preferred_element_type=F32)
+
+
+def iota(shape, axis):
+    return lax.broadcasted_iota(jnp.int32, shape, axis)
+
+
+def rotary_tables(length):
+    half = ROT // 2
+    frequency = np.float32(10000.0) ** (np.float32(-2.0) * np.arange(half, dtype=np.float32) / ROT)
+    angles = np.arange(length, dtype=np.float32)[:, None] * frequency[None, :].astype(np.float32)
+    cosine = np.ones((length, HEAD_DIM), np.float32)
+    sine = np.zeros((length, HEAD_DIM), np.float32)
+    cosine[:, :half] = cosine[:, half:ROT] = np.cos(angles)
+    sine[:, :half] = -np.sin(angles)
+    sine[:, half:ROT] = np.sin(angles)
+    return jnp.asarray(np.tile(cosine, (1, 2))), jnp.asarray(np.tile(sine, (1, 2)))
+
+
+def swap_halves(u):
+    low = lax.rem(iota(u.shape, 1), 16) < 8
+    return jnp.where(low, pltpu.roll(u, 120, 1), pltpu.roll(u, 8, 1))
+
+
+def column_of(c, sp, kind):
+    if kind == "qkv":
+        width = D // N_SP
+        return (c // width) * D + sp * width + lax.rem(c, width)
+    return c + sp * (FF // N_SP) if kind == "up" else c
+
+
+VECTORS_IN = (
+    (0, 6, "", D), (6, 6, "", D), (12, 6, "", D), (18, 6, "", D),
+    (24, 18, "qkv", PAGE), (42, 6, "", D), (48, 24, "up", PAGE), (72, 6, "", D),
+)
+VECTORS_OUT = (
+    (0, 6, "", D), (6, 6, "", D), (12, 6, "", D), (18, 6, "", D),
+    (24, 18, "qkv", PAGE), (42, 6, "", D), (48, 24, "up", PAGE),
+)
+
+
+def compute_kernel(
+    x_ref, g_ref, up_ref, qk_ref, down_ref, dense_ref, cos_ref, sin_ref,
+    up_out, qk_out, dense_out, down_out, small_out, out_out, dx_out, bias_out,
+    xhat_s, n1_s, n2_s, act_s, dpre_s, dx_s, sum_s, e_s, dqkv_s,
+    q_s, k_s, v_s, do_s, kt_s, vt_s, dk_s, dv_s, ctxt_s, dense_wide, dense_s, vec_s,
+):
+    sp = lax.axis_index("sp")
+    length = x_ref.shape[0]
+    heads = HEADS // N_SP
+    width = heads * HEAD_DIM
+    n_own = NY * NZ * NX * N_SP
+    steps = length // BLOCK
+
+    pick = (iota((n_own, D), 1) == PART * iota((n_own, D), 0)).astype(BF)
+    packed = dot(pick, qk_ref[:, 3 * width : 3 * width + SMALL]).astype(BF)
+    for n, (start, each, kind, size) in enumerate(VECTORS_IN):
+        lane = column_of(iota((SMALL, size), 1), sp, kind)
+        spread = (iota((SMALL, size), 0) == start + lax.rem(lane, each)).astype(BF)
+        lane = column_of(iota((n_own, size), 1), sp, kind)
+        values = jnp.where(lane // each == iota((n_own, size), 0), dot(packed, spread), 0.0)
+        vec_s[n : n + 1, :] = jnp.sum(values, 0, keepdims=True)
+    gain_1, shift_1, gain_2, shift_2 = (vec_s[n : n + 1, :] for n in range(4))
+    lanes = iota((1, PAGE), 1)
+    qkv_add = jnp.where(lanes < 3 * width, vec_s[4:5, :], 0.0)
+    up_add = vec_s[6:7, :]
+    bias_out[...] = vec_s[5:6, :] + vec_s[7:8, :]
+    for e in range(dense_ref.shape[0]):
+        dense_wide[e * PART : (e + 1) * PART, :] = dense_ref[e].astype(F32)
+    dense_s[...] = dense_wide[...].astype(BF)
+
+    def fold(values):
+        return jnp.sum(values.reshape(-1, 8, values.shape[-1]), 0)
+
+    def rows_at(i):
+        return pl.ds(pl.multiple_of(i * BLOCK, BLOCK), BLOCK)
+
+    zeros = jnp.zeros((8, D), F32)
+
+    def first(i, sums):
+        rows = rows_at(i)
+        x = x_ref[rows, :].astype(F32)
+        centered = x - jnp.mean(x, -1, keepdims=True)
+        xhat = centered * lax.rsqrt(jnp.mean(centered * centered, -1, keepdims=True) + 1e-05)
+        xhat_s[rows, :] = xhat
+        n1_s[rows, :] = (xhat * gain_1 + shift_1).astype(BF)
+        n2 = (xhat * gain_2 + shift_2).astype(BF)
+        n2_s[rows, :] = n2
+        g = g_ref[rows, :]
+        pre = dot(n2, up_ref[...]) + up_add
+        cdf = 0.5 * (1.0 + lax.erf(pre * 0.7071067811865476))
+        act = (pre * cdf).astype(BF)
+        act_s[rows, :] = act
+        pdf = jnp.exp(-0.5 * pre * pre) * 0.3989422804014327
+        dpre = (dot_nt(g, down_ref[...]) * (cdf + pre * pdf)).astype(BF)
+        dpre_s[rows, :] = dpre
+        sum_s[rows, :] = dot(act, down_ref[...])
+        dn2 = dot_nt(dpre, up_ref[...])
+        dx_s[rows, :] = dn2 * gain_2
+        bias, gain, shift = sums
+        return (bias + fold(dpre.astype(F32)), gain + fold(dn2 * xhat), shift + fold(dn2))
+
+    up_bias, gain_2_grad, shift_2_grad = lax.fori_loop(0, steps, first, (zeros,) * 3)
+
+    @pl.loop(0, steps)
+    def _(i):
+        rows = rows_at(i)
+        y = dot(n1_s[rows, :], qk_ref[...]) + qkv_add
+        cosine, sine = cos_ref[rows, :], sin_ref[rows, :]
+        turned = []
+        for p in range(2 * width // 128):
+            u = y[:, p * 128 : (p + 1) * 128]
+            turned.append(u * cosine + swap_halves(u) * sine)
+        d = dot_nt(g_ref[rows, :], dense_s[...])
+
+        def head(n):
+            u = turned[n // 2]
+            return u[:, (n % 2) * HEAD_DIM : (n % 2 + 1) * HEAD_DIM]
+
+        for h in range(heads):
+            at = 2 * width + h * HEAD_DIM
+            q_s[h, rows, :] = head(h).astype(BF)
+            k_s[h, rows, :] = head(heads + h).astype(BF)
+            v_s[h, rows, :] = y[:, at : at + HEAD_DIM].astype(BF)
+            do_s[h, rows, :] = d[:, h * HEAD_DIM : (h + 1) * HEAD_DIM].astype(BF)
+
+    scale = HEAD_DIM ** (-0.5)
+
+    @pl.loop(0, heads)
+    def _(h):
+        kt_s[...] = k_s[h].astype(F32).T.astype(BF)
+        vt_s[...] = v_s[h].astype(F32).T.astype(BF)
+        for i in reversed(range(steps)):
+            keys = (i + 1) * BLOCK
+            rows = slice(i * BLOCK, (i + 1) * BLOCK)
+            q, do = q_s[h, rows, :], do_s[h, rows, :]
+            scores = dot_nt(k_s[h, :keys, :], q) * scale
+            hidden = iota((BLOCK, BLOCK), 0) > iota((BLOCK, BLOCK), 1)
+            corner = jnp.where(hidden, -1e30, scores[i * BLOCK :, :])
+            if i:
+                scores = jnp.concatenate([scores[: i * BLOCK, :], corner], 0)
+            else:
+                scores = corner
+            expo = jnp.exp(scores - jnp.max(scores, 0, keepdims=True))
+            probs = expo * (1.0 / jnp.sum(expo, 0, keepdims=True))
+            low = probs.astype(BF)
+            ctxt_s[h, :, rows] = dot(vt_s[:, :keys], low).astype(BF)
+            dprobs = dot_nt(v_s[h, :keys, :], do)
+            delta = jnp.sum(probs * dprobs, 0, keepdims=True)
+            dscores = (probs * (dprobs - delta) * scale).astype(BF)
+            dq = dot(kt_s[:, :keys], dscores)
+            e_s[h, rows, :] = dq.T
+            dk = dot(dscores, q)
+            dv = dot(low, do)
+            if i == steps - 1:
+                dk_s[h] = dk
+                dv_s[h] = dv
+            else:
+                dk_s[h, :keys, :] += dk
+                dv_s[h, :keys, :] += dv
+
+    ctxt = ctxt_s[...].reshape(width, length)
+
+    def last(i, sums):
+        rows = rows_at(i)
+        cosine, sine = cos_ref[rows, :], sin_ref[rows, :]
+        parts = [ref[h, rows, :] for ref in (e_s, dk_s, dv_s) for h in range(heads)]
+        for p in range(2 * width // 128):
+            u = jnp.concatenate(parts[2 * p : 2 * p + 2], 1).astype(BF).astype(F32)
+            dqkv_s[rows, p * 128 : (p + 1) * 128] = (u * cosine - swap_halves(u) * sine).astype(BF)
+        rest = jnp.concatenate(
+            parts[2 * heads :] + [jnp.zeros((BLOCK, PAGE - 3 * width), F32)], 1
+        )
+        dqkv_s[rows, 2 * width :] = rest.astype(BF)
+        dqkv = dqkv_s[rows, :]
+        dn1 = dot_nt(dqkv, qk_ref[...])
+        dx_out[rows, :] = (dx_s[rows, :] + dn1 * gain_1).astype(BF)
+        bias, gain, shift = sums
+        return (
+            bias + fold(dqkv.astype(F32)),
+            gain + fold(dn1 * xhat_s[rows, :]),
+            shift + fold(dn1),
+        )
+
+    qkv_bias, gain_1_grad, shift_1_grad = lax.fori_loop(0, steps, last, (zeros,) * 3)
+    for i in range(steps):
+        rows = slice(i * BLOCK, (i + 1) * BLOCK)
+        out_out[rows, :] = (sum_s[rows, :] + dot_tn(ctxt[:, rows], dense_s[...])).astype(BF)
+
+    @pl.loop(0, D // BLOCK)
+    def _(i):
+        cols = rows_at(i)
+        up_out[:, cols] = dot_tn(n2_s[...], dpre_s[:, cols]).astype(BF)
+        down_out[:, cols] = dot_tn(act_s[...], g_ref[:, cols]).astype(BF)
+        qk_out[:, cols] = dot_tn(n1_s[...], dqkv_s[:, cols]).astype(BF)
+
+    dense_grad = dot(ctxt, g_ref[...])
+    for e in range(dense_out.shape[0]):
+        dense_out[e] = dense_grad[e * PART : (e + 1) * PART, :].astype(BF)
+
+    here = length // N_SP
+    g_here = g_ref[pl.ds(pl.multiple_of(sp * here, here), here), :].astype(F32)
+    n_rows = 2 * n_own
+    values = (
+        gain_1_grad, shift_1_grad, gain_2_grad, shift_2_grad, qkv_bias, fold(g_here), up_bias
+    )
+    result = jnp.zeros((n_rows, SMALL), F32)
+    for (start, each, kind, size), item in zip(VECTORS_OUT, values):
+        vector = jnp.sum(item, 0, keepdims=True)
+        lane = column_of(iota((n_rows, size), 1), sp, kind)
+        row = iota((n_rows, size), 0)
+        mine = jnp.logical_and(lane // each == row // 8 * N_SP + lax.rem(row, 8), lax.rem(row, 8) < N_SP)
+        if kind == "qkv":
+            mine = jnp.logical_and(mine, iota((n_rows, size), 1) < 3 * width)
+        rest = jnp.where(mine, vector, 0.0)
+        lane = column_of(iota((size, SMALL), 0), sp, kind)
+        gather = (iota((size, SMALL), 1) == start + lax.rem(lane, each)).astype(BF)
+        for _ in range(3):
+            piece = rest.astype(BF)
+            result = result + dot(piece, gather)
+            rest = rest - piece.astype(F32)
+    small_out[...] = result
+
+
+def compute_all(x, g, up, qk, down, dense):
+    length = x.shape[0]
+    heads = HEADS // N_SP
+    width = heads * HEAD_DIM
+    n_dp = NY * NZ * NX
+    cosine, sine = rotary_tables(length)
+    vmem = pl.BlockSpec(memory_space=pltpu.VMEM)
+
+    def array(shape, kind):
+        return pltpu.VMEM(shape, kind)
+
+    return pl.pallas_call(
+        compute_kernel,
+        out_shape=(
+            jax.ShapeDtypeStruct((D, PAGE), BF),
+            jax.ShapeDtypeStruct((D, PAGE), BF),
+            jax.ShapeDtypeStruct((n_dp, PART, D), BF),
+            jax.ShapeDtypeStruct((PAGE, D), BF),
+            jax.ShapeDtypeStruct((n_dp * 8, SMALL), F32),
+            jax.ShapeDtypeStruct((length, D), BF),
+            jax.ShapeDtypeStruct((length, D), BF),
+            jax.ShapeDtypeStruct((1, D), F32),
+        ),
+        in_specs=[vmem] * 8,
+        out_specs=(vmem,) * 8,
+        scratch_shapes=[
+            array((length, D), F32),
+            array((length, D), BF),
+            array((length, D), BF),
+            array((length, PAGE), BF),
+            array((length, PAGE), BF),
+            array((length, D), F32),
+            array((length, D), F32),
+            array((heads, length, HEAD_DIM), F32),
+            array((length, PAGE), BF),
+            array((heads, length, HEAD_DIM), BF),
+            array((heads, length, HEAD_DIM), BF),
+            array((heads, length, HEAD_DIM), BF),
+            array((heads, length, HEAD_DIM), BF),
+            array((HEAD_DIM, length), BF),
+            array((HEAD_DIM, length), BF),
+            array((heads, length, HEAD_DIM), F32),
+            array((heads, length, HEAD_DIM), F32),
+            array((heads, HEAD_DIM, length), BF),
+            array((width, D), F32),
+            array((width, D), BF),
+            array((8, PAGE), F32),
+        ],
+        compiler_params=pltpu.CompilerParams(vmem_limit_bytes=58 * 1024 * 1024),
+        cost_estimate=pl.CostEstimate(
+            flops=14_000_000_000, bytes_accessed=16_000_000, transcendentals=6_000_000
+        ),
+        name="compute_all",
+    )(x, g, up, qk, down, dense, cosine, sine)
+
+
+def local(
+    hidden_in,
+    cotangent,
+    attn_gain,
+    attn_shift,
+    mlp_gain,
+    mlp_shift,
+    qkv_weight,
+    qkv_bias,
+    dense_weight,
+    dense_bias,
+    up_weight,
+    up_bias,
+    down_weight,
+    down_bias,
+):
+    sp = lax.axis_index("sp")
+    small = (
         attn_gain,
         attn_shift,
         mlp_gain,
         mlp_shift,
+        qkv_bias,
+        dense_bias,
+        up_bias,
+        down_bias,
+    )
+    packed = jnp.zeros((SMALL,), F32)
+    at = 0
+    for item in small:
+        size = item.shape[0]
+        packed = packed + jnp.pad(item.astype(F32), (at, SMALL - at - size))
+        at += size
+    x_seq, g_seq, up_t, qk, down_t, dense_t = gather_all(
+        hidden_in,
+        cotangent,
+        up_weight,
         qkv_weight,
-        qkv_bias,
+        packed.reshape(1, SMALL),
+        down_weight,
         dense_weight,
-        dense_bias,
-        up_weight,
-        up_bias,
-        down_weight,
-        down_bias,
-    ):
-        sp = lax.axis_index("sp")
-        d_model = hidden_in.shape[1]
-        heads_here = HEADS // n_sp
-        width = heads_here * HEAD_DIM
-        ff_here = FF // n_sp
-
-        small = (
-            attn_gain,
-            attn_shift,
-            mlp_gain,
-            mlp_shift,
-            qkv_bias,
-            dense_bias,
-            up_bias,
-            down_bias,
+    )
+    n_dp = NY * NZ * NX
+    up_grad, qk_grad, dense_grad, down_grad, packed, out_part, dxhat, bias = compute_all(
+        x_seq,
+        g_seq,
+        up_t.reshape(D, PAGE),
+        qk.reshape(D, PAGE),
+        down_t.reshape(PAGE, D),
+        dense_t.reshape(n_dp, PART, D),
+    )
+    here = hidden_in.shape[0]
+    grid = (NY, NZ, NX)
+    up_own, qkv_own, down_own, dense_own, packed, out_sum, dxhat = reduce_all(
+        up_grad.reshape(grid + (PART * N_SP, PAGE)),
+        qk_grad.reshape(grid + (PART * N_SP, PAGE)),
+        dense_grad.reshape(grid + (PART, D)),
+        down_grad.reshape(grid + (PART * N_SP, D)),
+        packed.reshape(grid + (8, SMALL)),
+        out_part.reshape(N_SP, here, D),
+        dxhat.reshape(N_SP, here, D),
+    )
+    mine = lax.dynamic_slice_in_dim(packed, sp, 1, 0).reshape(-1)
+    x_here = hidden_in.astype(F32)
+    hidden_out = (x_here + out_sum + bias).astype(BF)
+    xhat, rstd = norm_components(x_here)
+    hidden_grad = (
+        cotangent.astype(F32)
+        + rstd
+        * (
+            dxhat
+            - jnp.mean(dxhat, -1, keepdims=True)
+            - xhat * jnp.mean(dxhat * xhat, -1, keepdims=True)
         )
-        sizes = [item.shape[0] for item in small]
-        part = up_weight.shape[0]
-        part = up_weight.shape[0]
-        packed = jnp.zeros((SMALL,), F32)
-        at = 0
-        for item in small:
-            size = item.shape[0]
-            packed = packed + jnp.pad(item.astype(F32), (at, SMALL - at - size))
-            at += size
-        x_seq, g_seq, up_t, qk, down_t, dense_t = gather_all(
-            hidden_in,
-            cotangent,
-            up_weight,
-            qkv_weight,
-            packed.reshape(1, SMALL),
-            down_weight,
-            dense_weight,
-        )
-        up_t = up_t.reshape(d_model, ff_here)
-        down_t = down_t.reshape(ff_here, d_model)
-        dense_t = dense_t.reshape(width, d_model)
-        qk = qk.reshape(d_model, PAGE)
-        qkv_t = qk[:, : 3 * width]
-        packed = qk[::part, 3 * width : 3 * width + SMALL].astype(F32)
-        vectors = []
-        at = 0
-        for size in sizes:
-            vectors.append(packed[:, at : at + size].reshape(-1))
-            at += size
-        gain_1, shift_1, gain_2, shift_2, qkv_add, dense_add, up_add, down_add = vectors
-        qkv_add = lax.dynamic_slice_in_dim(qkv_add.reshape(3, n_sp, width), sp, 1, 1).reshape(-1)
-        up_add = lax.dynamic_slice_in_dim(up_add, sp * ff_here, ff_here, 0)
-        x_seq = x_seq.astype(F32)
-        length = x_seq.shape[0]
-        xhat, rstd = norm_components(x_seq)
-        normed_1 = (xhat * gain_1 + shift_1).astype(BF)
-        normed_2 = (xhat * gain_2 + shift_2).astype(BF)
-
-        pre = dot(normed_2, up_t) + up_add
-        cdf = 0.5 * (1.0 + lax.erf(pre * 0.7071067811865476))
-        act = (pre * cdf).astype(BF)
-        out_part = dot(act, down_t)
-        pdf = jnp.exp(-0.5 * pre * pre) * 0.3989422804014327
-        dpre = (contract_cols(g_seq, down_t) * (cdf + pre * pdf)).astype(BF)
-        down_grad = contract_rows(act, g_seq)
-        up_grad = contract_rows(normed_2, dpre)
-        up_bias_grad = jnp.sum(dpre.astype(F32), 0)
-        dnormed_2 = contract_cols(dpre, up_t)
-
-        qkv = (dot(normed_1, qkv_t) + qkv_add).reshape(length, 3, heads_here, HEAD_DIM)
-        cosine, sine = rotary_tables(length)
-        q = rotate(qkv[:, 0], cosine, sine).astype(BF).transpose(1, 0, 2)
-        k = rotate(qkv[:, 1], cosine, sine).astype(BF).transpose(1, 0, 2)
-        v = qkv[:, 2].astype(BF).transpose(1, 0, 2)
-        dctx = contract_cols(g_seq, dense_t).astype(BF)
-        do = dctx.reshape(length, heads_here, HEAD_DIM).transpose(1, 0, 2)
-        scale = HEAD_DIM ** (-0.5)
-        scores = jnp.einsum("hqd,hkd->hqk", q, k, preferred_element_type=F32) * scale
-        where = jnp.arange(length)[:, None] >= jnp.arange(length)[None, :]
-        scores = jnp.where(where[None], scores, -1e30)
-        top = jnp.max(scores, -1, keepdims=True)
-        probs = jnp.exp(scores - top)
-        probs = probs / jnp.sum(probs, -1, keepdims=True)
-        probs_low = probs.astype(BF)
-        ctx = jnp.einsum("hqk,hkd->hqd", probs_low, v, preferred_element_type=F32)
-        ctx = ctx.astype(BF).transpose(1, 0, 2).reshape(length, width)
-        out_part = out_part + dot(ctx, dense_t)
-        dense_grad = contract_rows(ctx, g_seq)
-        dprobs = jnp.einsum("hqd,hkd->hqk", do, v, preferred_element_type=F32)
-        delta = jnp.sum(probs * dprobs, -1, keepdims=True)
-        dscores = (scale * probs * (dprobs - delta)).astype(BF)
-        dq = jnp.einsum("hqk,hkd->qhd", dscores, k, preferred_element_type=F32)
-        dk = jnp.einsum("hqk,hqd->khd", dscores, q, preferred_element_type=F32)
-        dv = jnp.einsum("hqk,hqd->khd", probs_low, do, preferred_element_type=F32)
-        dq = dq.astype(BF).astype(F32)
-        dk = dk.astype(BF).astype(F32)
-        dqkv = jnp.stack(
-            [rotate(dq, cosine, -sine), rotate(dk, cosine, -sine), dv], 1
-        ).astype(BF).reshape(length, 3 * width)
-        qkv_grad = contract_rows(normed_1, dqkv)
-        qkv_bias_grad = jnp.sum(dqkv.astype(F32), 0)
-        dnormed_1 = contract_cols(dqkv, qkv_t)
-
-        g_here = cotangent.astype(F32)
-        zeros_qkv = jnp.zeros((3, n_sp, width), F32)
-        qkv_bias_full = lax.dynamic_update_slice(
-            zeros_qkv, qkv_bias_grad.reshape(3, 1, width), (0, sp, 0)
-        ).reshape(-1)
-        up_bias_full = lax.dynamic_update_slice(
-            jnp.zeros((FF,), F32), up_bias_grad, (sp * ff_here,)
-        )
-        full = (
-            jnp.sum(dnormed_1 * xhat, 0),
-            jnp.sum(dnormed_1, 0),
-            jnp.sum(dnormed_2 * xhat, 0),
-            jnp.sum(dnormed_2, 0),
-            qkv_bias_full,
-            jnp.sum(g_here, 0),
-            up_bias_full,
-        )
-        packed = jnp.concatenate([item.reshape(n_all, -1) for item in full], 1)
-        packed = jnp.pad(packed, ((0, 0), (0, SMALL - packed.shape[1])))
-        packed = jnp.pad(packed.reshape(n_dp, n_sp, SMALL), ((0, 0), (0, -n_sp % 8), (0, 0)))
-
-        here = hidden_in.shape[0]
-        grid = (NY, NZ, NX)
-        own = part * n_sp
-        up_own, qkv_own, down_own, dense_own, packed, out_sum, dxhat = reduce_all(
-            up_grad.astype(BF).reshape(grid + (own, ff_here)),
-            jnp.pad(qkv_grad.astype(BF), ((0, 0), (0, PAGE - 3 * width))).reshape(
-                grid + (own, PAGE)
-            ),
-            dense_grad.astype(BF).reshape(grid + (part, d_model)),
-            down_grad.astype(BF).reshape(grid + (own, d_model)),
-            packed.reshape(grid + packed.shape[1:]),
-            out_part.astype(BF).reshape(n_sp, here, d_model),
-            (dnormed_1 * gain_1 + dnormed_2 * gain_2).astype(BF).reshape(n_sp, here, d_model),
-        )
-        mine = lax.dynamic_slice_in_dim(packed, sp, 1, 0).reshape(-1)
-
-        x_here = hidden_in.astype(F32)
-        hidden_out = (x_here + out_sum + (dense_add + down_add)).astype(BF)
-        xhat_here, rstd_here = norm_components(x_here)
-        hidden_grad = (
-            g_here
-            + rstd_here
-            * (
-                dxhat
-                - jnp.mean(dxhat, -1, keepdims=True)
-                - xhat_here * jnp.mean(dxhat * xhat_here, -1, keepdims=True)
-            )
-        ).astype(BF)
-        parts = []
-        at = 0
-        for item in full:
-            size = item.size // n_all
-            parts.append(mine[at : at + size])
-            at += size
-        return (
-            hidden_out,
-            hidden_grad,
-            parts[0],
-            parts[1],
-            parts[2],
-            parts[3],
-            qkv_own,
-            parts[4],
-            dense_own,
-            parts[5],
-            up_own,
-            parts[6],
-            down_own,
-            parts[5],
-        )
-
-    return local
+    ).astype(BF)
+    parts = [mine[start : start + each] for start, each, _, _ in VECTORS_OUT]
+    return (
+        hidden_out,
+        hidden_grad,
+        parts[0],
+        parts[1],
+        parts[2],
+        parts[3],
+        qkv_own,
+        parts[4],
+        dense_own,
+        parts[5],
+        up_own,
+        parts[6],
+        down_own,
+        parts[5],
+    )
 
 
 def solution(mesh):
     matrix = P(BOTH, None)
     vector = P(BOTH)
-    ins = (matrix, matrix) + (vector,) * 4 + (matrix, vector) * 4
-    outs = (matrix, matrix) + (vector,) * 4 + (matrix, vector) * 4
-    return jax.shard_map(
-        make_local(mesh.shape["dp"], mesh.shape["sp"]),
-        mesh=mesh,
-        in_specs=ins,
-        out_specs=outs,
-        check_vma=False,
-    )
+    split = (matrix, matrix) + (vector,) * 4 + (matrix, vector) * 4
+    return jax.shard_map(local, mesh=mesh, in_specs=split, out_specs=split, check_vma=False)

time: 237 us -> 176 us (0.74)
  matrix products: 62.1 us -> 0 us
  Pallas kernels: 115 us -> 157 us
  local copies, waits for them, and re-layouts: 34.7 us -> 13.5 us
  other arithmetic: 21.7 us -> 3.3 us
    dot_general x17 -> x0, matrix products: 54.6 us -> none  [the longest x4 14.3 us: contract_cols(): lax.dot_general(left, right, (((1,), (1,)), ((), ())), preferred_element_...]
    pallas_call x0 -> x1, Pallas kernels: none -> 42.2 us  [compute_all(): pl.pallas_call(compute_kernel, out_shape=(jax.ShapeDtypeStruct((D, PAGE),...]
    reshape x10 -> x0, local copies, waits for them, and re-layouts: 9.61 us -> none  [the longest x6 7.28 us: local(): packed = jnp.concatenate([item.reshape(n_all, -1) for item in full], 1)]
    sub x1 -> x0, matrix products: 7.51 us -> none  [local(): probs = jnp.exp(scores - top)]
    convert_element_type x3 -> x1, other arithmetic: 7.85 us -> 1.2 us  [local(): hidden_grad = (cotangent.astype(F32) + rstd * (dxhat - jnp.mean(dxhat, -1...]
    reduce_sum x2 -> x1, other arithmetic: 3.36 us -> 0.24 us  [norm_components(): spread = jnp.mean(centered * centered, -1, keepdims=True)]
    pad x3 -> x0, local copies, waits for them, and re-layouts: 2.82 us -> none  [the longest x1 1.3 us: local(): jnp.pad(qkv_grad.astype(BF), ((0, 0), (0, PAGE - 3 * width)))]
    reduce_sum x2 -> x1, other arithmetic: 2.93 us -> 0.13 us  [norm_components(): center = jnp.mean(values_in, -1, keepdims=True)]
where the time goes in v4:
time: 176 us; the launch traced here: 175 us
  Pallas kernels  157 us (89%)
  local copies, waits for them, and re-layouts  13.5 us (8%)
  other arithmetic  3.3 us (2%)
    pallas_call x1, Pallas kernels, gather_all(): pl.pallas_call(gather_kernel, out_shape=(jax.ShapeDtypeStruct((tokens * N...  64.2 us
    pallas_call x1, Pallas kernels, reduce_all(): pl.pallas_call(reduce_kernel, out_shape=(jax.ShapeDtypeStruct((PART, N_SP...  50.7 us
    pallas_call x1, Pallas kernels, compute_all(): pl.pallas_call(compute_kernel, out_shape=(jax.ShapeDtypeStruct((D, PAGE),...  42.2 us
    unnamed x27, local copies, waits for them, and re-layouts  11.8 us

profile of v4, /device:TPU:1, one launch (start us, length us, event | category | flops | bytes accessed | tf_op | source)
XLA Modules:
  0.0 174.7 jit_solution(6234717028944413308)
XLA Ops:
  0.6 1.4 add_bitcast_fusion.small_ref
  2.0 64.2 %gather_all.1 = (bf16[1024,768]{1,0:T(8,128)(2,1)}, bf16[1024,768]{1,0:T(8,128)(2,1)}, bf16[4,4,2,24,768]{4,3,2,1,0:T(8,128)(2,1)}, bf16[4,4,2,24,768]{4,3,2,1,0...) custom-call(bf16[256,768]{1,0:T(8,128)(2,1)} %x_ref.1, bf16[256,768]{1,0:T(8,128)(2,1)} %g_ref.1, ...), custom_call_target="tpu_custom_call" | custom-call | tf_op jit(solution)/shard_map/gather_all/pallas_call | solution.py:279
  66.2 42.2 %compute_all.1 = (bf16[768,768]{1,0:T(8,128)(2,1)}, bf16[768,768]{1,0:T(8,128)(2,1)}, bf16[32,6,768]{2,1,0:T(8,128)(2,1)}, bf16[768,768]{1,0:T(8,128)(2,1)}, f32...) custom-call(bf16[1024,768]{1,0:T(8,128)(2,1)} %get-tuple-element.35.x_ref, ...), custom_call_target="tpu_custom_call" | custom-call | flops 14000000000 | bytes 16000000 | tf_op jit(solution)/shard_map/compute_all/pallas_call | solution.py:808
  108.4 1.4 copy-done
  109.8 1.4 copy-done.1
  111.2 1.3 copy-done.2
  112.5 1.3 copy-done.3
  113.7 1.3 copy-done.4
  115.0 1.0 copy-done.5
  116.0 0.9 copy-done.6
  116.9 50.7 %reduce_all.1 = (f32[6,3072]{1,0:T(8,128)S(1)}, f32[6,2304]{1,0:T(8,128)S(1)}, f32[24,768]{1,0:T(8,128)S(1)}, f32[6,768]{1,0:T(8,128)S(1)}, f32[8,128]{1,0:T(8,1...) custom-call(bf16[4,4,2,24,768]{4,3,2,1,0:T(8,128)(2,1)S(1)} %bitcast.29, ...), custom_call_target="tpu_custom_call" | custom-call | tf_op jit(solution)/shard_map/reduce_all/pallas_call | solution.py:514
  167.7 0.1 convert_reduce_fusion
  167.8 0.2 fusion.9
  168.1 0.3 fusion.12
  168.5 0.2 copy-done.8
  168.7 1.2 fusion.8
  169.9 0.6 slice_bitcast_fusion.1
  170.5 0.6 slice_bitcast_fusion
  171.0 0.6 slice_bitcast_fusion.2
  171.6 0.5 copy.35
  172.1 0.6 copy.36
  172.8 0.6 copy.37
  173.4 0.6 copy.38
  174.0 0.6 copy.39
  (19 shorter events, 0.1 us)
Async XLA Ops:
  108.4 1.4 copy-start
  109.8 1.4 copy-start.1
  111.2 1.3 copy-start.2
  112.4 1.3 copy-start.3
  113.7 1.3 copy-start.4
  115.0 1.0 copy-start.5
  116.0 0.9 copy-start.6
  116.9 50.8 %copy-start.7 = (bf16[256,768]{1,0:T(8,128)(2,1)S(1)}, bf16[256,768]{1,0:T(8,128)(2,1)}, u32[]{:S(2)}) copy-start(bf16[256,768]{1,0:T(8,128)(2,1)} %x_ref.1) | copy-start | bytes 1179652
  167.6 0.8 copy-start.9
  167.7 1.0 copy-start.8
  170.5 4.2 %copy-start.10 = (f32[6]{0:T(128)}, f32[6]{0:T(128)S(1)}, u32[]{:S(2)}) copy-start(f32[6]{0:T(128)S(1)} %get-tuple-element.118) | copy-start | bytes 76

commit v5 on v1

v5 whole, which is shorter than its diff:
```python
import functools
import types

import jax
import jax.numpy as jnp
import numpy as np
from jax import lax
from jax.experimental import pallas as pl
from jax.experimental.pallas import tpu as pltpu
from jax.sharding import PartitionSpec as P

D = 768
HEADS = 12
HEAD_DIM = 64
ROT = 16
FF = 3072
BF = jnp.bfloat16
F32 = jnp.float32
BOTH = ("dp", "sp")


def dot(left, right):
    return jnp.dot(left, right, preferred_element_type=F32)


MESH = pl.DeviceIdType.MESH
SMALL = 128
PAGE = 768
NY, NZ, NX = 4, 4, 2
GROUP = NZ * NX
N_SP = 4
PART = 6


def place():
    dp, sp = lax.axis_index("dp"), lax.axis_index("sp")
    return dp, sp, dp // GROUP, lax.rem(dp // NX, NZ), lax.rem(dp, NX)


def send(src, dst, send_sem, recv_sem, device):
    return pltpu.make_async_remote_copy(
        src_ref=src,
        dst_ref=dst,
        send_sem=send_sem,
        recv_sem=recv_sem,
        device_id=device,
        device_id_type=MESH,
    )


def index_of(y, z, x):
    return (y * NZ + z) * NX + x


def slot_device(dp, sp):
    line = dp * N_SP + sp
    return lax.rem(line, NY * GROUP), line // (NY * GROUP)


def owner_device(dp, sp):
    line = sp * NY * GROUP + dp
    return line // N_SP, lax.rem(line, N_SP)


def differs(device, dp, sp):
    return jnp.logical_or(device[0] != dp, device[1] != sp)


class Plane:
    def __init__(self, last):
        self.last = last
        dp, sp, y, z, x = place()
        self.sp, self.y, self.z, self.x = sp, y, z, x
        self.mine = (z if last == "y" else y) * NX + x
        self.axis = y if last == "y" else z

    def member(self, k):
        e = lax.rem(self.mine + k, GROUP)
        a, x = e // NX, lax.rem(e, NX)
        y, z = (self.y, a) if self.last == "y" else (a, self.z)
        return (index_of(y, z, x), self.sp), e, a, x

    def along(self, k):
        a = lax.rem(self.axis + k, NY)
        y, z = (a, self.z) if self.last == "y" else (self.y, a)
        return (index_of(y, z, self.x), self.sp), a

    def block(self, ref, a):
        return ref.at[a] if self.last == "y" else ref.at[:, a]

    def chunk(self, ref, e):
        a, x = e // NX, lax.rem(e, NX)
        return ref.at[self.y, a, x] if self.last == "y" else ref.at[a, self.z, x]


def greet(*partners):
    dp, sp, y, z, x = place()
    barrier = pltpu.get_barrier_semaphore()

    def signal(device):
        pl.semaphore_signal(barrier, inc=1, device_id=device, device_id_type=MESH)

    for k in range(1, N_SP):
        signal((dp, lax.rem(sp + k, N_SP)))
    by_y, by_z = Plane("y"), Plane("z")
    for k in range(1, GROUP):
        signal(by_y.member(k)[0])
        signal(by_z.member(k)[0])

    @pl.when(differs(partners[0], dp, sp))
    def _():
        for partner in partners:
            signal(partner)

    count = N_SP - 1 + 2 * (GROUP - 1)
    more = jnp.where(differs(partners[0], dp, sp), len(partners), 0)
    pl.semaphore_wait(barrier, count + more)


BLOCK = 256


def dot_nt(left, right):
    return lax.dot_general(left, right, (((1,), (1,)), ((), ())), preferred_element_type=F32)


def dot_tn(left, right):
    return lax.dot_general(left, right, (((0,), (0,)), ((), ())), preferred_element_type=F32)


def iota(shape, axis):
    return lax.broadcasted_iota(jnp.int32, shape, axis)


def rotary_tables(length):
    half = ROT // 2
    frequency = np.float32(10000.0) ** (np.float32(-2.0) * np.arange(half, dtype=np.float32) / ROT)
    angles = np.arange(length, dtype=np.float32)[:, None] * frequency[None, :].astype(np.float32)
    cosine = np.ones((length, HEAD_DIM), np.float32)
    sine = np.zeros((length, HEAD_DIM), np.float32)
    cosine[:, :half] = cosine[:, half:ROT] = np.cos(angles)
    sine[:, :half] = -np.sin(angles)
    sine[:, half:ROT] = np.sin(angles)
    return jnp.asarray(np.tile(cosine, (1, 2))), jnp.asarray(np.tile(sine, (1, 2)))


def swap_halves(u):
    low = lax.rem(iota(u.shape, 1), 16) < 8
    return jnp.where(low, pltpu.roll(u, 120, 1), pltpu.roll(u, 8, 1))


def column_of(c, sp, kind):
    if kind == "qkv":
        width = D // N_SP
        return (c // width) * D + sp * width + lax.rem(c, width)
    return c + sp * (FF // N_SP) if kind == "up" else c


VECTORS_IN = (
    (0, 6, "", D), (6, 6, "", D), (12, 6, "", D), (18, 6, "", D),
    (24, 18, "qkv", PAGE), (42, 6, "", D), (48, 24, "up", PAGE), (72, 6, "", D),
)
VECTORS_OUT = (
    (0, 6, "", D), (6, 6, "", D), (12, 6, "", D), (18, 6, "", D),
    (24, 18, "qkv", PAGE), (42, 6, "", D), (48, 24, "up", PAGE),
)


QK = 640


def layer_kernel(names, *refs):
    r = types.SimpleNamespace(**dict(zip(names, refs)))
    dp, sp, y, z, x = place()
    to_slot, to_owner = slot_device(dp, sp), owner_device(dp, sp)
    sibling = sp + 1 - 2 * lax.rem(sp, 2)
    across = lax.rem(sp + 2, N_SP)
    sib_across = lax.rem(sibling + 2, N_SP)
    moves = differs(to_slot, dp, sp)
    stays = jnp.logical_not(moves)
    by_y, by_z = Plane("y"), Plane("z")
    length = r.x_all.shape[0]
    tokens = length // N_SP
    heads = HEADS // N_SP
    width = heads * HEAD_DIM
    n_own = NY * NZ * NX * N_SP
    steps = length // BLOCK
    slot = to_slot[0]
    slot_at = (slot // GROUP, lax.rem(slot // NX, NZ), lax.rem(slot, NX))

    def local_wait(ref, sem):
        pltpu.make_async_copy(ref, ref, sem).wait()

    def rows_of(s):
        return pl.ds(pl.multiple_of(s * tokens, tokens), tokens)

    def rows_at(i):
        return pl.ds(pl.multiple_of(i * BLOCK, BLOCK), BLOCK)

    greet(to_slot, to_owner)

    row_arrays = ((r.down_ref, r.down_all), (r.dense_ref, r.dense_all))

    def row_copies():
        return [
            send(src, dst.at[slot_at], r.r_send.at[i], r.r_recv.at[i], to_slot)
            for i, (src, dst) in enumerate(row_arrays)
        ]

    @pl.when(moves)
    def _():
        for item in row_copies():
            item.start()

    @pl.when(stays)
    def _():
        for i, (src, dst) in enumerate(row_arrays):
            pltpu.make_async_copy(src, dst.at[y, z, x], r.r_recv.at[i]).start()

    end = PAGE + 3 * width
    wide = r.qkv_ref[...].astype(F32)
    for t in range(N_SP):
        r.pieces[t, :, :PAGE] = r.up_ref[:, t * PAGE : (t + 1) * PAGE].astype(F32)
        for j in range(3):
            at = j * D + t * width
            r.pieces[t, :, PAGE + j * width : PAGE + (j + 1) * width] = wide[:, at : at + width]
        r.pieces[t, :, end : PAGE + QK] = jnp.zeros((PART, PAGE + QK - end), F32)
        r.pieces[t, 0:1, PAGE + QK :] = r.small_ref[...]
        r.pieces[t, 1:, PAGE + QK :] = jnp.zeros((PART - 1, SMALL), F32)

    def piece(k):
        t = lax.rem(sp + k, N_SP)
        return send(r.pieces.at[t], r.landed.at[sp], r.p_send.at[k], r.p_recv.at[sp], (dp, t))

    for k in range(1, N_SP):
        piece(k).start()
    pltpu.make_async_copy(r.pieces.at[sp], r.landed.at[sp], r.p_recv.at[sp]).start()

    token_arrays = ((r.x_ref, r.x_all), (r.g_ref, r.g_all))

    def token_copies(kind):
        made = []
        for i, (src, dst) in enumerate(token_arrays):
            if kind == "pass":
                there = dst.at[rows_of(across)]
                pair = (r.t_send.at[i, 2], r.t_recv.at[i, across])
                made.append(send(there, there, *pair, (dp, sibling)))
            else:
                to, n = (across, 0) if kind == "across" else (sibling, 1)
                pair = (r.t_send.at[i, n], r.t_recv.at[i, sp])
                made.append(send(src, dst.at[rows_of(sp)], *pair, (dp, to)))
        return made

    def token_wait(s):
        for i, (src, dst) in enumerate(token_arrays):
            pltpu.make_async_copy(src, dst.at[rows_of(s)], r.t_recv.at[i, s]).wait()

    for item in token_copies("across") + token_copies("sibling"):
        item.start()
    for i, (src, dst) in enumerate(token_arrays):
        pltpu.make_async_copy(src, dst.at[rows_of(sp)], r.t_recv.at[i, sp]).start()

    SMALLS, UP, DOWN, QKV, DENSE = range(5)
    gathered = (
        (by_y, r.small_all), (by_y, r.up_all), (by_z, r.down_all), (by_z, r.qk_all),
        (by_y, r.dense_all),
    )

    def stage_a(n):
        plane, out = gathered[n]
        mine = out.at[y, z, x]
        return [
            send(mine, mine, r.a_send.at[n, k], r.a_recv.at[n, plane.mine], plane.member(k)[0])
            for k in range(1, GROUP)
        ]

    def stage_b(n):
        plane, out = gathered[n]
        there = plane.block(out, plane.axis)
        return [
            send(there, there, r.b_send.at[n, k], r.b_recv.at[n, plane.axis], plane.along(k)[0])
            for k in range(1, NY)
        ]

    def start_a(n):
        for item in stage_a(n):
            item.start()

    def start_b(n):
        plane, out = gathered[n]
        for k in range(1, GROUP):
            e = lax.rem(plane.mine + k, GROUP)
            local_wait(plane.chunk(out, e), r.a_recv.at[n, e])
        for item in stage_b(n):
            item.start()

    def wait_b(n):
        plane, out = gathered[n]
        for k in range(1, NY):
            a = plane.along(k)[1]
            local_wait(plane.block(out, a), r.b_recv.at[n, a])

    for s in range(N_SP):
        local_wait(r.landed.at[s], r.p_recv.at[s])
    for s in range(N_SP):
        r.tight[s * PART : (s + 1) * PART, :] = r.landed[s]
    r.small_all[y, z, x] = jnp.zeros((8, SMALL), F32)
    for s in range(N_SP):
        r.small_all[y, z, x, s : s + 1, :] = r.landed[s, 0:1, PAGE + QK :]
    r.up_all[y, z, x] = r.tight[:, :PAGE].astype(BF)
    r.qk_all[y, z, x] = r.tight[:, PAGE : PAGE + QK].astype(BF)
    start_a(SMALLS)
    start_a(UP)
    local_wait(r.down_all.at[y, z, x], r.r_recv.at[0])
    start_a(DOWN)
    local_wait(r.dense_all.at[y, z, x], r.r_recv.at[1])
    start_b(SMALLS)
    start_b(UP)
    start_b(DOWN)
    token_wait(across)
    for item in token_copies("pass"):
        item.start()
    start_a(QKV)
    start_a(DENSE)

    wait_b(SMALLS)
    packed = r.small_all[...].reshape(2 * n_own, SMALL).astype(BF)
    n_rows = 2 * n_own

    def owner_rows(size):
        row = iota((n_rows, size), 0)
        inside = lax.rem(row, 8)
        return jnp.where(inside < N_SP, row // 8 * N_SP + inside, -1)

    for n, (start, each, kind, size) in enumerate(VECTORS_IN):
        lane = column_of(iota((SMALL, size), 1), sp, kind)
        spread = (iota((SMALL, size), 0) == start + lax.rem(lane, each)).astype(BF)
        lane = column_of(iota((n_rows, size), 1), sp, kind)
        values = jnp.where(lane // each == owner_rows(size), dot(packed, spread), 0.0)
        r.vec_s[n : n + 1, :] = jnp.sum(values, 0, keepdims=True)
    gain_1, shift_1, gain_2, shift_2 = (r.vec_s[n : n + 1, :] for n in range(4))
    qkv_add = r.vec_s[4:5, :QK]
    up_add = r.vec_s[6:7, :]
    bias = r.vec_s[5:6, :] + r.vec_s[7:8, :]

    def fold(values):
        return jnp.sum(values.reshape(-1, 8, values.shape[-1]), 0)

    for s in (sp, sibling, sib_across):
        token_wait(s)

    @pl.loop(0, steps)
    def _(i):
        rows = rows_at(i)
        values = r.x_all[rows, :].astype(F32)
        centered = values - jnp.mean(values, -1, keepdims=True)
        xhat = centered * lax.rsqrt(jnp.mean(centered * centered, -1, keepdims=True) + 1e-05)
        r.xhat_s[rows, :] = xhat
        r.n1_s[rows, :] = (xhat * gain_1 + shift_1).astype(BF)
        r.n2_s[rows, :] = (xhat * gain_2 + shift_2).astype(BF)

    def join(src, dst):
        @pl.loop(0, NY * NZ)
        def _(i):
            a, b = i // NZ, lax.rem(i, NZ)
            pair = [src[a, b, e].astype(F32) for e in range(NX)]
            own = pair[0].shape[0] * NX
            dst[pl.ds(pl.multiple_of(i * own, own), own), :] = jnp.concatenate(pair, 0).astype(BF)

    start_b(QKV)
    start_b(DENSE)
    wait_b(UP)
    join(r.up_all, r.up_s)
    wait_b(DOWN)
    join(r.down_all, r.down_s)

    zeros = jnp.zeros((8, D), F32)

    def first(i, sums):
        rows = rows_at(i)
        g = r.g_all[rows, :]
        pre = dot(r.n2_s[rows, :], r.up_s[...]) + up_add
        cdf = 0.5 * (1.0 + lax.erf(pre * 0.7071067811865476))
        act = (pre * cdf).astype(BF)
        r.act_s[rows, :] = act
        pdf = jnp.exp(-0.5 * pre * pre) * 0.3989422804014327
        dpre = (dot_nt(g, r.down_s[...]) * (cdf + pre * pdf)).astype(BF)
        r.dpre_s[rows, :] = dpre
        r.sum_s[rows, :] = dot(act, r.down_s[...])
        dn2 = dot_nt(dpre, r.up_s[...])
        r.dx_s[rows, :] = dn2 * gain_2
        one, two, three = sums
        return (
            one + fold(dpre.astype(F32)),
            two + fold(dn2 * r.xhat_s[rows, :]),
            three + fold(dn2),
        )

    up_bias, gain_2_grad, shift_2_grad = lax.fori_loop(0, steps, first, (zeros,) * 3)

    half = D // 2
    in_half = half // (PART * N_SP)

    def weight_grad(left, right, out):
        @pl.loop(0, 2)
        def _(i):
            lanes = pl.ds(pl.multiple_of(i * half, half), half)
            value = dot_tn(left[:, lanes], right[...])
            own = PART * N_SP
            for c in range(in_half):
                at = (i * (NY // 2) + c // GROUP, c // NX % NZ, c % NX)
                out[at[0], at[1], at[2]] = value[c * own : (c + 1) * own, :].astype(BF)

    reduced = (
        (by_y, r.small_g, r.small_1, r.small_m, r.small_2),
        (by_y, r.up_g, r.up_1, r.up_m, r.up_2),
        (by_z, r.down_g, r.down_1, r.down_m, r.down_2),
        (by_z, r.qk_g, r.qk_1, r.qk_m, r.qk_2),
        (by_y, r.dense_g, r.dense_1, r.dense_m, r.dense_2),
    )

    def stage_1(n):
        plane, src, land = reduced[n][:3]
        made = []
        for k in range(1, NY):
            device, a = plane.along(k)
            pair = (r.e_send.at[n, k], r.e_recv.at[n, plane.axis])
            made.append(send(plane.block(src, a), land.at[plane.axis], *pair, device))
        return made

    def stage_2(n):
        plane, _, _, mid, land = reduced[n]
        made = []
        for k in range(1, GROUP):
            device, e, a, xx = plane.member(k)
            pair = (r.f_send.at[n, k], r.f_recv.at[n, plane.mine])
            made.append(send(mid.at[a, xx], land.at[plane.mine], *pair, device))
        return made

    def start_1(n):
        for item in stage_1(n):
            item.start()

    def start_2(n):
        plane, src, land, mid, _ = reduced[n]
        for k in range(1, NY):
            a = plane.along(k)[1]
            local_wait(land.at[a], r.e_recv.at[n, a])

        @pl.loop(0, GROUP)
        def _(e):
            a, xx = e // NX, lax.rem(e, NX)
            own = src[plane.axis, a, xx] if plane.last == "y" else src[a, plane.axis, xx]
            total = own.astype(F32)
            for k in range(1, NY):
                total = total + land[lax.rem(plane.axis + k, NY), a, xx].astype(F32)
            mid[a, xx] = total.astype(mid.dtype)

        for item in stage_2(n):
            item.start()

    def finish(n):
        plane, _, _, mid, land = reduced[n]
        for k in range(1, GROUP):
            e = lax.rem(plane.mine + k, GROUP)
            local_wait(land.at[e], r.f_recv.at[n, e])
        total = mid[plane.mine // NX, lax.rem(plane.mine, NX)].astype(F32)
        for k in range(1, GROUP):
            total = total + land[lax.rem(plane.mine + k, GROUP)].astype(F32)
        return total

    weight_grad(r.act_s, r.g_all, r.down_g)
    start_1(DOWN)
    weight_grad(r.n2_s, r.dpre_s, r.up_g)
    start_1(UP)

    wait_b(QKV)
    join(r.qk_all, r.qk_s)
    wait_b(DENSE)
    for e in range(NY * NZ * NX):
        r.dense_wide[e * PART : (e + 1) * PART, :] = r.dense_all[
            e // GROUP, e // NX % NZ, e % NX
        ].astype(F32)
    r.dense_s[...] = r.dense_wide[...].astype(BF)

    @pl.loop(0, steps)
    def _(i):
        rows = rows_at(i)
        y_rows = dot(r.n1_s[rows, :], r.qk_s[...]) + qkv_add
        cosine, sine = r.cos_ref[rows, :], r.sin_ref[rows, :]
        turned = []
        for p in range(2 * width // 128):
            u = y_rows[:, p * 128 : (p + 1) * 128]
            turned.append(u * cosine + swap_halves(u) * sine)
        d = dot_nt(r.g_all[rows, :], r.dense_s[...])

        def head(n):
            u = turned[n // 2]
            return u[:, (n % 2) * HEAD_DIM : (n % 2 + 1) * HEAD_DIM]

        for h in range(heads):
            at = 2 * width + h * HEAD_DIM
            r.q_s[h, rows, :] = head(h).astype(BF)
            r.k_s[h, rows, :] = head(heads + h).astype(BF)
            r.v_s[h, rows, :] = y_rows[:, at : at + HEAD_DIM].astype(BF)
            r.do_s[h, rows, :] = d[:, h * HEAD_DIM : (h + 1) * HEAD_DIM].astype(BF)

    scale = HEAD_DIM ** (-0.5)

    def attend(h):
        r.kt_s[...] = r.k_s[h].astype(F32).T.astype(BF)
        r.vt_s[...] = r.v_s[h].astype(F32).T.astype(BF)
        for i in reversed(range(steps)):
            keys = (i + 1) * BLOCK
            rows = slice(i * BLOCK, (i + 1) * BLOCK)
            q, do = r.q_s[h, rows, :], r.do_s[h, rows, :]
            scores = dot_nt(r.k_s[h, :keys, :], q) * scale
            hidden = iota((BLOCK, BLOCK), 0) > iota((BLOCK, BLOCK), 1)
            corner = jnp.where(hidden, -1e30, scores[i * BLOCK :, :])
            scores = jnp.concatenate([scores[: i * BLOCK, :], corner], 0) if i else corner
            expo = jnp.exp(scores - jnp.max(scores, 0, keepdims=True))
            probs = expo * (1.0 / jnp.sum(expo, 0, keepdims=True))
            low = probs.astype(BF)
            r.ctxt_s[h, :, rows] = dot(r.vt_s[:, :keys], low).astype(BF)
            dprobs = dot_nt(r.v_s[h, :keys, :], do)
            delta = jnp.sum(probs * dprobs, 0, keepdims=True)
            dscores = (probs * (dprobs - delta) * scale).astype(BF)
            r.dq_s[h, rows, :] = dot(r.kt_s[:, :keys], dscores).T.astype(BF)
            dk = dot(dscores, q)
            dv = dot(low, do)
            if i == steps - 1:
                r.dk_s[h] = dk
                r.dv_s[h] = dv
            else:
                r.dk_s[h, :keys, :] += dk
                r.dv_s[h, :keys, :] += dv

    @pl.loop(0, heads)
    def _(h):
        attend(h)

        @pl.when(h == 0)
        def _():
            start_2(DOWN)

        @pl.when(h == 1)
        def _():
            start_2(UP)

    sums_of = (r.act_s, r.dpre_s)

    def token_pair(i):
        src = sums_of[i]
        return [
            send(
                src.at[rows_of(t)], r.token_in.at[i, n], r.g_send.at[i, n], r.g_recv.at[i, n],
                (dp, sibling),
            )
            for n, t in enumerate((sibling, sib_across))
        ]

    def token_far_copy(i):
        pair = (r.h_send.at[i], r.h_recv.at[i])
        return send(r.token_mid.at[i], r.token_far.at[i], *pair, (dp, across))

    def token_cross(i):
        for item in token_pair(i):
            item.wait_recv()
        own = sums_of[i][rows_of(across), :].astype(F32)
        r.token_mid[i] = (own + r.token_in[i, 1].astype(F32)).astype(BF)
        token_far_copy(i).start()

    def token_total(i):
        token_far_copy(i).wait()
        own = sums_of[i][rows_of(sp), :].astype(F32)
        return own + r.token_in[i, 0].astype(F32) + r.token_far[i].astype(F32)

    ctxt = r.ctxt_s[...].reshape(width, length)
    for i in range(steps):
        rows = slice(i * BLOCK, (i + 1) * BLOCK)
        r.act_s[rows, :] = (r.sum_s[rows, :] + dot_tn(ctxt[:, rows], r.dense_s[...])).astype(BF)
    for item in token_pair(0):
        item.start()

    def last(i, sums):
        rows = rows_at(i)
        cosine, sine = r.cos_ref[rows, :], r.sin_ref[rows, :]
        parts = [
            ref[h, rows, :].astype(F32) for ref in (r.dq_s, r.dk_s, r.dv_s) for h in range(heads)
        ]
        blocks = []
        for p in range(2 * width // 128):
            u = jnp.concatenate(parts[2 * p : 2 * p + 2], 1).astype(BF).astype(F32)
            blocks.append((u * cosine - swap_halves(u) * sine).astype(BF))
        rest = parts[2 * heads :] + [jnp.zeros((BLOCK, QK - 3 * width), F32)]
        dqkv = jnp.concatenate(blocks + [jnp.concatenate(rest, 1).astype(BF)], 1)
        r.dqkv_s[rows, :] = dqkv
        dn1 = dot_nt(dqkv, r.qk_s[...])
        r.dpre_s[rows, :] = (r.dx_s[rows, :] + dn1 * gain_1).astype(BF)
        one, two, three = sums
        return (
            one + fold(dqkv.astype(F32)),
            two + fold(dn1 * r.xhat_s[rows, :]),
            three + fold(dn1),
        )

    qkv_bias, gain_1_grad, shift_1_grad = lax.fori_loop(
        0, steps, last, (jnp.zeros((8, QK), F32), zeros, zeros)
    )
    weight_grad(r.n1_s, r.dqkv_s, r.qk_g)
    start_1(QKV)
    for item in token_pair(1):
        item.start()
    token_cross(0)
    dense_grad = dot(ctxt, r.g_all[...])
    for e in range(NY * NZ * NX):
        r.dense_g[e // GROUP, e // NX % NZ, e % NX] = dense_grad[
            e * PART : (e + 1) * PART, :
        ].astype(BF)
    start_1(DENSE)

    g_here = r.g_all[rows_of(sp), :].astype(F32)
    values = (
        gain_1_grad, shift_1_grad, gain_2_grad, shift_2_grad, qkv_bias, fold(g_here), up_bias
    )
    result = jnp.zeros((n_rows, SMALL), F32)
    for (start, each, kind, _), item in zip(VECTORS_OUT, values):
        vector = jnp.sum(item, 0, keepdims=True)
        size = vector.shape[1]
        lane = column_of(iota((n_rows, size), 1), sp, kind)
        mine = lane // each == owner_rows(size)
        if kind == "qkv":
            mine = jnp.logical_and(mine, iota((n_rows, size), 1) < 3 * width)
        rest = jnp.where(mine, vector, 0.0)
        lane = column_of(iota((size, SMALL), 0), sp, kind)
        pick = (iota((size, SMALL), 1) == start + lax.rem(lane, each)).astype(BF)
        for _ in range(3):
            part = rest.astype(BF)
            result = result + dot(part, pick)
            rest = rest - part.astype(F32)
    for e in range(NY * NZ * NX):
        r.small_g[e // GROUP, e // NX % NZ, e % NX] = result[e * 8 : (e + 1) * 8, :]
    start_1(SMALLS)
    token_cross(1)
    start_2(QKV)

    up_total = finish(UP)
    for t in range(N_SP):
        r.up_p[t] = up_total[t * PART : (t + 1) * PART, :]

    def back(n, k):
        src, land = ((r.up_p, r.up_l), (r.qk_p, r.qk_l))[n]
        t = lax.rem(sp + k, N_SP)
        return send(src.at[t], land.at[sp], r.i_send.at[n, k], r.i_recv.at[n, sp], (dp, t))

    for k in range(1, N_SP):
        back(0, k).start()
    owned = ((r.down_t, r.down_out), (r.dense_t, r.dense_out))

    def own_copy(i):
        src, dst = owned[i]
        return send(src, dst, r.j_send.at[i], r.j_recv.at[i], to_owner)

    def start_own(i):
        @pl.when(moves)
        def _():
            own_copy(i).start()

        @pl.when(stays)
        def _():
            pltpu.make_async_copy(*owned[i], r.j_recv.at[i]).start()

    r.down_t[...] = finish(DOWN)
    start_own(0)
    start_2(DENSE)
    start_2(SMALLS)
    qk_total = finish(QKV)
    for t in range(N_SP):
        r.qk_p[t] = qk_total[t * PART : (t + 1) * PART, :]
    for k in range(1, N_SP):
        back(1, k).start()
    r.dense_t[...] = finish(DENSE)
    start_own(1)
    r.small_l[sp] = finish(SMALLS)

    def small_copy(k):
        there = r.small_l.at[sp]
        return send(
            there, there, r.k_send.at[k], r.k_recv.at[sp], (dp, lax.rem(sp + k, N_SP))
        )

    for k in range(1, N_SP):
        small_copy(k).start()

    x_here = r.x_all[rows_of(sp), :].astype(F32)
    r.hidden_out[...] = (x_here + token_total(0) + bias).astype(BF)
    dxhat = token_total(1)
    centered = x_here - jnp.mean(x_here, -1, keepdims=True)
    rstd = lax.rsqrt(jnp.mean(centered * centered, -1, keepdims=True) + 1e-05)
    xhat = centered * rstd
    r.hidden_grad[...] = (
        r.g_all[rows_of(sp), :].astype(F32)
        + rstd
        * (
            dxhat
            - jnp.mean(dxhat, -1, keepdims=True)
            - xhat * jnp.mean(dxhat * xhat, -1, keepdims=True)
        )
    ).astype(BF)

    r.up_l[sp] = r.up_p[sp]
    r.qk_l[sp] = r.qk_p[sp]
    for n, land in enumerate((r.up_l, r.qk_l)):
        for k in range(1, N_SP):
            s = lax.rem(sp + k, N_SP)
            local_wait(land.at[s], r.i_recv.at[n, s])
    for s in range(N_SP):
        r.up_out[:, s * PAGE : (s + 1) * PAGE] = r.up_l[s]
        block = r.qk_l[s]
        for j in range(3):
            to = j * D + s * width
            r.qkv_out[:, to : to + width] = block[:, j * width : (j + 1) * width]
    for k in range(1, N_SP):
        s = lax.rem(sp + k, N_SP)
        local_wait(r.small_l.at[s], r.k_recv.at[s])
    r.small_out[...] = jnp.sum(r.small_l[...], 0)
    for i in range(2):
        pltpu.make_async_copy(*owned[i], r.j_recv.at[i]).wait()

    for kind in ("across", "sibling", "pass"):
        for item in token_copies(kind):
            item.wait_send()

    @pl.when(moves)
    def _():
        for item in row_copies():
            item.wait_send()
        for i in range(2):
            own_copy(i).wait_send()

    for k in range(1, N_SP):
        piece(k).wait_send()
        back(0, k).wait_send()
        back(1, k).wait_send()
        small_copy(k).wait_send()
    for i in range(2):
        for item in token_pair(i):
            item.wait_send()
    for n in range(5):
        for item in stage_a(n) + stage_b(n) + stage_1(n) + stage_2(n):
            item.wait_send()


def layer(x, g, up, qkv, small, down, dense):
    tokens = x.shape[0]
    length = tokens * N_SP
    heads = HEADS // N_SP
    width = heads * HEAD_DIM
    grid = (NY, NZ, NX)
    own = PART * N_SP
    cosine, sine = rotary_tables(length)
    dma = pltpu.SemaphoreType.DMA
    anywhere = pl.BlockSpec(memory_space=pl.ANY)
    vmem = pl.BlockSpec(memory_space=pltpu.VMEM)
    ins = ("x_ref", "g_ref", "up_ref", "qkv_ref", "small_ref", "down_ref", "dense_ref")
    ins += ("cos_ref", "sin_ref")
    outs = {
        "hidden_out": ((tokens, D), BF),
        "hidden_grad": ((tokens, D), BF),
        "up_out": ((PART, FF), F32),
        "qkv_out": ((PART, 3 * D), F32),
        "down_out": ((own, D), F32),
        "dense_out": ((PART, D), F32),
        "small_out": ((8, SMALL), F32),
    }
    chunk = {
        "up": ((own, PAGE), BF),
        "down": ((own, D), BF),
        "qk": ((own, QK), BF),
        "dense": ((PART, D), BF),
        "small": ((8, SMALL), F32),
    }
    scratch = {}
    for name, (shape, kind) in chunk.items():
        scratch[name + "_all"] = (grid + shape, kind)
        scratch[name + "_g"] = (grid + shape, kind)
        scratch[name + "_1"] = (grid + shape, kind)
        scratch[name + "_m"] = ((GROUP // NX, NX) + shape, kind)
        scratch[name + "_2"] = ((GROUP,) + shape, kind)
    per_head = (heads, length, HEAD_DIM)
    scratch.update(
        x_all=((length, D), BF),
        g_all=((length, D), BF),
        pieces=((N_SP, PART, PAGE + QK + SMALL), F32),
        landed=((N_SP, PART, PAGE + QK + SMALL), F32),
        tight=((own, PAGE + QK + SMALL), F32),
        up_s=((D, PAGE), BF),
        down_s=((PAGE, D), BF),
        qk_s=((D, QK), BF),
        dense_wide=((width, D), F32),
        dense_s=((width, D), BF),
        vec_s=((8, PAGE), F32),
        xhat_s=((length, D), F32),
        n1_s=((length, D), BF),
        n2_s=((length, D), BF),
        act_s=((length, PAGE), BF),
        dpre_s=((length, PAGE), BF),
        sum_s=((length, D), F32),
        dx_s=((length, D), F32),
        dqkv_s=((length, QK), BF),
        q_s=(per_head, BF),
        k_s=(per_head, BF),
        v_s=(per_head, BF),
        do_s=(per_head, BF),
        dq_s=(per_head, BF),
        dk_s=(per_head, F32),
        dv_s=(per_head, F32),
        kt_s=((HEAD_DIM, length), BF),
        vt_s=((HEAD_DIM, length), BF),
        ctxt_s=((heads, HEAD_DIM, length), BF),
        token_in=((2, 2, tokens, D), BF),
        token_mid=((2, tokens, D), BF),
        token_far=((2, tokens, D), BF),
        up_p=((N_SP, PART, PAGE), F32),
        up_l=((N_SP, PART, PAGE), F32),
        qk_p=((N_SP, PART, QK), F32),
        qk_l=((N_SP, PART, QK), F32),
        down_t=((own, D), F32),
        dense_t=((PART, D), F32),
        small_l=((N_SP, 8, SMALL), F32),
    )
    semaphores = {
        "r": (2,), "p": (N_SP,), "t": (2, N_SP), "a": (5, GROUP), "b": (5, NY), "e": (5, NY),
        "f": (5, GROUP), "g": (2, 2), "h": (2,), "i": (2, N_SP), "j": (2,), "k": (N_SP,),
    }
    names = list(ins) + list(outs) + list(scratch)
    shapes = [pltpu.VMEM(shape, kind) for shape, kind in scratch.values()]
    for name, shape in semaphores.items():
        names += [name + "_send", name + "_recv"]
        shapes += [dma(shape), dma(shape)]
    return pl.pallas_call(
        functools.partial(layer_kernel, names),
        out_shape=tuple(jax.ShapeDtypeStruct(*item) for item in outs.values()),
        in_specs=[anywhere, anywhere, vmem, vmem, vmem, anywhere, anywhere, vmem, vmem],
        out_specs=(vmem,) * len(outs),
        scratch_shapes=shapes,
        compiler_params=pltpu.CompilerParams(
            collective_id=0, has_side_effects=True, vmem_limit_bytes=61 * 1024 * 1024
        ),
        cost_estimate=pl.CostEstimate(
            flops=14_000_000_000, bytes_accessed=16_000_000, transcendentals=6_000_000
        ),
        name="layer",
    )(x, g, up, qkv, small, down, dense, cosine, sine)


def local(
    hidden_in,
    cotangent,
    attn_gain,
    attn_shift,
    mlp_gain,
    mlp_shift,
    qkv_weight,
    qkv_bias,
    dense_weight,
    dense_bias,
    up_weight,
    up_bias,
    down_weight,
    down_bias,
):
    sp = lax.axis_index("sp")
    small = (
        attn_gain,
        attn_shift,
        mlp_gain,
        mlp_shift,
        qkv_bias,
        dense_bias,
        up_bias,
        down_bias,
    )
    packed = jnp.zeros((SMALL,), F32)
    at = 0
    for item in small:
        size = item.shape[0]
        packed = packed + jnp.pad(item.astype(F32), (at, SMALL - at - size))
        at += size
    hidden_out, hidden_grad, up_own, qkv_own, down_own, dense_own, packed = layer(
        hidden_in,
        cotangent,
        up_weight,
        qkv_weight,
        packed.reshape(1, SMALL),
        down_weight,
        dense_weight,
    )
    mine = lax.dynamic_slice_in_dim(packed, sp, 1, 0).reshape(-1)
    parts = [mine[start : start + each] for start, each, _, _ in VECTORS_OUT]
    return (
        hidden_out,
        hidden_grad,
        parts[0],
        parts[1],
        parts[2],
        parts[3],
        qkv_own,
        parts[4],
        dense_own,
        parts[5],
        up_own,
        parts[6],
        down_own,
        parts[5],
    )


def solution(mesh):
    matrix = P(BOTH, None)
    vector = P(BOTH)
    split = (matrix, matrix) + (vector,) * 4 + (matrix, vector) * 4
    return jax.shard_map(local, mesh=mesh, in_specs=split, out_specs=split, check_vma=False)
```

time: 1470 us -> 142 us (0.10)
  waiting for transfers between devices: 1110 us -> 0 us
  blocking collectives: 203 us -> 0 us
  Pallas kernels: 0 us -> 131 us
  matrix products: 62 us -> 0 us
  starting transfers between devices: 33.3 us -> 0 us
  local copies, waits for them, and re-layouts: 30.3 us -> 9.81 us
    reduce_scatter x5 -> x0, waiting for transfers between devices: 735 us -> none  [the longest x1 226 us: local(): lax.psum_scatter(down_grad, 'dp', scatter_dimension=0, tiled=True)]
    unnamed x13 -> x0, waiting for transfers between devices: 328 us -> none
    all_gather x3 -> x0, blocking collectives: 196 us -> none  [the longest x1 82.3 us: local(): qkv_t = lax.all_gather(qkv_part, 'dp', axis=0, tiled=True)]
    pallas_call x0 -> x1, Pallas kernels: none -> 131 us  [layer(): pl.pallas_call(functools.partial(layer_kernel, names), out_shape=tuple((j...]
    dot_general x17 -> x0, matrix products: 53.7 us -> none  [the longest x4 12.7 us: contract_cols(): lax.dot_general(left, right, (((1,), (1,)), ((), ())), preferred_element_...]
    all_gather x4 -> x0, waiting for transfers between devices: 41.8 us -> none  [the longest x1 41.7 us: local(): down_t = lax.all_gather(down_part, 'dp', axis=0, tiled=True)]
    ppermute x4 -> x0, starting transfers between devices: 20 us -> none  [the longest x1 5.74 us: local(): down_part = lax.ppermute(down_weight, BOTH, to_slice)]
  transfers between devices with their start and end apart: 18 -> 0, of which waited for: 9 -> 0; matrix products, arithmetic and copies ran while one was open for 6% -> 0% of each run, Pallas kernels for 0% -> 0%
where the time goes in v5:
time: 142 us
  Pallas kernels  131 us (92%)
  local copies, waits for them, and re-layouts  9.81 us (7%)
    pallas_call x1, Pallas kernels, layer(): pl.pallas_call(functools.partial(layer_kernel, names), out_shape=tuple((j...  131 us
    unnamed x35, local copies, waits for them, and re-layouts  7.37 us

profile of v5, /device:TPU:1, one launch (start us, length us, event | category | flops | bytes accessed | tf_op | source)
XLA Modules:
  0.0 141.9 jit_solution(10509200626653402892)
XLA Ops:
  0.7 0.6 copy-done.12
  1.3 0.0 copy-done.9
  1.3 0.0 copy-done.10
  1.3 0.0 copy-done.11
  1.4 0.0 copy-done.5
  1.4 0.0 copy-done.6
  1.4 0.0 copy-done.7
  1.4 0.6 add_bitcast_fusion.refs_4_
  2.0 130.8 %layer.1 = (bf16[256,768]{1,0:T(8,128)(2,1)}, bf16[256,768]{1,0:T(8,128)(2,1)}, f32[6,3072]{1,0:T(8,128)}, f32[6,2304]{1,0:T(8,128)}, f32[24,768]{1,0:T(8,128)}, /*index=5*/f32[6,768]{1,0:T(8,128)}, f32[8,128]{1,0:T(8,128)}) custom-call(bf16[256,768]{1,0:T(8,128)(2,1)} %refs_0_.1, bf16[256,768]{1,0:T(8,128)(2,1)} %refs_1_.1, bf16[6,3072]{1,0:T(8,128)(2,1)} %refs_2_.1, ...), custom_call_target="tpu_custom_call" | custom-call | flops 14000000000 | bytes 16000000 | tf_op jit(solution)/shard_map/layer/pallas_call | solution.py:841
  132.8 0.7 constant_dynamic-slice_fusion
  133.5 0.6 slice_bitcast_fusion.2
  134.1 0.6 slice_bitcast_fusion
  134.7 0.6 slice_bitcast_fusion.1
  135.3 0.5 copy-done.13
  135.8 0.5 copy.37
  136.3 1.8 %copy.38 = bf16[256,768]{1,0:T(8,128)(2,1)} copy(bf16[256,768]{1,0:T(8,128)(2,1)} %get-tuple-element.75) | data formatting | bytes 786432
  138.1 0.7 copy.39
  138.9 0.2 copy-done.3
  139.0 0.6 copy.40
  139.7 0.1 copy-done.4
  139.8 0.6 copy.41
  140.4 0.6 copy.42
  141.0 0.3 copy-done.2
  141.3 0.6 copy.43
  (17 shorter events, 0.0 us)
Async XLA Ops:
  0.7 0.7 copy-start.12
  0.7 0.7 copy-start.9
  0.7 0.7 copy-start.10
  0.7 0.7 copy-start.11
  0.7 0.7 copy-start.5
  0.7 0.7 copy-start.6
  0.7 0.7 copy-start.7
  0.7 0.7 copy-start.8
  135.3 0.5 copy-start.13
  136.3 1.8 %copy-start = (bf16[256,768]{1,0:T(8,128)(2,1)S(1)}, bf16[256,768]{1,0:T(8,128)(2,1)}, u32[]{:S(2)}) copy-start(bf16[256,768]{1,0:T(8,128)(2,1)} %get-tuple-element.76) | copy-start | bytes 1179652
  138.1 0.9 copy-start.3
  139.0 0.7 copy-start.4
  139.0 1.3 copy-start.1
  140.4 0.9 copy-start.2

commit v6 on v5

--- a/solution.py
+++ b/solution.py
@@ -112,9 +112,12 @@
         for partner in partners:
             signal(partner)
 
+
+def await_greetings(*partners):
+    dp, sp, y, z, x = place()
     count = N_SP - 1 + 2 * (GROUP - 1)
     more = jnp.where(differs(partners[0], dp, sp), len(partners), 0)
-    pl.semaphore_wait(barrier, count + more)
+    pl.semaphore_wait(pltpu.get_barrier_semaphore(), count + more)
 
 
 BLOCK = 256
@@ -199,24 +202,6 @@
 
     greet(to_slot, to_owner)
 
-    row_arrays = ((r.down_ref, r.down_all), (r.dense_ref, r.dense_all))
-
-    def row_copies():
-        return [
-            send(src, dst.at[slot_at], r.r_send.at[i], r.r_recv.at[i], to_slot)
-            for i, (src, dst) in enumerate(row_arrays)
-        ]
-
-    @pl.when(moves)
-    def _():
-        for item in row_copies():
-            item.start()
-
-    @pl.when(stays)
-    def _():
-        for i, (src, dst) in enumerate(row_arrays):
-            pltpu.make_async_copy(src, dst.at[y, z, x], r.r_recv.at[i]).start()
-
     end = PAGE + 3 * width
     wide = r.qkv_ref[...].astype(F32)
     for t in range(N_SP):
@@ -228,6 +213,8 @@
         r.pieces[t, 0:1, PAGE + QK :] = r.small_ref[...]
         r.pieces[t, 1:, PAGE + QK :] = jnp.zeros((PART - 1, SMALL), F32)
 
+    await_greetings(to_slot, to_owner)
+
     def piece(k):
         t = lax.rem(sp + k, N_SP)
         return send(r.pieces.at[t], r.landed.at[sp], r.p_send.at[k], r.p_recv.at[sp], (dp, t))
@@ -236,35 +223,62 @@
         piece(k).start()
     pltpu.make_async_copy(r.pieces.at[sp], r.landed.at[sp], r.p_recv.at[sp]).start()
 
+    def row_copies():
+        return [
+            send(r.down_ref, r.down_in, r.r_send.at[0], r.r_recv.at[0], to_slot),
+            send(
+                r.dense_ref, r.dense_all.at[slot_at], r.r_send.at[1], r.r_recv.at[1], to_slot
+            ),
+        ]
+
+    @pl.when(moves)
+    def _():
+        for item in row_copies():
+            item.start()
+
+    @pl.when(stays)
+    def _():
+        pltpu.make_async_copy(r.down_ref, r.down_in, r.r_recv.at[0]).start()
+        pltpu.make_async_copy(r.dense_ref, r.dense_all.at[y, z, x], r.r_recv.at[1]).start()
+
     token_arrays = ((r.x_ref, r.x_all), (r.g_ref, r.g_all))
 
-    def token_copies(kind):
-        made = []
-        for i, (src, dst) in enumerate(token_arrays):
-            if kind == "pass":
-                there = dst.at[rows_of(across)]
-                pair = (r.t_send.at[i, 2], r.t_recv.at[i, across])
-                made.append(send(there, there, *pair, (dp, sibling)))
-            else:
-                to, n = (across, 0) if kind == "across" else (sibling, 1)
-                pair = (r.t_send.at[i, n], r.t_recv.at[i, sp])
-                made.append(send(src, dst.at[rows_of(sp)], *pair, (dp, to)))
-        return made
-
-    def token_wait(s):
-        for i, (src, dst) in enumerate(token_arrays):
-            pltpu.make_async_copy(src, dst.at[rows_of(s)], r.t_recv.at[i, s]).wait()
-
-    for item in token_copies("across") + token_copies("sibling"):
-        item.start()
-    for i, (src, dst) in enumerate(token_arrays):
+    def token_copies(i, kind):
+        src, dst = token_arrays[i]
+        if kind == "pass":
+            there = dst.at[rows_of(across)]
+            pair = (r.t_send.at[i, 2], r.t_recv.at[i, across])
+            return send(there, there, *pair, (dp, sibling))
+        to, n = (across, 0) if kind == "across" else (sibling, 1)
+        pair = (r.t_send.at[i, n], r.t_recv.at[i, sp])
+        return send(src, dst.at[rows_of(sp)], *pair, (dp, to))
+
+    def token_start(i):
+        src, dst = token_arrays[i]
+        token_copies(i, "across").start()
+        token_copies(i, "sibling").start()
         pltpu.make_async_copy(src, dst.at[rows_of(sp)], r.t_recv.at[i, sp]).start()
 
-    SMALLS, UP, DOWN, QKV, DENSE = range(5)
+    def token_wait(i, s):
+        src, dst = token_arrays[i]
+        pltpu.make_async_copy(src, dst.at[rows_of(s)], r.t_recv.at[i, s]).wait()
+
+    def token_pass(i):
+        token_wait(i, across)
+        token_copies(i, "pass").start()
+
+    def token_rest(i):
+        for s in (sp, sibling, sib_across):
+            token_wait(i, s)
+
+    token_start(0)
+
+    smalls, up_0, up_1, down_0, down_1, qkv_n, dense_n = range(7)
     gathered = (
-        (by_y, r.small_all), (by_y, r.up_all), (by_z, r.down_all), (by_z, r.qk_all),
-        (by_y, r.dense_all),
+        (by_y, r.small_all), (by_y, r.up_a), (by_z, r.up_b), (by_y, r.down_a), (by_z, r.down_b),
+        (by_z, r.qk_all), (by_y, r.dense_all),
     )
+    cut = PAGE // 2
 
     def stage_a(n):
         plane, out = gathered[n]
@@ -307,23 +321,29 @@
     r.small_all[y, z, x] = jnp.zeros((8, SMALL), F32)
     for s in range(N_SP):
         r.small_all[y, z, x, s : s + 1, :] = r.landed[s, 0:1, PAGE + QK :]
-    r.up_all[y, z, x] = r.tight[:, :PAGE].astype(BF)
+    r.up_a[y, z, x] = r.tight[:, :cut].astype(BF)
+    r.up_b[y, z, x] = r.tight[:, cut:PAGE].astype(BF)
     r.qk_all[y, z, x] = r.tight[:, PAGE : PAGE + QK].astype(BF)
-    start_a(SMALLS)
-    start_a(UP)
-    local_wait(r.down_all.at[y, z, x], r.r_recv.at[0])
-    start_a(DOWN)
+    start_a(smalls)
+    start_a(up_0)
+    start_a(up_1)
+    local_wait(r.down_in, r.r_recv.at[0])
+    r.down_a[y, z, x] = r.down_in[:, :cut]
+    r.down_b[y, z, x] = r.down_in[:, cut:]
+    start_a(down_0)
+    start_a(down_1)
+    token_start(1)
+    start_b(smalls)
+    start_b(up_0)
+    start_b(up_1)
+    token_pass(0)
+    start_b(down_0)
+    start_b(down_1)
     local_wait(r.dense_all.at[y, z, x], r.r_recv.at[1])
-    start_b(SMALLS)
-    start_b(UP)
-    start_b(DOWN)
-    token_wait(across)
-    for item in token_copies("pass"):
-        item.start()
-    start_a(QKV)
-    start_a(DENSE)
-
-    wait_b(SMALLS)
+    start_a(qkv_n)
+    start_a(dense_n)
+
+    wait_b(smalls)
     packed = r.small_all[...].reshape(2 * n_own, SMALL).astype(BF)
     n_rows = 2 * n_own
 
@@ -346,8 +366,7 @@
     def fold(values):
         return jnp.sum(values.reshape(-1, 8, values.shape[-1]), 0)
 
-    for s in (sp, sibling, sib_across):
-        token_wait(s)
+    token_rest(0)
 
     @pl.loop(0, steps)
     def _(i):
@@ -359,34 +378,46 @@
         r.n1_s[rows, :] = (xhat * gain_1 + shift_1).astype(BF)
         r.n2_s[rows, :] = (xhat * gain_2 + shift_2).astype(BF)
 
-    def join(src, dst):
+    def join(src, dst, lane=0):
         @pl.loop(0, NY * NZ)
         def _(i):
             a, b = i // NZ, lax.rem(i, NZ)
             pair = [src[a, b, e].astype(F32) for e in range(NX)]
-            own = pair[0].shape[0] * NX
-            dst[pl.ds(pl.multiple_of(i * own, own), own), :] = jnp.concatenate(pair, 0).astype(BF)
-
-    start_b(QKV)
-    start_b(DENSE)
-    wait_b(UP)
-    join(r.up_all, r.up_s)
-    wait_b(DOWN)
-    join(r.down_all, r.down_s)
+            own, wide_here = pair[0].shape[0] * NX, pair[0].shape[1]
+            here = (pl.ds(pl.multiple_of(i * own, own), own), pl.ds(lane, wide_here))
+            dst[here] = jnp.concatenate(pair, 0).astype(BF)
+
+    token_pass(1)
+    wait_b(up_0)
+    join(r.up_a, r.up_s)
+    wait_b(up_1)
+    join(r.up_b, r.up_s, cut)
 
     zeros = jnp.zeros((8, D), F32)
+
+    @pl.loop(0, steps)
+    def _(i):
+        rows = rows_at(i)
+        pre = dot(r.n2_s[rows, :], r.up_s[...]) + up_add
+        cdf = 0.5 * (1.0 + lax.erf(pre * 0.7071067811865476))
+        r.act_s[rows, :] = (pre * cdf).astype(BF)
+        pdf = jnp.exp(-0.5 * pre * pre) * 0.3989422804014327
+        r.sum_s[rows, :] = cdf + pre * pdf
+
+    start_b(qkv_n)
+    start_b(dense_n)
+    wait_b(down_0)
+    join(r.down_a, r.down_s)
+    wait_b(down_1)
+    join(r.down_b, r.down_s, cut)
+    token_rest(1)
 
     def first(i, sums):
         rows = rows_at(i)
-        g = r.g_all[rows, :]
-        pre = dot(r.n2_s[rows, :], r.up_s[...]) + up_add
-        cdf = 0.5 * (1.0 + lax.erf(pre * 0.7071067811865476))
-        act = (pre * cdf).astype(BF)
-        r.act_s[rows, :] = act
-        pdf = jnp.exp(-0.5 * pre * pre) * 0.3989422804014327
-        dpre = (dot_nt(g, r.down_s[...]) * (cdf + pre * pdf)).astype(BF)
+        dact = dot_nt(r.g_all[rows, :], r.down_s[...])
+        dpre = (dact * r.sum_s[rows, :]).astype(BF)
         r.dpre_s[rows, :] = dpre
-        r.sum_s[rows, :] = dot(act, r.down_s[...])
+        r.sum_s[rows, :] = dot(r.act_s[rows, :], r.down_s[...])
         dn2 = dot_nt(dpre, r.up_s[...])
         r.dx_s[rows, :] = dn2 * gain_2
         one, two, three = sums
@@ -411,6 +442,7 @@
                 at = (i * (NY // 2) + c // GROUP, c // NX % NZ, c % NX)
                 out[at[0], at[1], at[2]] = value[c * own : (c + 1) * own, :].astype(BF)
 
+    SMALLS, UP, DOWN, QKV, DENSE = range(5)
     reduced = (
         (by_y, r.small_g, r.small_1, r.small_m, r.small_2),
         (by_y, r.up_g, r.up_1, r.up_m, r.up_2),
@@ -474,9 +506,9 @@
     weight_grad(r.n2_s, r.dpre_s, r.up_g)
     start_1(UP)
 
-    wait_b(QKV)
+    wait_b(qkv_n)
     join(r.qk_all, r.qk_s)
-    wait_b(DENSE)
+    wait_b(dense_n)
     for e in range(NY * NZ * NX):
         r.dense_wide[e * PART : (e + 1) * PART, :] = r.dense_all[
             e // GROUP, e // NX % NZ, e % NX
@@ -727,9 +759,9 @@
     for i in range(2):
         pltpu.make_async_copy(*owned[i], r.j_recv.at[i]).wait()
 
-    for kind in ("across", "sibling", "pass"):
-        for item in token_copies(kind):
-            item.wait_send()
+    for i in range(2):
+        for kind in ("across", "sibling", "pass"):
+            token_copies(i, kind).wait_send()
 
     @pl.when(moves)
     def _():
@@ -746,8 +778,11 @@
     for i in range(2):
         for item in token_pair(i):
             item.wait_send()
-    for n in range(5):
-        for item in stage_a(n) + stage_b(n) + stage_1(n) + stage_2(n):
+    for n in range(len(gathered)):
+        for item in stage_a(n) + stage_b(n):
+            item.wait_send()
+    for n in range(len(reduced)):
+        for item in stage_1(n) + stage_2(n):
             item.wait_send()
 
 
@@ -782,7 +817,11 @@
     }
     scratch = {}
     for name, (shape, kind) in chunk.items():
-        scratch[name + "_all"] = (grid + shape, kind)
+        if name in ("up", "down"):
+            scratch[name + "_a"] = (grid + (own, PAGE // 2), kind)
+            scratch[name + "_b"] = (grid + (own, PAGE // 2), kind)
+        else:
+            scratch[name + "_all"] = (grid + shape, kind)
         scratch[name + "_g"] = (grid + shape, kind)
         scratch[name + "_1"] = (grid + shape, kind)
         scratch[name + "_m"] = ((GROUP // NX, NX) + shape, kind)
@@ -797,6 +836,7 @@
         up_s=((D, PAGE), BF),
         down_s=((PAGE, D), BF),
         qk_s=((D, QK), BF),
+        down_in=((own, D), BF),
         dense_wide=((width, D), F32),
         dense_s=((width, D), BF),
         vec_s=((8, PAGE), F32),
@@ -830,7 +870,7 @@
         small_l=((N_SP, 8, SMALL), F32),
     )
     semaphores = {
-        "r": (2,), "p": (N_SP,), "t": (2, N_SP), "a": (5, GROUP), "b": (5, NY), "e": (5, NY),
+        "r": (2,), "p": (N_SP,), "t": (2, N_SP), "a": (7, GROUP), "b": (7, NY), "e": (5, NY),
         "f": (5, GROUP), "g": (2, 2), "h": (2,), "i": (2, N_SP), "j": (2,), "k": (N_SP,),
     }
     names = list(ins) + list(outs) + list(scratch)
@@ -854,6 +894,31 @@
     )(x, g, up, qkv, small, down, dense, cosine, sine)
 
 
+def outputs_kernel(*refs):
+    n = 6
+    small_ref, outs = refs[n], refs[n + 1 :]
+    for i in range(n):
+        outs[i][...] = refs[i][...]
+    mine = small_ref[pl.ds(lax.axis_index("sp"), 1), :]
+    for (start, each, _, _), out in zip(VECTORS_OUT + VECTORS_OUT[5:6], outs[n:]):
+        out[...] = mine[:, start : start + each]
+
+
+def write_outputs(*arrays):
+    vmem = pl.BlockSpec(memory_space=pltpu.VMEM)
+    large = [jax.ShapeDtypeStruct(item.shape, item.dtype) for item in arrays[:-1]]
+    small = [
+        jax.ShapeDtypeStruct((1, each), F32) for _, each, _, _ in VECTORS_OUT + VECTORS_OUT[5:6]
+    ]
+    return pl.pallas_call(
+        outputs_kernel,
+        out_shape=tuple(large + small),
+        in_specs=[vmem] * len(arrays),
+        out_specs=(vmem,) * (len(large) + len(small)),
+        name="outputs",
+    )(*arrays)
+
+
 def local(
     hidden_in,
     cotangent,
@@ -870,7 +935,6 @@
     down_weight,
     down_bias,
 ):
-    sp = lax.axis_index("sp")
     small = (
         attn_gain,
         attn_shift,
@@ -887,7 +951,7 @@
         size = item.shape[0]
         packed = packed + jnp.pad(item.astype(F32), (at, SMALL - at - size))
         at += size
-    hidden_out, hidden_grad, up_own, qkv_own, down_own, dense_own, packed = layer(
+    results = layer(
         hidden_in,
         cotangent,
         up_weight,
@@ -896,8 +960,9 @@
         down_weight,
         dense_weight,
     )
-    mine = lax.dynamic_slice_in_dim(packed, sp, 1, 0).reshape(-1)
-    parts = [mine[start : start + each] for start, each, _, _ in VECTORS_OUT]
+    results = write_outputs(*results)
+    hidden_out, hidden_grad, up_own, qkv_own, down_own, dense_own = results[:6]
+    parts = [item.reshape(-1) for item in results[6:]]
     return (
         hidden_out,
         hidden_grad,
@@ -912,7 +977,7 @@
         up_own,
         parts[6],
         down_own,
-        parts[5],
+        parts[7],
     )
 
 

time: 142 us -> 126 us (0.89)
  local copies, waits for them, and re-layouts: 9.81 us -> 0 us
  Pallas kernels: 131 us -> 124 us
    pallas_call x1, Pallas kernels: 131 us -> 122 us  [layer(): pl.pallas_call(functools.partial(layer_kernel, names), out_shape=tuple((j...]
    unnamed x35 -> x0, local copies, waits for them, and re-layouts: 7.37 us -> none
    pallas_call x0 -> x1, Pallas kernels: none -> 2.23 us  [write_outputs(): pl.pallas_call(outputs_kernel, out_shape=tuple(large + small), in_specs=[...]
    slice x3 -> x0, local copies, waits for them, and re-layouts: 1.76 us -> none  [local(): parts = [mine[start:start + each] for start, each, _, _ in VECTORS_OUT]]
where the time goes in v6:
time: 126 us
  Pallas kernels  124 us (98%)
  other arithmetic  1.36 us (1%)
    pallas_call x1, Pallas kernels, layer(): pl.pallas_call(functools.partial(layer_kernel, names), out_shape=tuple((j...  122 us

profile of v6, /device:TPU:1, one launch (start us, length us, event | category | flops | bytes accessed | tf_op | source)
XLA Modules:
  0.0 126.3 jit_solution(9203449894120739079)
XLA Ops:
  0.6 1.4 %add_bitcast_fusion.refs_4_ = f32[1,128]{1,0:T(1,128)} fusion(bf16[6]{0:T(256)(128)(2,1)} %param.29, bf16[24]{0:T(256)(128)(2,1)} %param.27, bf16[6]{0:T(256)(128)(2,1)} %param.25, bf16[18]{0:T(256)(128)(2,1)} %param.23, bf16[6]{0:T(256)(128)(2,1)} %param.21, bf16[6]{0:T(256)(128)(2,1)} %param.20, bf16[6]{0:T(256)(128)(2,1)} %param.19, bf16[6]{0:T(256)(128)(2,1)} %param.18), kind=kLoop, calls=%fused_computation | loop fusion | flops 1920 | bytes 668 | tf_op jit(solution)/shard_map/reshape | solution.py:959
  2.0 121.9 %layer.1 = (bf16[256,768]{1,0:T(8,128)(2,1)}, bf16[256,768]{1,0:T(8,128)(2,1)}, f32[6,3072]{1,0:T(8,128)}, f32[6,2304]{1,0:T(8,128)}, f32[24,768]{1,0:T(8,128)}, /*index=5*/f32[6,768]{1,0:T(8,128)}, f32[8,128]{1,0:T(8,128)}) custom-call(bf16[256,768]{1,0:T(8,128)(2,1)} %refs_0_.1, bf16[256,768]{1,0:T(8,128)(2,1)} %refs_1_.1, bf16[6,3072]{1,0:T(8,128)(2,1)} %refs_2_.1, ...), custom_call_target="tpu_custom_call" | custom-call | flops 14000000000 | bytes 16000000 | tf_op jit(solution)/shard_map/layer/pallas_call | solution.py:881
  123.9 2.2 %outputs.1 = (bf16[256,768]{1,0:T(8,128)(2,1)}, bf16[256,768]{1,0:T(8,128)(2,1)}, f32[6,3072]{1,0:T(8,128)}, f32[6,2304]{1,0:T(8,128)}, f32[24,768]{1,0:T(8,128)...) custom-call(bf16[256,768]{1,0:T(8,128)(2,1)} %get-tuple-element.35.r, ...), custom_call_target="tpu_custom_call" | custom-call | tf_op jit(solution)/shard_map/outputs/pallas_call | solution.py:913

commit v7 on v6

--- a/solution.py
+++ b/solution.py
@@ -66,19 +66,20 @@
     return jnp.logical_or(device[0] != dp, device[1] != sp)
 
 
-class Plane:
+def other_half(dp):
+    return dp + 1 - 2 * lax.rem(dp, NX)
+
+
+class Path:
     def __init__(self, last):
         self.last = last
-        dp, sp, y, z, x = place()
-        self.sp, self.y, self.z, self.x = sp, y, z, x
-        self.mine = (z if last == "y" else y) * NX + x
-        self.axis = y if last == "y" else z
-
-    def member(self, k):
-        e = lax.rem(self.mine + k, GROUP)
-        a, x = e // NX, lax.rem(e, NX)
+        dp, self.sp, self.y, self.z, self.x = place()
+        self.first, self.axis = (self.z, self.y) if last == "y" else (self.y, self.z)
+
+    def along_first(self, k):
+        a = lax.rem(self.first + k, NY)
         y, z = (self.y, a) if self.last == "y" else (a, self.z)
-        return (index_of(y, z, x), self.sp), e, a, x
+        return (index_of(y, z, self.x), self.sp), a
 
     def along(self, k):
         a = lax.rem(self.axis + k, NY)
@@ -88,36 +89,38 @@
     def block(self, ref, a):
         return ref.at[a] if self.last == "y" else ref.at[:, a]
 
-    def chunk(self, ref, e):
-        a, x = e // NX, lax.rem(e, NX)
-        return ref.at[self.y, a, x] if self.last == "y" else ref.at[a, self.z, x]
-
-
-def greet(*partners):
+    def pair(self, ref, a):
+        return ref.at[self.y, a] if self.last == "y" else ref.at[a, self.z]
+
+
+def greet(partners):
     dp, sp, y, z, x = place()
     barrier = pltpu.get_barrier_semaphore()
 
     def signal(device):
         pl.semaphore_signal(barrier, inc=1, device_id=device, device_id_type=MESH)
 
-    for k in range(1, N_SP):
-        signal((dp, lax.rem(sp + k, N_SP)))
-    by_y, by_z = Plane("y"), Plane("z")
-    for k in range(1, GROUP):
-        signal(by_y.member(k)[0])
-        signal(by_z.member(k)[0])
-
-    @pl.when(differs(partners[0], dp, sp))
-    def _():
-        for partner in partners:
+    for k in range(N_SP):
+        if k:
+            signal((dp, lax.rem(sp + k, N_SP)))
+        signal((other_half(dp), lax.rem(sp + k, N_SP)))
+    by_y, by_z = Path("y"), Path("z")
+    for k in range(1, NY):
+        signal(by_y.along(k)[0])
+        signal(by_z.along(k)[0])
+    for partner in partners:
+
+        @pl.when(differs(partner, dp, sp))
+        def _():
             signal(partner)
 
 
-def await_greetings(*partners):
+def await_greetings(partners):
     dp, sp, y, z, x = place()
-    count = N_SP - 1 + 2 * (GROUP - 1)
-    more = jnp.where(differs(partners[0], dp, sp), len(partners), 0)
-    pl.semaphore_wait(pltpu.get_barrier_semaphore(), count + more)
+    count = 2 * N_SP - 1 + 2 * (NY - 1)
+    for partner in partners:
+        count = count + jnp.where(differs(partner, dp, sp), 1, 0)
+    pl.semaphore_wait(pltpu.get_barrier_semaphore(), count)
 
 
 BLOCK = 256
@@ -175,21 +178,35 @@
 def layer_kernel(names, *refs):
     r = types.SimpleNamespace(**dict(zip(names, refs)))
     dp, sp, y, z, x = place()
-    to_slot, to_owner = slot_device(dp, sp), owner_device(dp, sp)
+    half_dp = (dp, other_half(dp))
+    half_x = (x, 1 - x)
+    slot, column = slot_device(dp, sp)
+    to_slots = ((slot, column), (other_half(slot), column))
+    to_owners = tuple(owner_device(d, sp) for d in half_dp)
+    slot_x = lax.rem(slot, NX)
     sibling = sp + 1 - 2 * lax.rem(sp, 2)
     across = lax.rem(sp + 2, N_SP)
     sib_across = lax.rem(sibling + 2, N_SP)
-    moves = differs(to_slot, dp, sp)
-    stays = jnp.logical_not(moves)
-    by_y, by_z = Plane("y"), Plane("z")
+    others = [(q, k) for q in range(NX) for k in range(N_SP) if q or k]
+    by_y, by_z = Path("y"), Path("z")
     length = r.x_all.shape[0]
     tokens = length // N_SP
     heads = HEADS // N_SP
     width = heads * HEAD_DIM
     n_own = NY * NZ * NX * N_SP
     steps = length // BLOCK
-    slot = to_slot[0]
-    slot_at = (slot // GROUP, lax.rem(slot // NX, NZ), lax.rem(slot, NX))
+    slot_at = (slot // GROUP, lax.rem(slot // NX, NZ), slot_x)
+
+    def to_partner(device, copy, src, dst, recv, run):
+        @pl.when(differs(device, dp, sp))
+        def _():
+            getattr(copy, run)()
+
+        if run == "start":
+
+            @pl.when(jnp.logical_not(differs(device, dp, sp)))
+            def _():
+                pltpu.make_async_copy(src, dst, recv).start()
 
     def local_wait(ref, sem):
         pltpu.make_async_copy(ref, ref, sem).wait()
@@ -200,46 +217,37 @@
     def rows_at(i):
         return pl.ds(pl.multiple_of(i * BLOCK, BLOCK), BLOCK)
 
-    greet(to_slot, to_owner)
-
-    end = PAGE + 3 * width
+    greet(to_slots + to_owners)
+
     wide = r.qkv_ref[...].astype(F32)
+    fill = jnp.zeros((PART, QK - 3 * width), F32)
+    small = jnp.concatenate([r.small_ref[...], jnp.zeros((PART - 1, SMALL), F32)], 0)
     for t in range(N_SP):
-        r.pieces[t, :, :PAGE] = r.up_ref[:, t * PAGE : (t + 1) * PAGE].astype(F32)
-        for j in range(3):
-            at = j * D + t * width
-            r.pieces[t, :, PAGE + j * width : PAGE + (j + 1) * width] = wide[:, at : at + width]
-        r.pieces[t, :, end : PAGE + QK] = jnp.zeros((PART, PAGE + QK - end), F32)
-        r.pieces[t, 0:1, PAGE + QK :] = r.small_ref[...]
-        r.pieces[t, 1:, PAGE + QK :] = jnp.zeros((PART - 1, SMALL), F32)
-
-    await_greetings(to_slot, to_owner)
-
-    def piece(k):
+        parts = [r.up_ref[:, t * PAGE : (t + 1) * PAGE].astype(F32)]
+        parts += [wide[:, j * D + t * width : j * D + (t + 1) * width] for j in range(3)]
+        r.pieces[t] = jnp.concatenate(parts + [fill, small], 1).astype(BF)
+
+    await_greetings(to_slots + to_owners)
+
+    def piece(q, k):
         t = lax.rem(sp + k, N_SP)
-        return send(r.pieces.at[t], r.landed.at[sp], r.p_send.at[k], r.p_recv.at[sp], (dp, t))
-
-    for k in range(1, N_SP):
-        piece(k).start()
-    pltpu.make_async_copy(r.pieces.at[sp], r.landed.at[sp], r.p_recv.at[sp]).start()
-
-    def row_copies():
-        return [
-            send(r.down_ref, r.down_in, r.r_send.at[0], r.r_recv.at[0], to_slot),
-            send(
-                r.dense_ref, r.dense_all.at[slot_at], r.r_send.at[1], r.r_recv.at[1], to_slot
-            ),
-        ]
-
-    @pl.when(moves)
-    def _():
-        for item in row_copies():
-            item.start()
-
-    @pl.when(stays)
-    def _():
-        pltpu.make_async_copy(r.down_ref, r.down_in, r.r_recv.at[0]).start()
-        pltpu.make_async_copy(r.dense_ref, r.dense_all.at[y, z, x], r.r_recv.at[1]).start()
+        pair = (r.p_send.at[q, k], r.p_recv.at[x, sp])
+        return send(r.pieces.at[t], r.landed.at[x, sp], *pair, (half_dp[q], t))
+
+    for q, k in others:
+        piece(q, k).start()
+    pltpu.make_async_copy(r.pieces.at[sp], r.landed.at[x, sp], r.p_recv.at[x, sp]).start()
+
+    def row_copies(run):
+        for i, (src, dst) in enumerate(
+            ((r.down_ref, r.down_in.at[slot_x]), (r.dense_ref, r.dense_all.at[slot_at]))
+        ):
+            recv = r.r_recv.at[i, slot_x]
+            for q, device in enumerate(to_slots):
+                copy = send(src, dst, r.r_send.at[i, q], recv, device)
+                to_partner(device, copy, src, dst, recv, run)
+
+    row_copies("start")
 
     token_arrays = ((r.x_ref, r.x_all), (r.g_ref, r.g_all))
 
@@ -281,11 +289,11 @@
     cut = PAGE // 2
 
     def stage_a(n):
-        plane, out = gathered[n]
-        mine = out.at[y, z, x]
+        path, out = gathered[n]
+        mine = path.pair(out, path.first)
         return [
-            send(mine, mine, r.a_send.at[n, k], r.a_recv.at[n, plane.mine], plane.member(k)[0])
-            for k in range(1, GROUP)
+            send(mine, mine, r.a_send.at[n, k], r.a_recv.at[n, path.first], path.along_first(k)[0])
+            for k in range(1, NY)
         ]
 
     def stage_b(n):
@@ -302,9 +310,9 @@
 
     def start_b(n):
         plane, out = gathered[n]
-        for k in range(1, GROUP):
-            e = lax.rem(plane.mine + k, GROUP)
-            local_wait(plane.chunk(out, e), r.a_recv.at[n, e])
+        for k in range(1, NY):
+            a = plane.along_first(k)[1]
+            local_wait(plane.pair(out, a), r.a_recv.at[n, a])
         for item in stage_b(n):
             item.start()
 
@@ -314,22 +322,25 @@
             a = plane.along(k)[1]
             local_wait(plane.block(out, a), r.b_recv.at[n, a])
 
-    for s in range(N_SP):
-        local_wait(r.landed.at[s], r.p_recv.at[s])
-    for s in range(N_SP):
-        r.tight[s * PART : (s + 1) * PART, :] = r.landed[s]
-    r.small_all[y, z, x] = jnp.zeros((8, SMALL), F32)
-    for s in range(N_SP):
-        r.small_all[y, z, x, s : s + 1, :] = r.landed[s, 0:1, PAGE + QK :]
-    r.up_a[y, z, x] = r.tight[:, :cut].astype(BF)
-    r.up_b[y, z, x] = r.tight[:, cut:PAGE].astype(BF)
-    r.qk_all[y, z, x] = r.tight[:, PAGE : PAGE + QK].astype(BF)
+    for xx in range(NX):
+        for s in range(N_SP):
+            local_wait(r.landed.at[xx, s], r.p_recv.at[xx, s])
+    for xx in range(NX):
+        r.small_all[y, z, xx] = jnp.zeros((8, SMALL), F32)
+        for s in range(N_SP):
+            own = r.landed[xx, s].astype(F32)
+            r.tight[s * PART : (s + 1) * PART, :] = own
+            r.small_all[y, z, xx, s : s + 1, :] = own[0:1, PAGE + QK :]
+        r.up_a[y, z, xx] = r.tight[:, :cut].astype(BF)
+        r.up_b[y, z, xx] = r.tight[:, cut:PAGE].astype(BF)
+        r.qk_all[y, z, xx] = r.tight[:, PAGE : PAGE + QK].astype(BF)
     start_a(smalls)
     start_a(up_0)
     start_a(up_1)
-    local_wait(r.down_in, r.r_recv.at[0])
-    r.down_a[y, z, x] = r.down_in[:, :cut]
-    r.down_b[y, z, x] = r.down_in[:, cut:]
+    for xx in range(NX):
+        local_wait(r.down_in.at[xx], r.r_recv.at[0, xx])
+        r.down_a[y, z, xx] = r.down_in[xx, :, :cut]
+        r.down_b[y, z, xx] = r.down_in[xx, :, cut:]
     start_a(down_0)
     start_a(down_1)
     token_start(1)
@@ -339,7 +350,8 @@
     token_pass(0)
     start_b(down_0)
     start_b(down_1)
-    local_wait(r.dense_all.at[y, z, x], r.r_recv.at[1])
+    for xx in range(NX):
+        local_wait(r.dense_all.at[y, z, xx], r.r_recv.at[1, xx])
     start_a(qkv_n)
     start_a(dense_n)
 
@@ -461,12 +473,12 @@
         return made
 
     def stage_2(n):
-        plane, _, _, mid, land = reduced[n]
+        path, _, _, mid, land = reduced[n]
         made = []
-        for k in range(1, GROUP):
-            device, e, a, xx = plane.member(k)
-            pair = (r.f_send.at[n, k], r.f_recv.at[n, plane.mine])
-            made.append(send(mid.at[a, xx], land.at[plane.mine], *pair, device))
+        for k in range(1, NY):
+            device, a = path.along_first(k)
+            pair = (r.f_send.at[n, k], r.f_recv.at[n, path.first])
+            made.append(send(mid.at[a], land.at[path.first], *pair, device))
         return made
 
     def start_1(n):
@@ -492,14 +504,17 @@
             item.start()
 
     def finish(n):
-        plane, _, _, mid, land = reduced[n]
-        for k in range(1, GROUP):
-            e = lax.rem(plane.mine + k, GROUP)
-            local_wait(land.at[e], r.f_recv.at[n, e])
-        total = mid[plane.mine // NX, lax.rem(plane.mine, NX)].astype(F32)
-        for k in range(1, GROUP):
-            total = total + land[lax.rem(plane.mine + k, GROUP)].astype(F32)
-        return total
+        path, _, _, mid, land = reduced[n]
+        for k in range(1, NY):
+            a = path.along_first(k)[1]
+            local_wait(land.at[a], r.f_recv.at[n, a])
+        totals = []
+        for xx in half_x:
+            total = mid[path.first, xx].astype(F32)
+            for k in range(1, NY):
+                total = total + land[path.along_first(k)[1], xx].astype(F32)
+            totals.append(total)
+        return totals
 
     weight_grad(r.act_s, r.g_all, r.down_g)
     start_1(DOWN)
@@ -676,53 +691,46 @@
     token_cross(1)
     start_2(QKV)
 
-    up_total = finish(UP)
-    for t in range(N_SP):
-        r.up_p[t] = up_total[t * PART : (t + 1) * PART, :]
-
-    def back(n, k):
-        src, land = ((r.up_p, r.up_l), (r.qk_p, r.qk_l))[n]
+    def store_pieces(totals, out):
+        for q, total in enumerate(totals):
+            for t in range(N_SP):
+                out[q, t] = total[t * PART : (t + 1) * PART, :]
+
+    def back(n, q, k):
+        src, land = ((r.up_p, r.up_l), (r.qk_p, r.qk_l), (r.small_t, r.small_l))[n]
         t = lax.rem(sp + k, N_SP)
-        return send(src.at[t], land.at[sp], r.i_send.at[n, k], r.i_recv.at[n, sp], (dp, t))
-
-    for k in range(1, N_SP):
-        back(0, k).start()
-    owned = ((r.down_t, r.down_out), (r.dense_t, r.dense_out))
-
-    def own_copy(i):
+        pair = (r.i_send.at[n, q, k], r.i_recv.at[n, x, sp])
+        here = src.at[q] if n == 2 else src.at[q, t]
+        return send(here, land.at[x, sp], *pair, (half_dp[q], t))
+
+    def start_back(n):
+        for q, k in others:
+            back(n, q, k).start()
+
+    store_pieces(finish(UP), r.up_p)
+    start_back(0)
+    owned = ((r.down_t, r.down_l), (r.dense_t, r.dense_l))
+
+    def own_copies(i, run):
         src, dst = owned[i]
-        return send(src, dst, r.j_send.at[i], r.j_recv.at[i], to_owner)
-
-    def start_own(i):
-        @pl.when(moves)
-        def _():
-            own_copy(i).start()
-
-        @pl.when(stays)
-        def _():
-            pltpu.make_async_copy(*owned[i], r.j_recv.at[i]).start()
-
-    r.down_t[...] = finish(DOWN)
-    start_own(0)
+        recv = r.j_recv.at[i, x]
+        for q, device in enumerate(to_owners):
+            copy = send(src.at[q], dst.at[x], r.j_send.at[i, q], recv, device)
+            to_partner(device, copy, src.at[q], dst.at[x], recv, run)
+
+    for q, total in enumerate(finish(DOWN)):
+        r.down_t[q] = total
+    own_copies(0, "start")
     start_2(DENSE)
     start_2(SMALLS)
-    qk_total = finish(QKV)
-    for t in range(N_SP):
-        r.qk_p[t] = qk_total[t * PART : (t + 1) * PART, :]
-    for k in range(1, N_SP):
-        back(1, k).start()
-    r.dense_t[...] = finish(DENSE)
-    start_own(1)
-    r.small_l[sp] = finish(SMALLS)
-
-    def small_copy(k):
-        there = r.small_l.at[sp]
-        return send(
-            there, there, r.k_send.at[k], r.k_recv.at[sp], (dp, lax.rem(sp + k, N_SP))
-        )
-
-    for k in range(1, N_SP):
-        small_copy(k).start()
+    store_pieces(finish(QKV), r.qk_p)
+    start_back(1)
+    for q, total in enumerate(finish(DENSE)):
+        r.dense_t[q] = total
+    own_copies(1, "start")
+    for q, total in enumerate(finish(SMALLS)):
+        r.small_t[q] = total
+    start_back(2)
 
     x_here = r.x_all[rows_of(sp), :].astype(F32)
     r.hidden_out[...] = (x_here + token_total(0) + bias).astype(BF)
@@ -740,41 +748,43 @@
         )
     ).astype(BF)
 
-    r.up_l[sp] = r.up_p[sp]
-    r.qk_l[sp] = r.qk_p[sp]
-    for n, land in enumerate((r.up_l, r.qk_l)):
-        for k in range(1, N_SP):
+    r.up_l[x, sp] = r.up_p[0, sp]
+    r.qk_l[x, sp] = r.qk_p[0, sp]
+    r.small_l[x, sp] = r.small_t[0]
+
+    def wait_back(n, land):
+        for q, k in others:
             s = lax.rem(sp + k, N_SP)
-            local_wait(land.at[s], r.i_recv.at[n, s])
+            local_wait(land.at[half_x[q], s], r.i_recv.at[n, half_x[q], s])
+
+    wait_back(0, r.up_l)
     for s in range(N_SP):
-        r.up_out[:, s * PAGE : (s + 1) * PAGE] = r.up_l[s]
-        block = r.qk_l[s]
+        r.up_out[:, s * PAGE : (s + 1) * PAGE] = r.up_l[0, s] + r.up_l[1, s]
+    for i, out in enumerate((r.down_out, r.dense_out)):
+        land = owned[i][1]
+        for xx in range(NX):
+            local_wait(land.at[xx], r.j_recv.at[i, xx])
+        out[...] = land[0] + land[1]
+    wait_back(1, r.qk_l)
+    for s in range(N_SP):
+        block = r.qk_l[0, s] + r.qk_l[1, s]
         for j in range(3):
             to = j * D + s * width
             r.qkv_out[:, to : to + width] = block[:, j * width : (j + 1) * width]
-    for k in range(1, N_SP):
-        s = lax.rem(sp + k, N_SP)
-        local_wait(r.small_l.at[s], r.k_recv.at[s])
-    r.small_out[...] = jnp.sum(r.small_l[...], 0)
-    for i in range(2):
-        pltpu.make_async_copy(*owned[i], r.j_recv.at[i]).wait()
+    wait_back(2, r.small_l)
+    r.small_out[...] = jnp.sum(jnp.sum(r.small_l[...], 0), 0)
 
     for i in range(2):
         for kind in ("across", "sibling", "pass"):
             token_copies(i, kind).wait_send()
 
-    @pl.when(moves)
-    def _():
-        for item in row_copies():
-            item.wait_send()
-        for i in range(2):
-            own_copy(i).wait_send()
-
-    for k in range(1, N_SP):
-        piece(k).wait_send()
-        back(0, k).wait_send()
-        back(1, k).wait_send()
-        small_copy(k).wait_send()
+    row_copies("wait_send")
+    for i in range(2):
+        own_copies(i, "wait_send")
+    for q, k in others:
+        piece(q, k).wait_send()
+        for n in range(3):
+            back(n, q, k).wait_send()
     for i in range(2):
         for item in token_pair(i):
             item.wait_send()
@@ -825,18 +835,18 @@
         scratch[name + "_g"] = (grid + shape, kind)
         scratch[name + "_1"] = (grid + shape, kind)
         scratch[name + "_m"] = ((GROUP // NX, NX) + shape, kind)
-        scratch[name + "_2"] = ((GROUP,) + shape, kind)
+        scratch[name + "_2"] = ((GROUP // NX, NX) + shape, kind)
     per_head = (heads, length, HEAD_DIM)
     scratch.update(
         x_all=((length, D), BF),
         g_all=((length, D), BF),
-        pieces=((N_SP, PART, PAGE + QK + SMALL), F32),
-        landed=((N_SP, PART, PAGE + QK + SMALL), F32),
+        pieces=((N_SP, PART, PAGE + QK + SMALL), BF),
+        landed=((NX, N_SP, PART, PAGE + QK + SMALL), BF),
         tight=((own, PAGE + QK + SMALL), F32),
         up_s=((D, PAGE), BF),
         down_s=((PAGE, D), BF),
         qk_s=((D, QK), BF),
-        down_in=((own, D), BF),
+        down_in=((NX, own, D), BF),
         dense_wide=((width, D), F32),
         dense_s=((width, D), BF),
         vec_s=((8, PAGE), F32),
@@ -861,23 +871,28 @@
         token_in=((2, 2, tokens, D), BF),
         token_mid=((2, tokens, D), BF),
         token_far=((2, tokens, D), BF),
-        up_p=((N_SP, PART, PAGE), F32),
-        up_l=((N_SP, PART, PAGE), F32),
-        qk_p=((N_SP, PART, QK), F32),
-        qk_l=((N_SP, PART, QK), F32),
-        down_t=((own, D), F32),
-        dense_t=((PART, D), F32),
-        small_l=((N_SP, 8, SMALL), F32),
+        up_p=((NX, N_SP, PART, PAGE), F32),
+        up_l=((NX, N_SP, PART, PAGE), F32),
+        qk_p=((NX, N_SP, PART, QK), F32),
+        qk_l=((NX, N_SP, PART, QK), F32),
+        down_t=((NX, own, D), F32),
+        down_l=((NX, own, D), F32),
+        dense_t=((NX, PART, D), F32),
+        dense_l=((NX, PART, D), F32),
+        small_t=((NX, 8, SMALL), F32),
+        small_l=((NX, N_SP, 8, SMALL), F32),
     )
     semaphores = {
-        "r": (2,), "p": (N_SP,), "t": (2, N_SP), "a": (7, GROUP), "b": (7, NY), "e": (5, NY),
-        "f": (5, GROUP), "g": (2, 2), "h": (2,), "i": (2, N_SP), "j": (2,), "k": (N_SP,),
+        "r": (2, NX), "p": (NX, N_SP), "t": (2, N_SP), "a": (7, NY), "b": (7, NY), "e": (5, NY),
+        "f": (5, NY), "g": (2, 2), "h": (2,), "j": (2, NX),
     }
     names = list(ins) + list(outs) + list(scratch)
     shapes = [pltpu.VMEM(shape, kind) for shape, kind in scratch.values()]
     for name, shape in semaphores.items():
         names += [name + "_send", name + "_recv"]
         shapes += [dma(shape), dma(shape)]
+    names += ["i_send", "i_recv"]
+    shapes += [dma((3, NX, N_SP)), dma((3, NX, N_SP))]
     return pl.pallas_call(
         functools.partial(layer_kernel, names),
         out_shape=tuple(jax.ShapeDtypeStruct(*item) for item in outs.values()),

time: 126 us -> 117 us (0.929)
  Pallas kernels: 124 us -> 114 us
    pallas_call x1, Pallas kernels: 122 us -> 112 us  [layer(): pl.pallas_call(functools.partial(layer_kernel, names), out_shape=tuple((j...]
where the time goes in v7:
time: 117 us; the launch traced here: 116 us
  Pallas kernels  114 us (97%)
  other arithmetic  1.36 us (1%)
    pallas_call x1, Pallas kernels, layer(): pl.pallas_call(functools.partial(layer_kernel, names), out_shape=tuple((j...  112 us

profile of v7, /device:TPU:1, one launch (start us, length us, event | category | flops | bytes accessed | tf_op | source)
XLA Modules:
  0.0 116.4 jit_solution(930790093434805125)
XLA Ops:
  0.6 1.4 %add_bitcast_fusion.refs_4_ = f32[1,128]{1,0:T(1,128)} fusion(bf16[6]{0:T(256)(128)(2,1)} %param.29, bf16[24]{0:T(256)(128)(2,1)} %param.27, bf16[6]{0:T(256)(128)(2,1)} %param.25, bf16[18]{0:T(256)(128)(2,1)} %param.23, bf16[6]{0:T(256)(128)(2,1)} %param.21, bf16[6]{0:T(256)(128)(2,1)} %param.20, bf16[6]{0:T(256)(128)(2,1)} %param.19, bf16[6]{0:T(256)(128)(2,1)} %param.18), kind=kLoop, calls=%fused_computation | loop fusion | flops 1920 | bytes 668 | tf_op jit(solution)/shard_map/reshape | solution.py:974
  2.0 112.0 %layer.1 = (bf16[256,768]{1,0:T(8,128)(2,1)}, bf16[256,768]{1,0:T(8,128)(2,1)}, f32[6,3072]{1,0:T(8,128)}, f32[6,2304]{1,0:T(8,128)}, f32[24,768]{1,0:T(8,128)}, /*index=5*/f32[6,768]{1,0:T(8,128)}, f32[8,128]{1,0:T(8,128)}) custom-call(bf16[256,768]{1,0:T(8,128)(2,1)} %refs_0_.1, bf16[256,768]{1,0:T(8,128)(2,1)} %refs_1_.1, bf16[6,3072]{1,0:T(8,128)(2,1)} %refs_2_.1, ...), custom_call_target="tpu_custom_call" | custom-call | flops 14000000000 | bytes 16000000 | tf_op jit(solution)/shard_map/layer/pallas_call | solution.py:896
  114.0 2.2 %outputs.1 = (bf16[256,768]{1,0:T(8,128)(2,1)}, bf16[256,768]{1,0:T(8,128)(2,1)}, f32[6,3072]{1,0:T(8,128)}, f32[6,2304]{1,0:T(8,128)}, f32[24,768]{1,0:T(8,128)...) custom-call(bf16[256,768]{1,0:T(8,128)(2,1)} %get-tuple-element.35.r, ...), custom_call_target="tpu_custom_call" | custom-call | tf_op jit(solution)/shard_map/outputs/pallas_call | solution.py:928

commit v8 on v7

--- a/solution.py
+++ b/solution.py
@@ -297,12 +297,30 @@
         ]
 
     def stage_b(n):
-        plane, out = gathered[n]
-        there = plane.block(out, plane.axis)
+        path, out = gathered[n]
+        there = path.block(out, path.axis)
         return [
-            send(there, there, r.b_send.at[n, k], r.b_recv.at[n, plane.axis], plane.along(k)[0])
-            for k in range(1, NY)
+            send(there, there, r.b_send.at[n, k], r.b_recv.at[n, path.axis], path.along(k)[0])
+            for k in ((1, 2, 3) if n == smalls else (1, 3))
         ]
+
+    def half_block(n, a, part):
+        path, out = gathered[n]
+        some = pl.ds(part * (NZ // 2), NZ // 2)
+        return out.at[a, some] if path.last == "y" else out.at[some, a]
+
+    def passed_on(n, part):
+        path = gathered[n][0]
+        there = half_block(n, path.along((3, 1)[part])[1], part)
+        pair = (r.q_send.at[n, part], r.q_recv.at[n, part])
+        return send(there, there, *pair, path.along((1, 3)[part])[0])
+
+    def start_on(n):
+        path, out = gathered[n]
+        for part in range(2):
+            a = path.along((3, 1)[part])[1]
+            local_wait(path.block(out, a), r.b_recv.at[n, a])
+            passed_on(n, part).start()
 
     def start_a(n):
         for item in stage_a(n):
@@ -317,10 +335,14 @@
             item.start()
 
     def wait_b(n):
-        plane, out = gathered[n]
-        for k in range(1, NY):
-            a = plane.along(k)[1]
-            local_wait(plane.block(out, a), r.b_recv.at[n, a])
+        path, out = gathered[n]
+        if n == smalls:
+            for k in range(1, NY):
+                a = path.along(k)[1]
+                local_wait(path.block(out, a), r.b_recv.at[n, a])
+        else:
+            for part in range(2):
+                local_wait(half_block(n, path.along(2)[1], part), r.q_recv.at[n, part])
 
     for xx in range(NX):
         for s in range(N_SP):
@@ -350,6 +372,8 @@
     token_pass(0)
     start_b(down_0)
     start_b(down_1)
+    start_on(up_0)
+    start_on(up_1)
     for xx in range(NX):
         local_wait(r.dense_all.at[y, z, xx], r.r_recv.at[1, xx])
     start_a(qkv_n)
@@ -399,6 +423,8 @@
             here = (pl.ds(pl.multiple_of(i * own, own), own), pl.ds(lane, wide_here))
             dst[here] = jnp.concatenate(pair, 0).astype(BF)
 
+    start_on(down_0)
+    start_on(down_1)
     token_pass(1)
     wait_b(up_0)
     join(r.up_a, r.up_s)
@@ -440,6 +466,8 @@
         )
 
     up_bias, gain_2_grad, shift_2_grad = lax.fori_loop(0, steps, first, (zeros,) * 3)
+    start_on(qkv_n)
+    start_on(dense_n)
 
     half = D // 2
     in_half = half // (PART * N_SP)
@@ -791,6 +819,9 @@
     for n in range(len(gathered)):
         for item in stage_a(n) + stage_b(n):
             item.wait_send()
+        if n != smalls:
+            for part in range(2):
+                passed_on(n, part).wait_send()
     for n in range(len(reduced)):
         for item in stage_1(n) + stage_2(n):
             item.wait_send()
@@ -883,7 +914,7 @@
         small_l=((NX, N_SP, 8, SMALL), F32),
     )
     semaphores = {
-        "r": (2, NX), "p": (NX, N_SP), "t": (2, N_SP), "a": (7, NY), "b": (7, NY), "e": (5, NY),
+        "r": (2, NX), "p": (NX, N_SP), "t": (2, N_SP), "a": (7, NY), "b": (7, NY), "q": (7, 2), "e": (5, NY),
         "f": (5, NY), "g": (2, 2), "h": (2,), "j": (2, NX),
     }
     names = list(ins) + list(outs) + list(scratch)

time: 117 us -> 114 us (0.974)
  Pallas kernels: 114 us -> 110 us
    pallas_call x1, Pallas kernels: 112 us -> 108 us  [layer(): pl.pallas_call(functools.partial(layer_kernel, names), out_shape=tuple((j...]
where the time goes in v8:
time: 114 us; the launch traced here: 112 us
  Pallas kernels  110 us (96%)
  other arithmetic  1.36 us (1%)
    pallas_call x1, Pallas kernels, layer(): pl.pallas_call(functools.partial(layer_kernel, names), out_shape=tuple((j...  108 us

profile of v8, /device:TPU:1, one launch (start us, length us, event | category | flops | bytes accessed | tf_op | source)
XLA Modules:
  0.0 112.3 jit_solution(5704877334521938837)
XLA Ops:
  0.6 1.4 %add_bitcast_fusion.refs_4_ = f32[1,128]{1,0:T(1,128)} fusion(bf16[6]{0:T(256)(128)(2,1)} %param.29, bf16[24]{0:T(256)(128)(2,1)} %param.27, bf16[6]{0:T(256)(128)(2,1)} %param.25, bf16[18]{0:T(256)(128)(2,1)} %param.23, bf16[6]{0:T(256)(128)(2,1)} %param.21, bf16[6]{0:T(256)(128)(2,1)} %param.20, bf16[6]{0:T(256)(128)(2,1)} %param.19, bf16[6]{0:T(256)(128)(2,1)} %param.18), kind=kLoop, calls=%fused_computation | loop fusion | flops 1920 | bytes 668 | tf_op jit(solution)/shard_map/reshape | solution.py:1005
  2.0 107.9 %layer.1 = (bf16[256,768]{1,0:T(8,128)(2,1)}, bf16[256,768]{1,0:T(8,128)(2,1)}, f32[6,3072]{1,0:T(8,128)}, f32[6,2304]{1,0:T(8,128)}, f32[24,768]{1,0:T(8,128)}, /*index=5*/f32[6,768]{1,0:T(8,128)}, f32[8,128]{1,0:T(8,128)}) custom-call(bf16[256,768]{1,0:T(8,128)(2,1)} %refs_0_.1, bf16[256,768]{1,0:T(8,128)(2,1)} %refs_1_.1, bf16[6,3072]{1,0:T(8,128)(2,1)} %refs_2_.1, ...), custom_call_target="tpu_custom_call" | custom-call | flops 14000000000 | bytes 16000000 | tf_op jit(solution)/shard_map/layer/pallas_call | solution.py:927
  109.9 2.2 %outputs.1 = (bf16[256,768]{1,0:T(8,128)(2,1)}, bf16[256,768]{1,0:T(8,128)(2,1)}, f32[6,3072]{1,0:T(8,128)}, f32[6,2304]{1,0:T(8,128)}, f32[24,768]{1,0:T(8,128)...) custom-call(bf16[256,768]{1,0:T(8,128)(2,1)} %get-tuple-element.35.r, ...), custom_call_target="tpu_custom_call" | custom-call | tf_op jit(solution)/shard_map/outputs/pallas_call | solution.py:959

commit v9 on v8

--- a/solution.py
+++ b/solution.py
@@ -549,6 +549,7 @@
     weight_grad(r.n2_s, r.dpre_s, r.up_g)
     start_1(UP)
 
+    scale = HEAD_DIM ** (-0.5)
     wait_b(qkv_n)
     join(r.qk_all, r.qk_s)
     wait_b(dense_n)
@@ -575,21 +576,19 @@
 
         for h in range(heads):
             at = 2 * width + h * HEAD_DIM
-            r.q_s[h, rows, :] = head(h).astype(BF)
+            r.q_s[h, rows, :] = (head(h).astype(BF).astype(F32) * scale).astype(BF)
             r.k_s[h, rows, :] = head(heads + h).astype(BF)
             r.v_s[h, rows, :] = y_rows[:, at : at + HEAD_DIM].astype(BF)
             r.do_s[h, rows, :] = d[:, h * HEAD_DIM : (h + 1) * HEAD_DIM].astype(BF)
 
-    scale = HEAD_DIM ** (-0.5)
-
     def attend(h):
-        r.kt_s[...] = r.k_s[h].astype(F32).T.astype(BF)
+        r.kt_s[...] = (r.k_s[h].astype(F32).T * scale).astype(BF)
         r.vt_s[...] = r.v_s[h].astype(F32).T.astype(BF)
         for i in reversed(range(steps)):
             keys = (i + 1) * BLOCK
             rows = slice(i * BLOCK, (i + 1) * BLOCK)
             q, do = r.q_s[h, rows, :], r.do_s[h, rows, :]
-            scores = dot_nt(r.k_s[h, :keys, :], q) * scale
+            scores = dot_nt(r.k_s[h, :keys, :], q)
             hidden = iota((BLOCK, BLOCK), 0) > iota((BLOCK, BLOCK), 1)
             corner = jnp.where(hidden, -1e30, scores[i * BLOCK :, :])
             scores = jnp.concatenate([scores[: i * BLOCK, :], corner], 0) if i else corner
@@ -599,7 +598,7 @@
             r.ctxt_s[h, :, rows] = dot(r.vt_s[:, :keys], low).astype(BF)
             dprobs = dot_nt(r.v_s[h, :keys, :], do)
             delta = jnp.sum(probs * dprobs, 0, keepdims=True)
-            dscores = (probs * (dprobs - delta) * scale).astype(BF)
+            dscores = (probs * (dprobs - delta)).astype(BF)
             r.dq_s[h, rows, :] = dot(r.kt_s[:, :keys], dscores).T.astype(BF)
             dk = dot(dscores, q)
             dv = dot(low, do)
@@ -682,10 +681,10 @@
     qkv_bias, gain_1_grad, shift_1_grad = lax.fori_loop(
         0, steps, last, (jnp.zeros((8, QK), F32), zeros, zeros)
     )
+    for item in token_pair(1):
+        item.start()
     weight_grad(r.n1_s, r.dqkv_s, r.qk_g)
     start_1(QKV)
-    for item in token_pair(1):
-        item.start()
     token_cross(0)
     dense_grad = dot(ctxt, r.g_all[...])
     for e in range(NY * NZ * NX):
@@ -693,6 +692,8 @@
             e * PART : (e + 1) * PART, :
         ].astype(BF)
     start_1(DENSE)
+
+    token_cross(1)
 
     g_here = r.g_all[rows_of(sp), :].astype(F32)
     values = (
@@ -716,7 +717,6 @@
     for e in range(NY * NZ * NX):
         r.small_g[e // GROUP, e // NX % NZ, e % NX] = result[e * 8 : (e + 1) * 8, :]
     start_1(SMALLS)
-    token_cross(1)
     start_2(QKV)
 
     def store_pieces(totals, out):

time: 114 us -> 113 us (level)
  no operation moved by 1% of the time
where the time goes in v9:
time: 113 us; the launch traced here: 112 us
  Pallas kernels  110 us (97%)
  other arithmetic  1.36 us (1%)
    pallas_call x1, Pallas kernels, layer(): pl.pallas_call(functools.partial(layer_kernel, names), out_shape=tuple((j...  108 us

profile of v9, /device:TPU:1, one launch (start us, length us, event | category | flops | bytes accessed | tf_op | source)
XLA Modules:
  0.0 112.1 jit_solution(13595447311855376281)
XLA Ops:
  0.6 1.4 %add_bitcast_fusion.refs_4_ = f32[1,128]{1,0:T(1,128)} fusion(bf16[6]{0:T(256)(128)(2,1)} %param.29, bf16[24]{0:T(256)(128)(2,1)} %param.27, bf16[6]{0:T(256)(128)(2,1)} %param.25, bf16[18]{0:T(256)(128)(2,1)} %param.23, bf16[6]{0:T(256)(128)(2,1)} %param.21, bf16[6]{0:T(256)(128)(2,1)} %param.20, bf16[6]{0:T(256)(128)(2,1)} %param.19, bf16[6]{0:T(256)(128)(2,1)} %param.18), kind=kLoop, calls=%fused_computation | loop fusion | flops 1920 | bytes 668 | tf_op jit(solution)/shard_map/reshape | solution.py:1005
  2.0 107.7 %layer.1 = (bf16[256,768]{1,0:T(8,128)(2,1)}, bf16[256,768]{1,0:T(8,128)(2,1)}, f32[6,3072]{1,0:T(8,128)}, f32[6,2304]{1,0:T(8,128)}, f32[24,768]{1,0:T(8,128)}, /*index=5*/f32[6,768]{1,0:T(8,128)}, f32[8,128]{1,0:T(8,128)}) custom-call(bf16[256,768]{1,0:T(8,128)(2,1)} %refs_0_.1, bf16[256,768]{1,0:T(8,128)(2,1)} %refs_1_.1, bf16[6,3072]{1,0:T(8,128)(2,1)} %refs_2_.1, ...), custom_call_target="tpu_custom_call" | custom-call | flops 14000000000 | bytes 16000000 | tf_op jit(solution)/shard_map/layer/pallas_call | solution.py:927
  109.7 2.2 %outputs.1 = (bf16[256,768]{1,0:T(8,128)(2,1)}, bf16[256,768]{1,0:T(8,128)(2,1)}, f32[6,3072]{1,0:T(8,128)}, f32[6,2304]{1,0:T(8,128)}, f32[24,768]{1,0:T(8,128)...) custom-call(bf16[256,768]{1,0:T(8,128)(2,1)} %get-tuple-element.35.r, ...), custom_call_target="tpu_custom_call" | custom-call | tf_op jit(solution)/shard_map/outputs/pallas_call | solution.py:959
